TPU v7x, 32 devices: a whole 2x2x4 slice. The times are simulated.
32 devices in a mesh: grp: 2 (over y), bin: 4 (over z), off: 2 (over x), sub: 2 (over core).
Axes of the slice: x: 2, y: 2, z: 4, core: 2. Of those that a mesh axis runs over, the one named last changes fastest.
Arguments:
- traces: bfloat16 [4, 4096, 2048], P(('grp', 'off'), ('bin', 'sub')), parts along dimension 0, may hold values from -6 to 6
- mid_bin: int32 [4, 4096], P(('grp', 'off'), ('bin', 'sub')), parts along dimension 0, may hold values from 0 to 2047, as said below
- live_count: int32 [4, 8], P(('grp', 'off'), ('bin', 'sub')), parts along dimension 0, may hold values from 256 to 512, as said below
- fine_class: int32 [4, 4096], P(('grp', 'off'), ('bin', 'sub')), parts along dimension 0, may hold values from 0 to 1
- operator: bfloat16 [4, 2, 4, 8, 8, 128, 128], P(('grp', 'off'), None, 'bin', 'sub'), parts along dimension 0, may hold values from -0.1875 to 0.1875
- block_index: int32 [4, 2, 4, 8, 8], P(('grp', 'off'), None, 'bin', 'sub'), parts along dimension 0, may hold values from 0 to 15
Outputs:
- image: float32 [4096, 1024], P(('grp', 'bin', 'off'), 'sub'), parts along dimension 0
There are 2 independent parts, one for each index of `grp`. A program takes and returns all parts, laid end to end along the dimension named above; each array names one. Nothing has to cross between parts.
Inputs may be any that keep to these rules, and one draw needn't show every extreme that they name: `mid_bin`: among the live rows of one shot-order device at most 192 lie in the bins of one owner (bins o * 512 to o * 512 + 511), and on every device some owner has exactly 192. `live_count`: some device holds 512 live rows in every draw.
All inputs are finite; a program needn't handle non-finite values.
Results may differ from a plain program's by a relative error of at most 0.0023.
Values may be sent and summed in bfloat16 or wider, within the bound.
No kernel may reach another device: no remote copies, remote signals or barrier semaphores. Data moves between devices by JAX's collectives and lax.ppermute only.
A program may use at most 64 MiB of HBM per device.

v0:
```python
import jax
import jax.numpy as jnp
from jax import lax
from jax.sharding import PartitionSpec as P

FINE = 2
COLS = 512


def pack(records, trace_tags, owner, owners, capacity):
    is_live = trace_tags >= 0
    hits = (owner[:, None] == jnp.arange(owners, dtype=jnp.int32)[None, :]) & is_live[:, None]
    ranks = jnp.cumsum(hits.astype(jnp.int32), axis=0) - 1
    places = jnp.sum(jnp.where(hits, ranks, 0), axis=1)
    target = jnp.where(is_live, owner * capacity + places, owners * capacity)
    samples = records.shape[1]
    buffer = jnp.zeros((owners * capacity + 1, samples), records.dtype).at[target].set(records)
    labels = jnp.full((owners * capacity + 1,), -1, jnp.int32).at[target].set(trace_tags)
    return (buffer[:-1].reshape(owners, capacity, samples), labels[:-1].reshape(owners, capacity))


def pick_blocks(columns, chosen):
    return jnp.take(columns, chosen, axis=1)


def local(traces, mid_bin, live_count, fine_class, operator, block_index):
    records = traces[0]
    tr_dev = records.shape[0]
    samples = records.shape[1]
    owners = lax.axis_size("bin")
    capacity = 3 * tr_dev // (2 * owners)
    is_live = jnp.arange(tr_dev, dtype=jnp.int32) < live_count[0, 0]
    owner = mid_bin[0] // COLS
    trace_tags = jnp.where(is_live, fine_class[0] * COLS + mid_bin[0] - owner * COLS, -1)
    buffer, labels = pack(records, trace_tags, owner, owners, capacity)
    buffer, labels = (
        lax.all_to_all(buffer, "bin", split_axis=0, concat_axis=0, tiled=True),
        lax.all_to_all(labels, "bin", split_axis=0, concat_axis=0, tiled=True),
    )
    arrived, marks = (
        lax.all_gather(buffer, "sub", axis=0, tiled=True),
        lax.all_gather(labels, "sub", axis=0, tiled=True),
    )
    arrived = arrived.reshape(-1, samples)
    marks = marks.reshape(-1)
    segment = jnp.where(marks >= 0, marks, FINE * COLS)
    width = operator.shape[-1]
    stacked = jax.ops.segment_sum(
        arrived.astype(jnp.float32), segment, num_segments=FINE * COLS + 1
    )[: FINE * COLS]
    stacked = stacked.astype(jnp.bfloat16).reshape(FINE, COLS, samples // width, width)
    local_ops = jnp.moveaxis(operator[0, :, 0], 1, 0)
    local_chosen = jnp.moveaxis(block_index[0, :, 0], 1, 0)
    depth_local = local_ops.shape[0]
    part_columns = stacked

    def one_depth(members):
        depth_ops, depth_chosen = members
        picked = jax.vmap(pick_blocks)(part_columns, depth_chosen)
        return jnp.einsum("fckq,fkpq->cp", picked, depth_ops, preferred_element_type=jnp.float32)

    result = lax.map(one_depth, (local_ops, local_chosen))
    return lax.psum_scatter(
        jnp.moveaxis(result, 0, 1).reshape(
            COLS // lax.axis_size("off") * lax.axis_size("off"), depth_local * width
        ),
        "off",
        scatter_dimension=0,
        tiled=True,
    )


def solution(mesh):
    placed = (
        P(("grp", "off"), ("bin", "sub"), None),
        P(("grp", "off"), ("bin", "sub")),
        P(("grp", "off"), ("bin", "sub")),
        P(("grp", "off"), ("bin", "sub")),
        P(("grp", "off"), None, "bin", "sub", None, None, None),
        P(("grp", "off"), None, "bin", "sub", None),
    )
    return jax.shard_map(
        local,
        mesh=mesh,
        in_specs=placed,
        out_specs=P(("grp", "bin", "off"), "sub"),
        check_vma=False,
    )
```

profile of v0, /device:TPU:0, one launch (start us, length us, event | category | flops | bytes accessed | tf_op | source)
XLA Modules:
  0.0 207.5 jit_solution(12657003503599538506)
XLA Ops:
  9.4 1.2 reduce-window.6
  13.3 5.7 %scatter_custom_fusion.1 = bf16[769,2048]{1,0:T(8,128)(2,1)} fusion(s32[512]{0:T(512)S(1)} %bitcast.126, bf16[1,512,2048]{2,1,0:T(8,128)(2,1)S(1)} %copy-done, bf16[]{:T(256)} %constant.68.clone.1), kind=kCustom, calls=%fused_computation.27 | custom fusion | bytes 5246978 | tf_op jit(solution)/shard_map/scatter | solution.py:17
  19.0 1.9 slice-done
  20.9 76.9 %all_to_all.17 = bf16[4,192,2048]{2,1,0:T(8,128)(2,1)} all-to-all(bf16[4,192,2048]{2,1,0:T(8,128)(2,1)S(1)} %bitcast.111), channel_id=1, replica_groups=mesh['grp'=2,'bin'=4,'off'=2,'sub'=2] {'bin'}, dimensions={0} | all-to-all | bytes 6291456 | tf_op jit(solution)/shard_map/all_to_all | solution.py:37
  97.8 2.4 %scatter_custom_fusion = s32[769]{0:T(1024)S(1)} fusion(s32[512]{0:T(512)S(1)} %bitcast.127, s32[512]{0:T(512)S(1)} %get-tuple-element.64, s32[]{:T(128)} %constant.58.clone.1), kind=kCustom, calls=%fused_computation.70 | custom fusion | bytes 3080 | tf_op jit(solution)/shard_map/scatter | solution.py:18
  100.9 3.3 %all-to-all-start = ((s32[4,1,192]{2,1,0:T(1,128)}), s32[4,1,192]{2,1,0:T(1,128)S(1)}, u32[]{:S(2)}, u32[]{:S(2)}) async-start(s32[4,1,192]{2,1,0:T(1,128)} %all_to_all.11), calls=%async_computation | async-start | bytes 8192 | tf_op jit(solution)/shard_map/all_to_all | solution.py:38
  104.2 3.5 %copy.30 = bf16[1,2,1,4,8,128,128]{6,5,4,1,3,2,0:T(8,128)(2,1)} copy(bf16[1,2,1,4,8,128,128]{6,5,4,3,2,1,0:T(8,128)(2,1)} %param.12) | data formatting | bytes 4194304 | tf_op args[4]
  107.7 2.0 all-to-all-done
  109.7 2.0 all-gather
  111.8 2.2 %all-gather.3.cloned.1.call-done = bf16[8,192,2048]{2,1,0:T(8,128)(2,1)} async-done(((bf16[4,192,2048]{2,1,0:T(8,128)(2,1)}), bf16[8,192,2048]{2,1,0:T(8,128)(2,1)}) %all-gather.3.cloned.1.call-update) | async-done | bytes 6291472 | tf_op jit(solution)/shard_map/all_gather | solution.py:41
  114.0 24.8 %scatter_custom_fusion.2 = f32[1025,2048]{1,0:T(8,128)} fusion(s32[1536]{0:T(1024)S(1)} %fusion.30, bf16[1536,2048]{1,0:T(8,128)(2,1)} %bitcast.112, f32[]{:T(128)} %constant.41.clone.1), kind=kCustom, calls=%fused_computation.22 | custom fusion | flops 6291456 | bytes 14688260 | tf_op jit(solution)/shard_map/scatter-add | solution.py:48
  138.8 4.4 %fusion.21 = bf16[128,8,16,128]{3,1,2,0:T(8,128)(2,1)S(1)} fusion(f32[1025,2048]{1,0:T(8,128)} %scatter_custom_fusion.2), kind=kLoop, calls=%fused_computation.26 | loop fusion | bytes 8388608
  143.2 1.4 copy.26
  144.6 3.0 %copy.20 = bf16[2,512,16,128]{3,1,2,0:T(8,128)(2,1)} copy(bf16[2,512,16,128]{3,2,1,0:T(8,128)(2,1)S(1)} %bitcast.110) | data formatting | bytes 8388608 | tf_op jit(solution)/shard_map/while | solution.py:62
  147.6 30.3 %while.10 = (s32[]{:T(128)}, f32[4,512,128]{2,1,0:T(8,128)S(1)}, s32[4,2,8]{2,0,1:T(4,128)}, bf16[2,512,16,128]{3,1,2,0:T(8,128)(2,1)}, bf16[4,2,8,128,128]{4,3,2,1,0:T(8,128)(2,1)}, /*index=5*/s32[]{:T(128)}) while((s32[]{:T(128)}, f32[4,512,128]{2,1,0:T(8,128)S(1)}, s32[4,2,8]{2,0,1:T(4,128)}, bf16[2,512,16,128]{3,1,2,0:T(8,128)(2,1)}, ...), condition=%wide.region_7.8_spmd, body=%wide.region_6.7_spmd.sunk | while | flops 269484256 | bytes 7080089 | solution.py:62
  148.4 4.3 %gather_fusion = bf16[16,512,128]{2,1,0:T(8,128)(2,1)} fusion(bf16[2,512,16,128]{3,1,2,0:T(8,128)(2,1)} %get-tuple-element.111, s32[16]{0:T(128)S(1)} %reshape.320), kind=kCustom, calls=%fused_computation.clone.1 | custom fusion | bytes 4194432 | tf_op jit(solution)/shard_map/while/body/eval_jaxpr/vmap(jit(_take))/gather | solution.py:23
  152.8 2.4 %fusion.46 = f32[4,512,128]{2,1,0:T(8,128)S(1)} fusion(f32[4,512,128]{2,1,0:T(8,128)S(1)} %get-tuple-element.103, s32[]{:T(128)} %get-tuple-element.102, bf16[2,8,512,128]{3,2,1,0:T(8,128)(2,1)} %bitcast.109, pred[2,8]{1,0:T(4,128)(4,1)S(1)} %compare_and_fusion.2, bf16[4,2,8,128,128]{4,3,2,1,0:T(8,128)(2,1)} %get-tuple-element.112), kind=kOutput, calls=%fused_computation.9.clone.1 | convolution fusion | flops 269484032 | bytes 2885120 | tf_op jit(solution)/shard_map/while/body/eval_jaxpr/fckq,fkpq->cp/dot_general | solution.py:60
  156.0 4.3 %gather_fusion = bf16[16,512,128]{2,1,0:T(8,128)(2,1)} fusion(bf16[2,512,16,128]{3,1,2,0:T(8,128)(2,1)} %get-tuple-element.111, s32[16]{0:T(128)S(1)} %reshape.320), kind=kCustom, calls=%fused_computation.clone.1 | custom fusion | bytes 4194432 | tf_op jit(solution)/shard_map/while/body/eval_jaxpr/vmap(jit(_take))/gather | solution.py:23
  160.3 2.4 %fusion.46 = f32[4,512,128]{2,1,0:T(8,128)S(1)} fusion(f32[4,512,128]{2,1,0:T(8,128)S(1)} %get-tuple-element.103, s32[]{:T(128)} %get-tuple-element.102, bf16[2,8,512,128]{3,2,1,0:T(8,128)(2,1)} %bitcast.109, pred[2,8]{1,0:T(4,128)(4,1)S(1)} %compare_and_fusion.2, bf16[4,2,8,128,128]{4,3,2,1,0:T(8,128)(2,1)} %get-tuple-element.112), kind=kOutput, calls=%fused_computation.9.clone.1 | convolution fusion | flops 269484032 | bytes 2885120 | tf_op jit(solution)/shard_map/while/body/eval_jaxpr/fckq,fkpq->cp/dot_general | solution.py:60
  163.6 4.3 %gather_fusion = bf16[16,512,128]{2,1,0:T(8,128)(2,1)} fusion(bf16[2,512,16,128]{3,1,2,0:T(8,128)(2,1)} %get-tuple-element.111, s32[16]{0:T(128)S(1)} %reshape.320), kind=kCustom, calls=%fused_computation.clone.1 | custom fusion | bytes 4194432 | tf_op jit(solution)/shard_map/while/body/eval_jaxpr/vmap(jit(_take))/gather | solution.py:23
  167.9 2.4 %fusion.46 = f32[4,512,128]{2,1,0:T(8,128)S(1)} fusion(f32[4,512,128]{2,1,0:T(8,128)S(1)} %get-tuple-element.103, s32[]{:T(128)} %get-tuple-element.102, bf16[2,8,512,128]{3,2,1,0:T(8,128)(2,1)} %bitcast.109, pred[2,8]{1,0:T(4,128)(4,1)S(1)} %compare_and_fusion.2, bf16[4,2,8,128,128]{4,3,2,1,0:T(8,128)(2,1)} %get-tuple-element.112), kind=kOutput, calls=%fused_computation.9.clone.1 | convolution fusion | flops 269484032 | bytes 2885120 | tf_op jit(solution)/shard_map/while/body/eval_jaxpr/fckq,fkpq->cp/dot_general | solution.py:60
  171.1 4.3 %gather_fusion = bf16[16,512,128]{2,1,0:T(8,128)(2,1)} fusion(bf16[2,512,16,128]{3,1,2,0:T(8,128)(2,1)} %get-tuple-element.111, s32[16]{0:T(128)S(1)} %reshape.320), kind=kCustom, calls=%fused_computation.clone.1 | custom fusion | bytes 4194432 | tf_op jit(solution)/shard_map/while/body/eval_jaxpr/vmap(jit(_take))/gather | solution.py:23
  175.5 2.4 %fusion.46 = f32[4,512,128]{2,1,0:T(8,128)S(1)} fusion(f32[4,512,128]{2,1,0:T(8,128)S(1)} %get-tuple-element.103, s32[]{:T(128)} %get-tuple-element.102, bf16[2,8,512,128]{3,2,1,0:T(8,128)(2,1)} %bitcast.109, pred[2,8]{1,0:T(4,128)(4,1)S(1)} %compare_and_fusion.2, bf16[4,2,8,128,128]{4,3,2,1,0:T(8,128)(2,1)} %get-tuple-element.112), kind=kOutput, calls=%fused_computation.9.clone.1 | convolution fusion | flops 269484032 | bytes 2885120 | tf_op jit(solution)/shard_map/while/body/eval_jaxpr/fckq,fkpq->cp/dot_general | solution.py:60
  179.1 21.6 %reduce-scatter.2.cloned.1.call-done = f32[256,512]{1,0:T(8,128)} async-done(((f32[512,512]{1,0:T(8,128)}), f32[256,512]{1,0:T(8,128)}) %reduce-scatter.2.cloned.1.call-update) | async-done | bytes 524304 | tf_op jit(solution)/shard_map/reduce_scatter | solution.py:63
  (40 shorter events, 9.9 us)
Async XLA Ops:
  6.5 6.7 %copy-start = (bf16[1,512,2048]{2,1,0:T(8,128)(2,1)S(1)}, bf16[1,512,2048]{2,1,0:T(8,128)(2,1)}, u32[]{:S(2)}) copy-start(bf16[1,512,2048]{2,1,0:T(8,128)(2,1)} %param.8) | copy-start | bytes 6291460
  6.5 107.5 %all-gather.3.cloned.1.call-start = ((), (), s32[]{:S(2)}) async-start(), calls=%async_computation.3 | async-start | bytes 9437184 | tf_op jit(solution)/shard_map/all_gather | solution.py:41
  19.0 1.9 slice-start
  100.9 8.8 %all-to-all-start = ((s32[4,1,192]{2,1,0:T(1,128)}), s32[4,1,192]{2,1,0:T(1,128)S(1)}, u32[]{:S(2)}, u32[]{:S(2)}) async-start(s32[4,1,192]{2,1,0:T(1,128)} %all_to_all.11), calls=%async_computation | async-start | bytes 8192 | tf_op jit(solution)/shard_map/all_to_all | solution.py:38
  104.1 96.5 %reduce-scatter.2.cloned.1.call-start = ((), (), s32[]{:S(2)}) async-start(), calls=%async_computation.4 | async-start | bytes 1572864 | tf_op jit(solution)/shard_map/reduce_scatter | solution.py:63
Sparse Core Ops, SparseCore 0:
  97.9 16.0 all-gather.2
  179.2 21.4 reduce-scatter.1
where the time goes:
time: 208 us
  blocking collectives  78.8 us (38%)
  local copies, waits for them, and re-layouts  44.8 us (22%)
  other arithmetic  30.7 us (15%)
  waiting for transfers between devices  25.9 us (12%)
  between operations  14.3 us (7%)
  matrix products  9.66 us (5%)
  starting transfers between devices  3.3 us (2%)
    all_to_all x1, blocking collectives, local(): lax.all_to_all(buffer, 'bin', split_axis=0, concat_axis=0, tiled=True)  76.9 us
    scatter-add x1, other arithmetic, local(): jax.ops.segment_sum(arrived.astype(jnp.float32), segment, num_segments=FI...  24.8 us
    reduce_scatter x1, waiting for transfers between devices, local(): lax.psum_scatter(jnp.moveaxis(result, 0, 1).reshape(COLS // lax.axis_size...  21.6 us
    gather x8, local copies, waits for them, and re-layouts, pick_blocks(): return jnp.take(columns, chosen, axis=1)  17.7 us
    dot_general x4, matrix products, one_depth(): jnp.einsum('fckq,fkpq->cp', picked, depth_ops, preferred_element_type=jnp...  9.66 us
    unnamed x5, local copies, waits for them, and re-layouts  9.24 us
    scatter x1, local copies, waits for them, and re-layouts, pack(): jnp.zeros((owners * capacity + 1, samples), records.dtype).at[target]  5.69 us
  transfers between devices with their start and end apart: 3, of which 3 were waited for; matrix products, arithmetic and copies ran while one was open for 3% of the time, Pallas kernels for 0%

commit v1 on v0

v1 whole, which is shorter than its diff:
```python
import functools

import jax
import jax.numpy as jnp
from jax import lax
from jax.experimental import pallas as pl
from jax.experimental.pallas import tpu as pltpu
from jax.sharding import PartitionSpec as P

FINE = 2
COLS = 512
LABEL_ROWS = 16
TILE = 256
BF = jnp.bfloat16
F32 = jnp.float32
MIB = 1 << 20


def params(mib):
    return pltpu.CompilerParams(vmem_limit_bytes=mib * MIB)


def vmem():
    return pl.BlockSpec(memory_space=pltpu.VMEM)


def smem():
    return pl.BlockSpec(memory_space=pltpu.SMEM)


def pack_kernel(plan, live_ref, mid_ref, fine_ref, traces_ref, *outs):
    owners, subs, cap, start, width, labelled = plan
    z = lax.axis_index("bin")
    s = lax.axis_index("sub")
    rows, samples = traces_ref.shape
    half = samples // subs
    live = lax.broadcasted_iota(jnp.int32, (1, rows), 1) < live_ref[0, 0]
    mid = mid_ref[...]
    owner = mid // COLS
    group = max(owners, 16)
    target = lax.broadcasted_iota(jnp.int32, (group, rows), 0) ^ z
    hits = jnp.where(live, owner, -1) == target
    upper = (
        lax.broadcasted_iota(jnp.int32, (rows, rows), 0) <= lax.broadcasted_iota(jnp.int32, (rows, rows), 1)
    )
    rank = jnp.dot(
        jnp.where(hits, 1.0, 0.0).astype(BF), jnp.where(upper, 1.0, 0.0).astype(BF), preferred_element_type=F32
    )
    slot = jnp.where(hits, rank - 1.0, -1.0).astype(jnp.int32)
    place = lax.broadcasted_iota(jnp.int32, (cap, rows), 0)
    select = [jnp.where(slot[d : d + 1] == place, 1.0, 0.0).astype(BF) for d in range(owners)]
    if labelled:
        tag = jnp.where(live, fine_ref[...] * COLS + mid - owner * COLS + 1, 0)
        line = lax.broadcasted_iota(jnp.int32, (LABEL_ROWS, rows), 0)
        digits = jnp.where(line == 0, tag // 256, jnp.where(line == 1, tag % 256, 0)).astype(F32).astype(BF)
    for e in range(subs):
        at = pl.multiple_of((s ^ e) * half + start, 128)
        block = traces_ref[:, pl.ds(at, width)]
        for d in range(owners):
            out = outs[e * owners + d]
            out[0:cap, :] = jnp.dot(select[d], block, preferred_element_type=F32).astype(BF)
            if labelled:
                out[cap : cap + LABEL_ROWS, :] = jnp.zeros((LABEL_ROWS, width), BF)
                out[cap : cap + LABEL_ROWS, 0:cap] = lax.dot_general(
                    digits, select[d], (((1,), (1,)), ((), ())), preferred_element_type=F32
                ).astype(BF)


def pack(plan, live_count, mid_bin, fine_class, records):
    owners, subs, cap, start, width, labelled = plan
    rows = cap + (LABEL_ROWS if labelled else 0)
    return pl.pallas_call(
        functools.partial(pack_kernel, plan),
        out_shape=[jax.ShapeDtypeStruct((rows, width), BF)] * (owners * subs),
        in_specs=[smem(), vmem(), vmem(), vmem()],
        out_specs=[vmem()] * (owners * subs),
        compiler_params=params(24),
        name="pack",
    )(live_count, mid_bin, fine_class, records)


def apply_blocks(first, blocks, stacked_ref, index_ref, ops_ref, acc_ref):
    fine, depth, taps = index_ref.shape
    width = ops_ref.shape[-1]
    for f in range(fine):
        for d in range(depth):
            for k in range(taps):
                at = index_ref[f, d, k] - first

                @pl.when((at >= 0) & (at < blocks))
                def _(f=f, d=d, k=k, at=at):
                    column = pl.multiple_of(at * width, width)
                    acc_ref[:, d * width : (d + 1) * width] += lax.dot_general(
                        stacked_ref[f * COLS : (f + 1) * COLS, pl.ds(column, width)],
                        ops_ref[f, d, k],
                        (((1,), (1,)), ((), ())),
                        preferred_element_type=F32,
                    )


def stack_kernel(cap, labelled, count, *refs):
    label_in = None if labelled else refs[0]
    given = refs[0 if labelled else 1 :][:count]
    stacked_ref = refs[count + (0 if labelled else 1)]
    scratch = refs[-1]
    if labelled:
        label_out = refs[count + 1]
        pieces = []
        for ref in given:
            digits = ref[cap : cap + LABEL_ROWS, 0:cap].astype(F32)
            pieces.append(256.0 * digits[0:1] + digits[1:2] - 1.0)
        label = jnp.concatenate(pieces, axis=1)
        label_out[...] = jnp.broadcast_to(label, label_out.shape)
    else:
        label = label_in[0:1, :]
    for i, ref in enumerate(given):
        scratch[i * cap : (i + 1) * cap, :] = ref[0:cap, :]
    segments = FINE * COLS

    def tile(t, carry):
        base = pl.multiple_of(t * TILE, TILE)
        line = (lax.broadcasted_iota(jnp.int32, (TILE, 1), 0) + base).astype(F32)
        chosen = jnp.where(label == line, 1.0, 0.0).astype(BF)
        stacked_ref[pl.ds(base, TILE), :] = jnp.dot(
            chosen, scratch[...], preferred_element_type=F32
        ).astype(BF)
        return carry

    lax.fori_loop(0, segments // TILE, tile, 0)


def stack(cap, label, given):
    width = given[0].shape[1]
    labelled = label is None
    slots = cap * len(given)
    out_shape = [jax.ShapeDtypeStruct((FINE * COLS, width), BF)]
    if labelled:
        out_shape.append(jax.ShapeDtypeStruct((8, slots), F32))
    operands = list(given) if labelled else [label, *given]
    return pl.pallas_call(
        functools.partial(stack_kernel, cap, labelled, len(given)),
        out_shape=out_shape,
        in_specs=[vmem()] * len(operands),
        out_specs=[vmem()] * len(out_shape),
        scratch_shapes=[pltpu.VMEM((slots, width), BF)],
        compiler_params=params(24),
        name="stack",
    )(*operands)


def operate_kernel(plan, index_ref, ops_ref, *refs):
    opening, closing, parts = plan
    refs = list(refs)
    acc_in = None if opening else refs.pop(0)
    given = refs[: len(parts)]
    outs = refs[len(parts) :]
    acc = outs[0]
    if opening:
        acc[...] = jnp.zeros_like(acc)
    else:
        acc[...] = acc_in[...]
    s = lax.axis_index("sub")
    width = ops_ref.shape[-1]
    for (other, half, start), ref in zip(parts, given):
        first = ((s ^ other) * half + start) // width
        apply_blocks(first, ref.shape[1] // width, ref, index_ref, ops_ref, acc)
    if closing:
        own, sent = outs[0], outs[1:]
        share = own.shape[0] // closing
        x = lax.axis_index("off")
        for k, ref in enumerate(sent):
            at = pl.multiple_of((x ^ (k + 1)) * share, share)
            ref[...] = own[pl.ds(at, share), :].astype(BF)


def operate(plan, index, ops, acc, given):
    opening, closing, parts = plan
    depth, width = ops.shape[1], ops.shape[-1]
    out_shape = [jax.ShapeDtypeStruct((COLS, depth * width), F32)]
    if closing:
        out_shape += [jax.ShapeDtypeStruct((COLS // closing, depth * width), BF)] * (closing - 1)
    operands = [index, ops] + ([] if opening else [acc]) + list(given)
    return pl.pallas_call(
        functools.partial(operate_kernel, plan),
        out_shape=out_shape,
        in_specs=[smem()] + [vmem()] * (len(operands) - 1),
        out_specs=[vmem()] * len(out_shape),
        input_output_aliases={} if opening else {2: 0},
        compiler_params=params(24),
        name="operate",
    )(*operands)


def swap(x, axis, mask):
    return lax.ppermute(x, axis, [(i, i ^ mask) for i in range(lax.axis_size(axis))])


def local(traces, mid_bin, live_count, fine_class, operator, block_index):
    records = traces[0]
    samples = records.shape[1]
    owners, subs, offs = (lax.axis_size(a) for a in ("bin", "sub", "off"))
    cap = 3 * records.shape[0] // (2 * owners)
    half = samples // subs
    ops = operator[0, :, 0]
    index = block_index[0, :, 0]
    cuts = ((0, half * 3 // 4), (half * 3 // 4, half // 4))

    def move(x, d, e):
        if d == 0 and e == 0:
            return x
        pairs = [
            (i * subs + j, (i ^ d) * subs + (j ^ e)) for i in range(owners) for j in range(subs)
        ]
        return lax.ppermute(x, ("bin", "sub"), pairs)

    arrived = []
    order = sorted(range(owners), key=lambda d: -d)
    for c, (start, width) in enumerate(cuts):
        packed = pack((owners, subs, cap, start, width, c == 0), live_count, mid_bin, fine_class, records)
        got = [None] * (owners * subs)
        for d in order:
            for e in range(subs):
                got[e * owners + d] = move(packed[e * owners + d], d, e)
        arrived.append(got)

    stacked0, label = stack(cap, None, arrived[0])
    other0 = swap(stacked0, "sub", 1)
    (acc,) = operate((True, 0, ((0, half, cuts[0][0]),)), index, ops, None, [stacked0])
    (acc,) = operate((False, 0, ((1, half, cuts[0][0]),)), index, ops, acc, [other0])
    (stacked1,) = stack(cap, label, arrived[1])
    other1 = swap(stacked1, "sub", 1)
    (acc,) = operate((False, 0, ((0, half, cuts[1][0]),)), index, ops, acc, [stacked1])
    acc, *sent = operate((False, offs, ((1, half, cuts[1][0]),)), index, ops, acc, [other1])
    share = COLS // offs
    total = lax.dynamic_slice_in_dim(acc, lax.axis_index("off") * share, share, axis=0)
    for k, piece in enumerate(sent):
        total = total + swap(piece, "off", k + 1).astype(F32)
    return total


def solution(mesh):
    placed = (
        P(("grp", "off"), ("bin", "sub"), None),
        P(("grp", "off"), ("bin", "sub")),
        P(("grp", "off"), ("bin", "sub")),
        P(("grp", "off"), ("bin", "sub")),
        P(("grp", "off"), None, "bin", "sub", None, None, None),
        P(("grp", "off"), None, "bin", "sub", None),
    )
    return jax.shard_map(
        local,
        mesh=mesh,
        in_specs=placed,
        out_specs=P(("grp", "bin", "off"), "sub"),
        check_vma=False,
    )
```

time: 208 us -> 119 us (0.57)
  blocking collectives: 78.8 us -> 0 us
  waiting for transfers between devices: 25.9 us -> 68.5 us
  local copies, waits for them, and re-layouts: 44.8 us -> 2.97 us
  other arithmetic: 30.7 us -> 0.86 us
  Pallas kernels: 0 us -> 24.5 us
  starting transfers between devices: 3.3 us -> 21.3 us
  between operations: 14.3 us -> 0.8 us
  matrix products: 9.66 us -> 0 us
    all_to_all x1 -> x0, blocking collectives: 76.9 us -> none  [local(): lax.all_to_all(buffer, 'bin', split_axis=0, concat_axis=0, tiled=True)]
    ppermute x0 -> x17, waiting for transfers between devices: none -> 68.5 us  [the longest x14 61.3 us: move(): return lax.ppermute(x, ('bin', 'sub'), pairs)]
    scatter-add x1 -> x0, other arithmetic: 24.8 us -> none  [local(): jax.ops.segment_sum(arrived.astype(jnp.float32), segment, num_segments=FI...]
    pallas_call x0 -> x8, Pallas kernels: none -> 24.5 us  [the longest x4 17.2 us: operate(): pl.pallas_call(functools.partial(operate_kernel, plan), out_shape=out_sha...]
    reduce_scatter x1 -> x0, waiting for transfers between devices: 21.6 us -> none  [local(): lax.psum_scatter(jnp.moveaxis(result, 0, 1).reshape(COLS // lax.axis_size...]
    ppermute x0 -> x17, starting transfers between devices: none -> 21.3 us  [the longest x14 16.9 us: move(): return lax.ppermute(x, ('bin', 'sub'), pairs)]
    gather x8 -> x0, local copies, waits for them, and re-layouts: 17.7 us -> none  [pick_blocks(): return jnp.take(columns, chosen, axis=1)]
    dot_general x4 -> x0, matrix products: 9.66 us -> none  [one_depth(): jnp.einsum('fckq,fkpq->cp', picked, depth_ops, preferred_element_type=jnp...]
  transfers between devices with their start and end apart: 3 -> 17, of which waited for: 3 -> 8; matrix products, arithmetic and copies ran while one was open for 3% -> 0% of each run, Pallas kernels for 0% -> 14%
where the time goes in v1:
time: 119 us
  waiting for transfers between devices  68.5 us (58%)
  Pallas kernels  24.5 us (21%)
  starting transfers between devices  21.3 us (18%)
  local copies, waits for them, and re-layouts  2.97 us (2%)
    ppermute x14, waiting for transfers between devices, move(): return lax.ppermute(x, ('bin', 'sub'), pairs)  61.3 us
    pallas_call x4, Pallas kernels, operate(): pl.pallas_call(functools.partial(operate_kernel, plan), out_shape=out_sha...  17.2 us
    ppermute x14, starting transfers between devices, move(): return lax.ppermute(x, ('bin', 'sub'), pairs)  16.9 us
    ppermute x3, waiting for transfers between devices, swap(): lax.ppermute(x, axis, [(i, i ^ mask) for i in range(lax.axis_size(axis))])  7.2 us
    pallas_call x2, Pallas kernels, stack(): pl.pallas_call(functools.partial(stack_kernel, cap, labelled, len(given))...  4.84 us
    ppermute x3, starting transfers between devices, swap(): lax.ppermute(x, axis, [(i, i ^ mask) for i in range(lax.axis_size(axis))])  4.35 us
    unnamed x16, local copies, waits for them, and re-layouts  2.97 us
    pallas_call x2, Pallas kernels, pack(): pl.pallas_call(functools.partial(pack_kernel, plan), out_shape=[jax.Shape...  2.45 us
  transfers between devices with their start and end apart: 17, of which 8 were waited for; matrix products, arithmetic and copies ran while one was open for 0% of the time, Pallas kernels for 14%

profile of v1, /device:TPU:0, one launch (start us, length us, event | category | flops | bytes accessed | tf_op | source)
XLA Modules:
  0.0 118.9 jit_solution(7570318281940988488)
XLA Ops:
  0.7 1.6 %copy-done.1 = bf16[1,512,2048]{2,1,0:T(8,128)(2,1)S(1)} copy-done((bf16[1,512,2048]{2,1,0:T(8,128)(2,1)S(1)}, bf16[1,512,2048]{2,1,0:T(8,128)(2,1)}, u32[]{:S(2)}) %copy-start.1) | copy-done | bytes 2097176
  3.6 1.7 %pack.2 = (bf16[208,768]{1,0:T(8,128)(2,1)S(1)}, bf16[208,768]{1,0:T(8,128)(2,1)S(1)}, bf16[208,768]{1,0:T(8,128)(2,1)S(1)}, bf16[208,768]{1,0:T(8,128)(2,1)S(1)...) custom-call(s32[1,1]{1,0:T(1,128)S(6)} %copy.13.live_ref, ...), custom_call_target="tpu_custom_call" | custom-call | tf_op jit(solution)/shard_map/pack/pallas_call | solution.py:72
  5.4 3.1 %collective-permute-start = (bf16[208,768]{1,0:T(8,128)(2,1)S(1)}, bf16[208,768]{1,0:T(8,128)(2,1)S(1)}, u32[]{:S(2)}, u32[]{:S(2)}) collective-permute-start(bf16[208,768]{1,0:T(8,128)(2,1)S(1)} %get-tuple-element.26), channel_id=1, source_target_pairs={{0,4},{1,5},{4,0},{5,1},{8,12},{9,13},{12,8},{13,9},{2,6},{3,7},{6... | collective-permute-start | bytes 958472 | tf_op jit(solution)/shard_map/ppermute | solution.py:214
  8.4 2.6 %collective-permute-start.1 = (bf16[208,768]{1,0:T(8,128)(2,1)S(1)}, bf16[208,768]{1,0:T(8,128)(2,1)S(1)}, u32[]{:S(2)}, u32[]{:S(2)}) collective-permute-start(bf16[208,768]{1,0:T(8,128)(2,1)S(1)} %get-tuple-element.27), channel_id=1, source_target_pairs={{0,8},{1,9},{4,12},{5,13},{8,0},{9,1},{12,4},{13,5},{2,10},{3,11},... | collective-permute-start | bytes 958472 | tf_op jit(solution)/shard_map/ppermute | solution.py:214
  11.0 1.0 collective-permute-start.4
  12.0 10.8 %collective-permute-done.refs_1_ = bf16[208,768]{1,0:T(8,128)(2,1)S(1)} collective-permute-done((bf16[208,768]{1,0:T(8,128)(2,1)S(1)}, bf16[208,768]{1,0:T(8,128)(2,1)S(1)}, u32[]{:S(2)}, u32[]{:S(2)}) %collective-permute-start) | collective-permute-done | bytes 319520 | tf_op jit(solution)/shard_map/ppermute | solution.py:214
  22.9 10.7 %collective-permute-done.1.refs_2_ = bf16[208,768]{1,0:T(8,128)(2,1)S(1)} collective-permute-done((bf16[208,768]{1,0:T(8,128)(2,1)S(1)}, bf16[208,768]{1,0:T(8,128)(2,1)S(1)}, u32[]{:S(2)}, u32[]{:S(2)}) %collective-permute-start.1) | collective-permute-done | bytes 319520 | tf_op jit(solution)/shard_map/ppermute | solution.py:214
  33.6 3.5 %collective-permute-done.4.refs_5_ = bf16[208,768]{1,0:T(8,128)(2,1)S(1)} collective-permute-done((bf16[208,768]{1,0:T(8,128)(2,1)S(1)}, bf16[208,768]{1,0:T(8,128)(2,1)S(1)}, u32[]{:S(2)}, u32[]{:S(2)}) %collective-permute-start.4) | collective-permute-done | bytes 319520 | tf_op jit(solution)/shard_map/ppermute | solution.py:214
  37.0 21.1 %collective-permute-done.5.refs_6_ = bf16[208,768]{1,0:T(8,128)(2,1)S(1)} collective-permute-done((bf16[208,768]{1,0:T(8,128)(2,1)S(1)}, bf16[208,768]{1,0:T(8,128)(2,1)S(1)}, u32[]{:S(2)}, u32[]{:S(2)}) %collective-permute-start.5) | collective-permute-done | bytes 319520 | tf_op jit(solution)/shard_map/ppermute | solution.py:214
  58.1 3.3 %stack.2 = (bf16[1024,768]{1,0:T(8,128)(2,1)S(1)}, f32[8,1536]{1,0:T(8,128)S(1)}) custom-call(bf16[208,768]{1,0:T(8,128)(2,1)S(1)} %get-tuple-element.25.refs_0_, bf16[208,768]{1,0:T(8,128)(2,1)S(1)} %collective-permute-done.refs_1_, bf16[208,768]{1,0:T(8,128)(2,1)S(1)} %collective-permute-done.1.refs_2_, ...), custom_call_target="tpu_custom_call" | custom-call | tf_op jit(solution)/shard_map/stack/pallas_call | solution.py:140
  61.4 2.7 %collective-permute-start.7 = (bf16[1024,768]{1,0:T(8,128)(2,1)S(1)}, bf16[1024,768]{1,0:T(8,128)(2,1)S(1)}, u32[]{:S(2)}, u32[]{:S(2)}) collective-permute-start(bf16[1024,768]{1,0:T(8,128)(2,1)S(1)} %get-tuple-element.33.refs_0_), channel_id=1, source_target_pairs={{0,1},{1,0},{2,3},{3,2},{4,5},{5,4},{6,7},{7,6},{8,9},{9,8},{10,11... | collective-permute-start | bytes 4718600 | tf_op jit(solution)/shard_map/ppermute | solution.py:195
  64.9 6.0 %collective-permute-start.8 = (bf16[192,256]{1,0:T(8,128)(2,1)S(1)}, bf16[192,256]{1,0:T(8,128)(2,1)S(1)}, u32[]{:S(2)}, u32[]{:S(2)}) collective-permute-start(bf16[192,256]{1,0:T(8,128)(2,1)S(1)} %get-tuple-element.36), channel_id=1, source_target_pairs={{0,4},{1,5},{4,0},{5,1},{8,12},{9,13},{12,8},{13,9},{2,6},{3,7},{6... | collective-permute-start | bytes 294920 | tf_op jit(solution)/shard_map/ppermute | solution.py:214
  70.9 1.1 collective-permute-start.9
  72.0 1.4 %collective-permute-start.10 = (bf16[192,256]{1,0:T(8,128)(2,1)S(1)}, bf16[192,256]{1,0:T(8,128)(2,1)S(1)}, u32[]{:S(2)}, u32[]{:S(2)}) collective-permute-start(bf16[192,256]{1,0:T(8,128)(2,1)S(1)} %get-tuple-element.38), channel_id=1, source_target_pairs={{0,12},{1,13},{4,8},{5,9},{8,4},{9,5},{12,0},{13,1},{2,14},{3,15},... | collective-permute-start | bytes 294920 | tf_op jit(solution)/shard_map/ppermute | solution.py:214
  74.5 7.1 %collective-permute-done.9.refs_3_ = bf16[192,256]{1,0:T(8,128)(2,1)S(1)} collective-permute-done((bf16[192,256]{1,0:T(8,128)(2,1)S(1)}, bf16[192,256]{1,0:T(8,128)(2,1)S(1)}, u32[]{:S(2)}, u32[]{:S(2)}) %collective-permute-start.9) | collective-permute-done | bytes 98336 | tf_op jit(solution)/shard_map/ppermute | solution.py:214
  81.6 1.2 %collective-permute-start.14 = (bf16[192,256]{1,0:T(8,128)(2,1)S(1)}, bf16[192,256]{1,0:T(8,128)(2,1)S(1)}, u32[]{:S(2)}, u32[]{:S(2)}) collective-permute-start(bf16[192,256]{1,0:T(8,128)(2,1)S(1)} %get-tuple-element.42), channel_id=1, source_target_pairs={{0,13},{1,12},{4,9},{5,8},{8,5},{9,4},{12,1},{13,0},{2,15},{3,14},... | collective-permute-start | bytes 294920 | tf_op jit(solution)/shard_map/ppermute | solution.py:214
  82.9 7.5 %collective-permute-done.13.refs_7_ = bf16[192,256]{1,0:T(8,128)(2,1)S(1)} collective-permute-done((bf16[192,256]{1,0:T(8,128)(2,1)S(1)}, bf16[192,256]{1,0:T(8,128)(2,1)S(1)}, u32[]{:S(2)}, u32[]{:S(2)}) %collective-permute-start.13) | collective-permute-done | bytes 98336 | tf_op jit(solution)/shard_map/ppermute | solution.py:214
  90.3 1.5 %stack.3.refs_1_ = bf16[1024,256]{1,0:T(8,128)(2,1)S(1)} custom-call(f32[8,1536]{1,0:T(8,128)S(1)} %get-tuple-element.34.refs_0_, bf16[192,256]{1,0:T(8,128)(2,1)S(1)} %get-tuple-element.35.refs_1_, bf16[192,256]{1,0:T(8,128)(2,1)S(1)} %collective-permute-done.8.refs_2_, bf16[192,256]{1,0:T(8,128)(2,1)S(1)} %collective-permute-done.9.refs_3_, ...), custom_call_target="tpu_custom_call" | custom-call | tf_op jit(solution)/shard_map/stack/pallas_call | solution.py:140
  92.0 5.7 %operate.4.refs_0_ = f32[512,512]{1,0:T(8,128)S(1)} custom-call(s32[2,4,8]{2,1,0:T(4,128)S(1)} %bitcast.9, bf16[2,4,8,128,128]{4,3,2,1,0:T(8,128)(2,1)S(1)} %bitcast.3, bf16[1024,768]{1,0:T(8,128)(2,1)S(1)} %get-tuple-element.33.refs_0_), custom_call_target="tpu_custom_call" | custom-call | tf_op jit(solution)/shard_map/operate/pallas_call | solution.py:183
  97.7 5.9 %operate.5.refs_0_ = f32[512,512]{1,0:T(8,128)S(1)} custom-call(s32[2,4,8]{2,1,0:T(4,128)S(1)} %bitcast.10, bf16[2,4,8,128,128]{4,3,2,1,0:T(8,128)(2,1)S(1)} %bitcast.4, f32[512,512]{1,0:T(8,128)S(1)} %operate.4.refs_0_, bf16[1024,768]{1,0:T(8,128)(2,1)S(1)} %collective-permute-done.7.refs_1_), custom_call_target="tpu_custom_call", output_to_operand_aliasing={{}: (2, {})} | custom-call | tf_op jit(solution)/shard_map/operate/pallas_call | solution.py:183
  103.6 3.2 %operate.6.refs_0_ = f32[512,512]{1,0:T(8,128)S(1)} custom-call(s32[2,4,8]{2,1,0:T(4,128)S(1)} %bitcast.11, bf16[2,4,8,128,128]{4,3,2,1,0:T(8,128)(2,1)S(1)} %bitcast.5, f32[512,512]{1,0:T(8,128)S(1)} %operate.5.refs_0_, bf16[1024,256]{1,0:T(8,128)(2,1)S(1)} %stack.3.refs_1_), custom_call_target="tpu_custom_call", output_to_operand_aliasing={{}: (2, {})} | custom-call | tf_op jit(solution)/shard_map/operate/pallas_call | solution.py:183
  106.8 2.5 %operate.7 = (f32[512,512]{1,0:T(8,128)S(1)}, bf16[256,512]{1,0:T(8,128)(2,1)S(1)}) custom-call(s32[2,4,8]{2,1,0:T(4,128)S(1)} %bitcast.12, bf16[2,4,8,128,128]{4,3,2,1,0:T(8,128)(2,1)S(1)} %bitcast.6, f32[512,512]{1,0:T(8,128)S(1)} %operate.6.refs_0_, bf16[1024,256]{1,0:T(8,128)(2,1)S(1)} %collective-permute-done.15.refs_1_), custom_call_target="tpu_custom_call", output_to_operand_aliasing={{0}: (2, {})} | custom-call | tf_op jit(solution)/shard_map/operate/pallas_call | solution.py:183
  109.3 1.5 %collective-permute-start.16 = (bf16[256,512]{1,0:T(8,128)(2,1)S(1)}, bf16[256,512]{1,0:T(8,128)(2,1)S(1)}, u32[]{:S(2)}, u32[]{:S(2)}) collective-permute-start(bf16[256,512]{1,0:T(8,128)(2,1)S(1)} %get-tuple-element.44), channel_id=1, source_target_pairs={{0,2},{2,0},{1,3},{3,1},{4,6},{6,4},{5,7},{7,5},{8,10},{10,8},{9,1... | collective-permute-start | bytes 786440 | tf_op jit(solution)/shard_map/ppermute | solution.py:195
  110.8 7.2 %collective-permute-done.16 = bf16[256,512]{1,0:T(8,128)(2,1)S(1)} collective-permute-done((bf16[256,512]{1,0:T(8,128)(2,1)S(1)}, bf16[256,512]{1,0:T(8,128)(2,1)S(1)}, u32[]{:S(2)}, u32[]{:S(2)}) %collective-permute-start.16) | collective-permute-done | bytes 262176 | tf_op jit(solution)/shard_map/ppermute | solution.py:195
  (35 shorter events, 4.2 us)
Async XLA Ops:
  0.7 1.6 %copy-start.1 = (bf16[1,512,2048]{2,1,0:T(8,128)(2,1)S(1)}, bf16[1,512,2048]{2,1,0:T(8,128)(2,1)}, u32[]{:S(2)}) copy-start(bf16[1,512,2048]{2,1,0:T(8,128)(2,1)} %param.6) | copy-start | bytes 6291460
  2.2 0.7 copy-start.4
  3.6 60.5 %copy-start.2 = (bf16[1,512,2048]{2,1,0:T(8,128)(2,1)S(1)}, bf16[1,512,2048]{2,1,0:T(8,128)(2,1)}, u32[]{:S(2)}) copy-start(bf16[1,512,2048]{2,1,0:T(8,128)(2,1)} %param.6) | copy-start | bytes 6291460
  3.6 60.5 %copy-start.5 = (s32[1,512]{1,0:T(1,128)S(1)}, s32[1,512]{1,0:T(1,128)}, u32[]{:S(2)}) copy-start(s32[1,512]{1,0:T(1,128)} %mid_ref.3) | copy-start | bytes 6148
  3.6 60.5 %copy-start.7 = (s32[1,512]{1,0:T(1,128)S(1)}, s32[1,512]{1,0:T(1,128)}, u32[]{:S(2)}) copy-start(s32[1,512]{1,0:T(1,128)} %fine_ref.3) | copy-start | bytes 6148
  5.4 17.5 %collective-permute-start = (bf16[208,768]{1,0:T(8,128)(2,1)S(1)}, bf16[208,768]{1,0:T(8,128)(2,1)S(1)}, u32[]{:S(2)}, u32[]{:S(2)}) collective-permute-start(bf16[208,768]{1,0:T(8,128)(2,1)S(1)} %get-tuple-element.26), channel_id=1, source_target_pairs={{0,4},{1,5},{4,0},{5,1},{8,12},{9,13},{12,8},{13,9},{2,6},{3,7},{6... | collective-permute-start | bytes 958472 | tf_op jit(solution)/shard_map/ppermute | solution.py:214
  8.4 25.1 %collective-permute-start.1 = (bf16[208,768]{1,0:T(8,128)(2,1)S(1)}, bf16[208,768]{1,0:T(8,128)(2,1)S(1)}, u32[]{:S(2)}, u32[]{:S(2)}) collective-permute-start(bf16[208,768]{1,0:T(8,128)(2,1)S(1)} %get-tuple-element.27), channel_id=1, source_target_pairs={{0,8},{1,9},{4,12},{5,13},{8,0},{9,1},{12,4},{13,5},{2,10},{3,11},... | collective-permute-start | bytes 958472 | tf_op jit(solution)/shard_map/ppermute | solution.py:214
  11.0 22.5 %collective-permute-start.2 = (bf16[208,768]{1,0:T(8,128)(2,1)S(1)}, bf16[208,768]{1,0:T(8,128)(2,1)S(1)}, u32[]{:S(2)}, u32[]{:S(2)}) collective-permute-start(bf16[208,768]{1,0:T(8,128)(2,1)S(1)} %get-tuple-element.28), channel_id=1, source_target_pairs={{0,12},{1,13},{4,8},{5,9},{8,4},{9,5},{12,0},{13,1},{2,14},{3,15},... | collective-permute-start | bytes 958472 | tf_op jit(solution)/shard_map/ppermute | solution.py:214
  11.0 22.5 %collective-permute-start.3 = (bf16[208,768]{1,0:T(8,128)(2,1)S(1)}, bf16[208,768]{1,0:T(8,128)(2,1)S(1)}, u32[]{:S(2)}, u32[]{:S(2)}) collective-permute-start(bf16[208,768]{1,0:T(8,128)(2,1)S(1)} %get-tuple-element.29), channel_id=1, source_target_pairs={{0,1},{1,0},{4,5},{5,4},{8,9},{9,8},{12,13},{13,12},{2,3},{3,2},{6... | collective-permute-start | bytes 958472 | tf_op jit(solution)/shard_map/ppermute | solution.py:214
  11.0 26.0 %collective-permute-start.4 = (bf16[208,768]{1,0:T(8,128)(2,1)S(1)}, bf16[208,768]{1,0:T(8,128)(2,1)S(1)}, u32[]{:S(2)}, u32[]{:S(2)}) collective-permute-start(bf16[208,768]{1,0:T(8,128)(2,1)S(1)} %get-tuple-element.30), channel_id=1, source_target_pairs={{0,5},{1,4},{4,1},{5,0},{8,13},{9,12},{12,9},{13,8},{2,7},{3,6},{6... | collective-permute-start | bytes 958472 | tf_op jit(solution)/shard_map/ppermute | solution.py:214
  22.9 35.2 %collective-permute-start.5 = (bf16[208,768]{1,0:T(8,128)(2,1)S(1)}, bf16[208,768]{1,0:T(8,128)(2,1)S(1)}, u32[]{:S(2)}, u32[]{:S(2)}) collective-permute-start(bf16[208,768]{1,0:T(8,128)(2,1)S(1)} %get-tuple-element.31), channel_id=1, source_target_pairs={{0,9},{1,8},{4,13},{5,12},{8,1},{9,0},{12,5},{13,4},{2,11},{3,10},... | collective-permute-start | bytes 958472 | tf_op jit(solution)/shard_map/ppermute | solution.py:214
  33.5 24.5 %collective-permute-start.6 = (bf16[208,768]{1,0:T(8,128)(2,1)S(1)}, bf16[208,768]{1,0:T(8,128)(2,1)S(1)}, u32[]{:S(2)}, u32[]{:S(2)}) collective-permute-start(bf16[208,768]{1,0:T(8,128)(2,1)S(1)} %get-tuple-element.32), channel_id=1, source_target_pairs={{0,13},{1,12},{4,9},{5,8},{8,5},{9,4},{12,1},{13,0},{2,15},{3,14},... | collective-permute-start | bytes 958472 | tf_op jit(solution)/shard_map/ppermute | solution.py:214
  61.4 30.6 %copy-start = (bf16[1,2,1,4,8,128,128]{6,5,4,3,2,1,0:T(8,128)(2,1)S(1)}, bf16[1,2,1,4,8,128,128]{6,5,4,3,2,1,0:T(8,128)(2,1)}, u32[]{:S(2)}) copy-start(bf16[1,2,1,4,8,128,128]{6,5,4,3,2,1,0:T(8,128)(2,1)} %param.10) | copy-start | bytes 6291460
  61.4 30.6 %copy-start.3 = (s32[1,2,1,4,8]{4,3,2,1,0:T(4,128)S(1)}, s32[1,2,1,4,8]{4,3,2,1,0:T(4,128)}, u32[]{:S(2)}) copy-start(s32[1,2,1,4,8]{4,3,2,1,0:T(4,128)} %param.11) | copy-start | bytes 772
  61.4 36.2 %collective-permute-start.7 = (bf16[1024,768]{1,0:T(8,128)(2,1)S(1)}, bf16[1024,768]{1,0:T(8,128)(2,1)S(1)}, u32[]{:S(2)}, u32[]{:S(2)}) collective-permute-start(bf16[1024,768]{1,0:T(8,128)(2,1)S(1)} %get-tuple-element.33.refs_0_), channel_id=1, source_target_pairs={{0,1},{1,0},{2,3},{3,2},{4,5},{5,4},{6,7},{7,6},{8,9},{9,8},{10,11... | collective-permute-start | bytes 4718600 | tf_op jit(solution)/shard_map/ppermute | solution.py:195
  64.9 9.2 %collective-permute-start.8 = (bf16[192,256]{1,0:T(8,128)(2,1)S(1)}, bf16[192,256]{1,0:T(8,128)(2,1)S(1)}, u32[]{:S(2)}, u32[]{:S(2)}) collective-permute-start(bf16[192,256]{1,0:T(8,128)(2,1)S(1)} %get-tuple-element.36), channel_id=1, source_target_pairs={{0,4},{1,5},{4,0},{5,1},{8,12},{9,13},{12,8},{13,9},{2,6},{3,7},{6... | collective-permute-start | bytes 294920 | tf_op jit(solution)/shard_map/ppermute | solution.py:214
  70.9 10.7 %collective-permute-start.9 = (bf16[192,256]{1,0:T(8,128)(2,1)S(1)}, bf16[192,256]{1,0:T(8,128)(2,1)S(1)}, u32[]{:S(2)}, u32[]{:S(2)}) collective-permute-start(bf16[192,256]{1,0:T(8,128)(2,1)S(1)} %get-tuple-element.37), channel_id=1, source_target_pairs={{0,8},{1,9},{4,12},{5,13},{8,0},{9,1},{12,4},{13,5},{2,10},{3,11},... | collective-permute-start | bytes 294920 | tf_op jit(solution)/shard_map/ppermute | solution.py:214
  72.0 9.6 %collective-permute-start.10 = (bf16[192,256]{1,0:T(8,128)(2,1)S(1)}, bf16[192,256]{1,0:T(8,128)(2,1)S(1)}, u32[]{:S(2)}, u32[]{:S(2)}) collective-permute-start(bf16[192,256]{1,0:T(8,128)(2,1)S(1)} %get-tuple-element.38), channel_id=1, source_target_pairs={{0,12},{1,13},{4,8},{5,9},{8,4},{9,5},{12,0},{13,1},{2,14},{3,15},... | collective-permute-start | bytes 294920 | tf_op jit(solution)/shard_map/ppermute | solution.py:214
  73.4 9.5 %collective-permute-start.11 = (bf16[192,256]{1,0:T(8,128)(2,1)S(1)}, bf16[192,256]{1,0:T(8,128)(2,1)S(1)}, u32[]{:S(2)}, u32[]{:S(2)}) collective-permute-start(bf16[192,256]{1,0:T(8,128)(2,1)S(1)} %get-tuple-element.39), channel_id=1, source_target_pairs={{0,1},{1,0},{4,5},{5,4},{8,9},{9,8},{12,13},{13,12},{2,3},{3,2},{6... | collective-permute-start | bytes 294920 | tf_op jit(solution)/shard_map/ppermute | solution.py:214
  74.1 8.8 %collective-permute-start.12 = (bf16[192,256]{1,0:T(8,128)(2,1)S(1)}, bf16[192,256]{1,0:T(8,128)(2,1)S(1)}, u32[]{:S(2)}, u32[]{:S(2)}) collective-permute-start(bf16[192,256]{1,0:T(8,128)(2,1)S(1)} %get-tuple-element.40), channel_id=1, source_target_pairs={{0,5},{1,4},{4,1},{5,0},{8,13},{9,12},{12,9},{13,8},{2,7},{3,6},{6... | collective-permute-start | bytes 294920 | tf_op jit(solution)/shard_map/ppermute | solution.py:214
  81.6 8.7 %collective-permute-start.13 = (bf16[192,256]{1,0:T(8,128)(2,1)S(1)}, bf16[192,256]{1,0:T(8,128)(2,1)S(1)}, u32[]{:S(2)}, u32[]{:S(2)}) collective-permute-start(bf16[192,256]{1,0:T(8,128)(2,1)S(1)} %get-tuple-element.41), channel_id=1, source_target_pairs={{0,9},{1,8},{4,13},{5,12},{8,1},{9,0},{12,5},{13,4},{2,11},{3,10},... | collective-permute-start | bytes 294920 | tf_op jit(solution)/shard_map/ppermute | solution.py:214
  81.6 8.7 %collective-permute-start.14 = (bf16[192,256]{1,0:T(8,128)(2,1)S(1)}, bf16[192,256]{1,0:T(8,128)(2,1)S(1)}, u32[]{:S(2)}, u32[]{:S(2)}) collective-permute-start(bf16[192,256]{1,0:T(8,128)(2,1)S(1)} %get-tuple-element.42), channel_id=1, source_target_pairs={{0,13},{1,12},{4,9},{5,8},{8,5},{9,4},{12,1},{13,0},{2,15},{3,14},... | collective-permute-start | bytes 294920 | tf_op jit(solution)/shard_map/ppermute | solution.py:214
  91.9 14.9 %collective-permute-start.15 = (bf16[1024,256]{1,0:T(8,128)(2,1)S(1)}, bf16[1024,256]{1,0:T(8,128)(2,1)S(1)}, u32[]{:S(2)}, u32[]{:S(2)}) collective-permute-start(bf16[1024,256]{1,0:T(8,128)(2,1)S(1)} %stack.3.refs_1_), channel_id=1, source_target_pairs={{0,1},{1,0},{2,3},{3,2},{4,5},{5,4},{6,7},{7,6},{8,9},{9,8},{10,11... | collective-permute-start | bytes 1572872 | tf_op jit(solution)/shard_map/ppermute | solution.py:195
  109.3 8.7 %collective-permute-start.16 = (bf16[256,512]{1,0:T(8,128)(2,1)S(1)}, bf16[256,512]{1,0:T(8,128)(2,1)S(1)}, u32[]{:S(2)}, u32[]{:S(2)}) collective-permute-start(bf16[256,512]{1,0:T(8,128)(2,1)S(1)} %get-tuple-element.44), channel_id=1, source_target_pairs={{0,2},{2,0},{1,3},{3,1},{4,6},{6,4},{5,7},{7,5},{8,10},{10,8},{9,1... | collective-permute-start | bytes 786440 | tf_op jit(solution)/shard_map/ppermute | solution.py:195
  (1 other events, 0.7 us)

commit v2 on v0

v2 whole, which is shorter than its diff:
```python
import functools

import jax
import jax.numpy as jnp
from jax import lax
from jax.experimental import pallas as pl
from jax.experimental.pallas import tpu as pltpu
from jax.sharding import PartitionSpec as P

FINE = 2
COLS = 512
LINES = 16
TILE = 256
BF = jnp.bfloat16
F32 = jnp.float32
MIB = 1 << 20


def params(mib):
    return pltpu.CompilerParams(vmem_limit_bytes=mib * MIB)


def vmem():
    return pl.BlockSpec(memory_space=pltpu.VMEM)


def smem():
    return pl.BlockSpec(memory_space=pltpu.SMEM)


def call(body, out_shape, operands, scalars, name, mib=24, scratch=(), flops=0, after=()):
    moved = sum(a.size * a.dtype.itemsize for a in (*operands, *out_shape))
    count, late = len(operands), len(after)

    def run(*refs):
        body(*refs[:count], *refs[count + late :])

    return pl.pallas_call(
        run,
        out_shape=list(out_shape),
        in_specs=[smem()] * scalars + [vmem()] * (count - scalars + late),
        out_specs=[vmem()] * len(out_shape),
        scratch_shapes=list(scratch),
        compiler_params=params(mib),
        cost_estimate=pl.CostEstimate(flops=flops, bytes_accessed=moved, transcendentals=0),
        name=name,
    )(*operands, *(corner(a) for a in after))


def corner(a):
    return a[:LINES, :128]


def gate(given, after):
    return pl.pallas_call(
        lambda *refs: None,
        out_shape=[jax.ShapeDtypeStruct(a.shape, a.dtype) for a in given],
        in_specs=[vmem()] * (len(given) + len(after)),
        out_specs=[vmem()] * len(given),
        input_output_aliases={i: i for i in range(len(given))},
        compiler_params=params(4),
        cost_estimate=pl.CostEstimate(flops=0, bytes_accessed=0, transcendentals=0),
        name="gate",
    )(*given, *(corner(a) for a in after))


def shape(rows, columns, kind=BF):
    return jax.ShapeDtypeStruct((rows, columns), kind)


def one_hot(mask):
    return jnp.where(mask, 1.0, 0.0).astype(BF)


def running_count(mask_rows):
    rows = mask_rows.shape[1]
    upper = lax.broadcasted_iota(jnp.int32, (rows, rows), 0) <= lax.broadcasted_iota(jnp.int32, (rows, rows), 1)
    return jnp.dot(one_hot(mask_rows), one_hot(upper), preferred_element_type=F32)


def choose(position, slots):
    place = lax.broadcasted_iota(jnp.int32, (slots, position.shape[1]), 0).astype(F32)
    return one_hot(position == place)


def tag_digits(live, owner, mid, fine, lines=LINES):
    tag = jnp.where(live, fine * COLS + mid - owner * COLS + 1, 0)
    line = lax.broadcasted_iota(jnp.int32, (lines, tag.shape[1]), 0)
    return jnp.where(line == 0, tag // 256, jnp.where(line == 1, tag % 256, 0)).astype(F32).astype(BF)


def across(digits, chosen):
    return lax.dot_general(digits, chosen, (((1,), (1,)), ((), ())), preferred_element_type=F32)


def tag_of(lines):
    lines = lines.astype(F32)
    return 256.0 * lines[0:1] + lines[1:2] - 1.0


def full_pack_kernel(owners, cap, live_ref, mid_ref, fine_ref, traces_ref, *outs):
    z = lax.axis_index("bin")
    rows, samples = traces_ref.shape
    live = lax.broadcasted_iota(jnp.int32, (1, rows), 1) < live_ref[0, 0]
    mid = mid_ref[...]
    owner = mid // COLS
    target = lax.broadcasted_iota(jnp.int32, (max(owners, 16), rows), 0) ^ z
    hits = jnp.where(live, owner, -1) == target
    slot = jnp.where(hits, running_count(hits) - 1.0, -1.0)
    digits = tag_digits(live, owner, mid, fine_ref[...])
    for d in range(owners):
        select = choose(slot[d : d + 1], cap)
        outs[d][0:cap, :] = jnp.dot(select, traces_ref[...], preferred_element_type=F32).astype(BF)
        outs[d][cap : cap + LINES, :] = jnp.zeros((LINES, samples), BF)
        outs[d][cap : cap + LINES, 0:cap] = across(digits, select).astype(BF)


def full_stack_kernel(cap, *refs):
    *given, stacked_ref, rows_ref = refs
    label = jnp.concatenate([tag_of(ref[cap : cap + LINES, 0:cap]) for ref in given], axis=1)
    for i, ref in enumerate(given):
        rows_ref[i * cap : (i + 1) * cap, :] = ref[0:cap, :]

    def tile(t, carry):
        base = pl.multiple_of(t * TILE, TILE)
        line = (lax.broadcasted_iota(jnp.int32, (TILE, 1), 0) + base).astype(F32)
        stacked_ref[pl.ds(base, TILE), :] = jnp.dot(
            one_hot(label == line), rows_ref[...], preferred_element_type=F32
        ).astype(BF)
        return carry

    lax.fori_loop(0, FINE * COLS // TILE, tile, 0)


def image_terms(d, index_ref, ops_ref, stacked_ref):
    fine, _, taps = index_ref.shape
    width = ops_ref.shape[-1]
    columns = stacked_ref.shape[0] // fine
    picked, weights = [], []
    for f in range(fine):
        for k in range(taps):
            at = pl.multiple_of(index_ref[f, d, k] * width, width)
            picked.append(stacked_ref[f * columns : (f + 1) * columns, pl.ds(at, width)])
            weights.append(ops_ref[f, d, k])
    return lax.dot_general(
        jnp.concatenate(picked, axis=1),
        jnp.concatenate(weights, axis=1),
        (((1,), (1,)), ((), ())),
        preferred_element_type=F32,
    )


def operate_kernel(index_ref, ops_ref, stacked_ref, out_ref):
    width = ops_ref.shape[-1]
    for d in range(index_ref.shape[1]):
        terms = image_terms(d, index_ref, ops_ref, stacked_ref)
        out_ref[0 : terms.shape[0], d * width : (d + 1) * width] = terms.astype(out_ref.dtype)


def operate(index, ops, stacked, kind):
    columns, depth = stacked.shape[0] // FINE, ops.shape[1] * ops.shape[-1]
    (out,) = call(
        operate_kernel,
        [shape(columns, depth, kind)],
        [index, ops, stacked],
        1,
        "operate",
        flops=2 * columns * ops.size,
    )
    return out


def send_kernel(index_ref, ops_ref, stacked_ref, *outs):
    width = ops_ref.shape[-1]
    each = outs[0].shape[1]
    for d in range(index_ref.shape[1]):
        piece, at = outs[d * width // each], d * width % each
        piece[:, at : at + width] = image_terms(d, index_ref, ops_ref, stacked_ref).astype(BF)


def finish_kernel(index_ref, ops_ref, stacked_ref, *refs):
    *came, out_ref = refs
    width = ops_ref.shape[-1]
    each = came[0].shape[1]
    for d in range(index_ref.shape[1]):
        piece, at = came[d * width // each], d * width % each
        more = piece[:, at : at + width].astype(F32)
        out_ref[:, d * width : (d + 1) * width] = image_terms(d, index_ref, ops_ref, stacked_ref) + more


def swap(x, axis, mask):
    return lax.ppermute(x, axis, [(i, i ^ mask) for i in range(lax.axis_size(axis))])


def static_path(cap, records, mid_bin, live_count, fine_class, ops, index):
    owners, subs, offs = (lax.axis_size(a) for a in ("bin", "sub", "off"))
    samples = records.shape[1]
    packed = call(
        functools.partial(full_pack_kernel, owners, cap),
        [shape(cap + LINES, samples)] * owners,
        [live_count, mid_bin, fine_class, records],
        1,
        "full_pack",
    )
    arrived = [packed[0]] + [swap(packed[d], "bin", d) for d in range(1, owners)]
    arrived += [swap(a, "sub", e) for e in range(1, subs) for a in arrived]
    (stacked,) = call(
        functools.partial(full_stack_kernel, cap),
        [shape(FINE * COLS, samples)],
        arrived,
        0,
        "full_stack",
        mib=32,
        scratch=[pltpu.VMEM((cap * len(arrived), samples), BF)],
    )
    terms = operate(index, ops, stacked, F32)
    share = COLS // offs
    x = lax.axis_index("off")
    total = lax.dynamic_slice_in_dim(terms, x * share, share, axis=0)
    for k in range(1, offs):
        total = total + swap(lax.dynamic_slice_in_dim(terms, (x ^ k) * share, share, axis=0), "off", k)
    return total


class Slots:
    def __init__(self, cap):
        self.cap = cap
        self.each = 2 * cap // 3
        self.spare = cap - self.each
        self.front = 5 * cap // 12
        self.back = self.each - self.front
        self.near_front = 2 * cap // 3
        self.near_back = cap - self.near_front
        self.first = 2 * self.spare + 2 * self.front + self.near_front
        self.second = 2 * self.back + self.near_back


def positions(q, live_ref, mid_ref):
    rows = mid_ref.shape[1]
    z, x = lax.axis_index("bin"), lax.axis_index("off")
    live = lax.broadcasted_iota(jnp.int32, (1, rows), 1) < live_ref[0, 0]
    mid = mid_ref[...]
    owner = mid // COLS
    share = COLS // 2
    kept = jnp.where((mid - owner * COLS) // share == x, 1, 0)
    kind = jnp.where(live, (owner ^ z) * 2 + kept, -1)
    hits = lax.broadcasted_iota(jnp.int32, (16, rows), 0) == kind
    rank = running_count(hits)
    seat = jnp.where(hits, rank - 1.0, -1.0)
    place, late = [], []
    for d in range(4):
        first, second = seat[2 * d : 2 * d + 1], seat[2 * d + 1 : 2 * d + 2]
        if d < 2:
            place.append(jnp.where(first >= 0, first, jnp.where(second >= 0, q.cap - 1.0 - second, -1.0)))
            continue
        taken = jnp.minimum(rank[2 * d : 2 * d + 1, rows - 1 : rows], float(q.front))
        mirrored = q.each - 1.0 - second
        in_front = (first >= 0) & (first < q.front)
        in_rest = (second >= 0) & (mirrored >= taken)
        place.append(jnp.where(in_front, first, jnp.where(in_rest, mirrored, -1.0)))
        late.append(((first >= q.front) | ((second >= 0) & (mirrored < taken))))
    line = lax.broadcasted_iota(jnp.int32, (16, rows), 0)
    either = jnp.where(late[0] | late[1], 1, 0)
    after = running_count((line == 0) & (either == 1))[0:1]
    spare = jnp.where(either == 1, after - 1.0, -1.0)
    excess = jnp.maximum(after[:, rows - 1 : rows] - q.spare, rank[2:3, rows - 1 : rows] - q.near_front)
    return live, mid, owner, place, spare, late, excess


def lay(ref, rows, tags):
    size = rows.shape[0]
    ref[0:size, :] = rows
    ref[size : size + LINES, :] = jnp.zeros((LINES, ref.shape[1]), BF)
    ref[size : size + LINES, 0 : tags.shape[1]] = tags.astype(BF)


def pack_spare_kernel(q, live_ref, mid_ref, fine_ref, traces_ref, spare_ref, own_ref, flag_ref):
    live, mid, owner, place, spare, late, excess = positions(q, live_ref, mid_ref)
    digits = tag_digits(live, owner, mid, fine_ref[...])
    extra = [choose(jnp.where(late[i], spare, -1.0), q.spare) for i in range(2)]
    tags = [across(digits, jnp.concatenate([choose(place[d], q.each), extra[d - 2]], axis=0)) for d in (2, 3)]
    crossing = jnp.concatenate([tags[0][0:4], tags[1][0:4], jnp.zeros((LINES - 8, q.cap), F32)], axis=0)
    own = choose(place[0], q.cap)
    chosen = jnp.concatenate([extra[0] + extra[1], own], axis=0)
    rows = jnp.dot(chosen, traces_ref[...], preferred_element_type=F32).astype(BF)
    lay(spare_ref, rows[: q.spare], crossing)
    lay(own_ref, rows[q.spare :], across(digits, own))
    flag_ref[...] = jnp.broadcast_to(jnp.where(excess > 0.0, 1.0, 0.0), flag_ref.shape)


def pack_rest_kernel(
    q, live_ref, mid_ref, fine_ref, traces_ref, cross2_ref, cross3_ref, near_ref, back2_ref, back3_ref, near_back_ref
):
    live, mid, owner, place, _, _, _ = positions(q, live_ref, mid_ref)
    digits = tag_digits(live, owner, mid, fine_ref[...])
    near = choose(place[1], q.cap)
    chosen = jnp.concatenate([choose(place[2], q.each), choose(place[3], q.each), near], axis=0)
    rows = jnp.dot(chosen, traces_ref[...], preferred_element_type=F32).astype(BF)
    cross2_ref[...] = rows[: q.front]
    back2_ref[...] = rows[q.front : q.each]
    cross3_ref[...] = rows[q.each : q.each + q.front]
    back3_ref[...] = rows[q.each + q.front : 2 * q.each]
    at = 2 * q.each + q.near_front
    lay(near_ref, rows[2 * q.each : at], across(digits, near))
    near_back_ref[...] = rows[at:]


def relay_kernel(q, spare_ref, flag_ref, out_ref):
    out_ref[0 : q.spare, :] = spare_ref[0 : q.spare, :]
    lines = spare_ref[q.spare : q.spare + LINES, :]
    row = lax.broadcasted_iota(jnp.int32, lines.shape, 0)
    out_ref[q.spare : q.spare + LINES, :] = jnp.where(row == 3, flag_ref[0:1, 0:1].astype(BF), lines)


def gather_kernel(
    q, spare_ref, cross2_ref, cross3_ref, near_ref, relay_ref, own_flag_ref, rows_ref, flag_ref
):
    at = 0
    for ref, size in (
        (spare_ref, q.spare),
        (cross2_ref, q.front),
        (cross3_ref, q.front),
        (near_ref, q.near_front),
        (relay_ref, q.spare),
    ):
        rows_ref[at : at + size, :] = ref[0:size, :]
        at += size
    cross2, cross3, near = (
        ref[size : size + LINES, 0 : q.cap].astype(F32)
        for ref, size in ((spare_ref, q.spare), (relay_ref, q.spare), (near_ref, q.near_front))
    )
    flag_ref[...] = jnp.maximum(own_flag_ref[...], jnp.broadcast_to(cross3[3:4, 0:128], flag_ref.shape))
    cross2, cross3, near = cross2[0:2], cross3[4:6], near[0:2]
    tags = jnp.concatenate(
        [
            cross2[:, q.each :],
            cross2[:, : q.front],
            cross3[:, : q.front],
            near[:, : q.near_front],
            cross3[:, q.each :],
            cross2[:, q.front : q.each],
            cross3[:, q.front : q.each],
            near[:, q.near_front :],
        ],
        axis=1,
    )
    tags = jnp.concatenate([tags, jnp.zeros((LINES - 2, tags.shape[1]), F32)], axis=0)
    rows_ref[at : at + LINES, :] = jnp.zeros((LINES, rows_ref.shape[1]), BF)
    rows_ref[at : at + LINES, 0 : tags.shape[1]] = tags.astype(BF)


def segment_line(f, part):
    base = f * COLS + part * (COLS // 2)
    return (lax.broadcasted_iota(jnp.int32, (COLS // 2, 1), 0) + base).astype(F32)


def stack_into(out_ref, given, part):
    labels = []
    for ref in given:
        count = ref.shape[0] - LINES
        labels.append(tag_of(ref[count : count + LINES, 0:count]))
    share = COLS // 2
    for f in range(FINE):
        line = segment_line(f, part)
        out_ref[f * share : (f + 1) * share, :] = sum(
            jnp.dot(one_hot(label == line), ref[0 : label.shape[1], :], preferred_element_type=F32)
            for label, ref in zip(labels, given)
        ).astype(out_ref.dtype)


def stack_sent_kernel(q, *refs):
    *given, sent_ref, tags_ref = refs
    tags = [tag_of(ref[q.first : q.first + LINES, q.first : q.first + q.second]) for ref in given[:2]]
    tags_ref[...] = jnp.broadcast_to(jnp.concatenate(tags, axis=1), tags_ref.shape)
    stack_into(sent_ref, given, 1 - lax.axis_index("off"))


def stack_kept_kernel(*refs):
    *given, kept_ref = refs
    stack_into(kept_ref, given, lax.axis_index("off"))


def join_kernel(*refs):
    *given, out_ref = refs
    at = 0
    for ref in given:
        out_ref[at : at + ref.shape[0], :] = ref[...]
        at += ref.shape[0]


def stack_second_kernel(q, tags_ref, kept_ref, own_ref, other_ref, out_ref, rows_ref):
    x = lax.axis_index("off")
    rows_ref[: q.second, :] = own_ref[...]
    rows_ref[q.second :, :] = other_ref[...]
    label = tags_ref[0:1, :]
    share = COLS // 2
    for f in range(FINE):
        span = slice(f * share, (f + 1) * share)
        more = jnp.dot(one_hot(label == segment_line(f, x)), rows_ref[...], preferred_element_type=F32)
        out_ref[span, :] = (kept_ref[span, :] + more).astype(BF)


def short_path(cap, records, mid_bin, live_count, fine_class, ops, index):
    q = Slots(cap)
    samples = records.shape[1]
    share, depth = COLS // 2, ops.shape[1] * ops.shape[-1]
    packed, own, flag = call(
        functools.partial(pack_spare_kernel, q),
        [shape(q.spare + LINES, samples), shape(q.cap + LINES, samples), shape(8, 128, F32)],
        [live_count, mid_bin, fine_class, records],
        1,
        "pack_spare",
        flops=2 * (q.spare + q.cap) * records.size,
    )
    spare, own_other = swap(packed, "bin", 2), swap(own, "sub", 1)
    cross2, cross3, near, back2, back3, near_back = call(
        functools.partial(pack_rest_kernel, q),
        [shape(q.front, samples)] * 2
        + [shape(q.near_front + LINES, samples)]
        + [shape(q.back, samples)] * 2
        + [shape(q.near_back, samples)],
        [live_count, mid_bin, fine_class, records],
        1,
        "pack_rest",
        flops=2 * (2 * q.each + q.cap) * records.size,
        after=[packed],
    )
    cross2, cross3, near = swap(cross2, "bin", 2), swap(cross3, "bin", 3), swap(near, "bin", 1)
    for axis in ("sub", "off", "grp"):
        mask = 1
        while mask < lax.axis_size(axis):
            flag = jnp.maximum(flag, swap(flag, axis, mask))
            mask *= 2
    (relay,) = call(
        functools.partial(relay_kernel, q), [shape(q.spare + LINES, samples)], [spare, flag], 0, "relay"
    )
    relay = swap(relay, "bin", 1)
    back2, back3, near_back = gate([back2, back3, near_back], [cross3])
    rows, flag = call(
        functools.partial(gather_kernel, q),
        [shape(q.first + LINES, samples), shape(8, 128, F32)],
        [spare, cross2, cross3, near, relay, flag],
        0,
        "gather",
        after=[back2],
    )
    back2, back3, near_back = swap(back2, "bin", 2), swap(back3, "bin", 3), swap(near_back, "bin", 1)
    given = [rows, swap(rows, "sub", 1), own, own_other]
    flops = 2 * FINE * COLS * (q.first + q.cap) * samples
    sent, tags = call(
        functools.partial(stack_sent_kernel, q),
        [shape(FINE * share, samples), shape(8, 2 * q.second, F32)],
        given,
        0,
        "stack_sent",
        flops=flops,
    )
    terms = call(
        send_kernel,
        [shape(share, depth // 2)] * 2,
        [index, ops, sent],
        1,
        "operate",
        flops=2 * share * ops.size,
    )
    came = [swap(piece, "off", 1) for piece in terms]
    (kept,) = call(
        stack_kept_kernel,
        [shape(FINE * share, samples, F32)],
        given,
        0,
        "stack_kept",
        flops=flops,
        after=[terms[0]],
    )
    flag = jnp.maximum(flag, swap(flag, "bin", 2))
    (late,) = call(
        join_kernel,
        [shape(q.second, samples)],
        [back2, back3, near_back],
        0,
        "join",
        after=[kept, *came, flag],
    )
    (stacked,) = call(
        functools.partial(stack_second_kernel, q),
        [shape(FINE * share, samples)],
        [tags, kept, late, swap(late, "sub", 1)],
        0,
        "stack_second",
        scratch=[pltpu.VMEM((2 * q.second, samples), BF)],
        flops=2 * FINE * COLS * q.second * samples,
    )
    (image,) = call(
        finish_kernel,
        [shape(share, depth, F32)],
        [index, ops, stacked, *came],
        1,
        "finish",
        flops=2 * share * ops.size,
    )
    given = (records, mid_bin, live_count, fine_class, ops, index)
    return lax.cond(flag[0, 0] > 0.0, lambda image, *a: static_path(cap, *a), lambda image, *a: image, image, *given)


def local(traces, mid_bin, live_count, fine_class, operator, block_index):
    records = traces[0]
    owners, offs = lax.axis_size("bin"), lax.axis_size("off")
    cap = 3 * records.shape[0] // (2 * owners)
    path = short_path if owners == 4 and offs == 2 else static_path
    return path(cap, records, mid_bin, live_count, fine_class, operator[0, :, 0], block_index[0, :, 0])


def solution(mesh):
    placed = (
        P(("grp", "off"), ("bin", "sub"), None),
        P(("grp", "off"), ("bin", "sub")),
        P(("grp", "off"), ("bin", "sub")),
        P(("grp", "off"), ("bin", "sub")),
        P(("grp", "off"), None, "bin", "sub", None, None, None),
        P(("grp", "off"), None, "bin", "sub", None),
    )
    return jax.shard_map(
        local,
        mesh=mesh,
        in_specs=placed,
        out_specs=P(("grp", "bin", "off"), "sub"),
        check_vma=False,
    )
```

time: 208 us -> 80.7 us (0.39)
  blocking collectives: 78.8 us -> 0 us
  local copies, waits for them, and re-layouts: 44.8 us -> 1.34 us
  other arithmetic: 30.7 us -> 0.01 us
  starting transfers between devices: 3.3 us -> 23.3 us
  Pallas kernels: 0 us -> 16.4 us
  between operations: 14.3 us -> 1.65 us
  waiting for transfers between devices: 25.9 us -> 37.6 us
  matrix products: 9.66 us -> 0 us
    all_to_all x1 -> x0, blocking collectives: 76.9 us -> none  [local(): lax.all_to_all(buffer, 'bin', split_axis=0, concat_axis=0, tiled=True)]
    ppermute x0 -> x17, waiting for transfers between devices: none -> 37.6 us  [swap(): lax.ppermute(x, axis, [(i, i ^ mask) for i in range(lax.axis_size(axis))])]
    scatter-add x1 -> x0, other arithmetic: 24.8 us -> none  [local(): jax.ops.segment_sum(arrived.astype(jnp.float32), segment, num_segments=FI...]
    ppermute x0 -> x17, starting transfers between devices: none -> 23.3 us  [swap(): lax.ppermute(x, axis, [(i, i ^ mask) for i in range(lax.axis_size(axis))])]
    reduce_scatter x1 -> x0, waiting for transfers between devices: 21.6 us -> none  [local(): lax.psum_scatter(jnp.moveaxis(result, 0, 1).reshape(COLS // lax.axis_size...]
    gather x8 -> x0, local copies, waits for them, and re-layouts: 17.7 us -> none  [pick_blocks(): return jnp.take(columns, chosen, axis=1)]
    pallas_call x0 -> x11, Pallas kernels: none -> 16.4 us  [the longest x10 16.4 us: call(): pl.pallas_call(run, out_shape=list(out_shape), in_specs=[smem()] * scalar...]
    dot_general x4 -> x0, matrix products: 9.66 us -> none  [one_depth(): jnp.einsum('fckq,fkpq->cp', picked, depth_ops, preferred_element_type=jnp...]
  transfers between devices with their start and end apart: 3 -> 17, of which waited for: 3 -> 10; matrix products, arithmetic and copies ran while one was open for 3% -> 1% of each run, Pallas kernels for 0% -> 13%
where the time goes in v2:
time: 80.7 us; the launch traced here: 80.5 us
  waiting for transfers between devices  37.6 us (47%)
  starting transfers between devices  23.3 us (29%)
  Pallas kernels  16.4 us (20%)
  between operations  1.65 us (2%)
  local copies, waits for them, and re-layouts  1.34 us (2%)
    ppermute x17, waiting for transfers between devices, swap(): lax.ppermute(x, axis, [(i, i ^ mask) for i in range(lax.axis_size(axis))])  37.6 us
    ppermute x17, starting transfers between devices, swap(): lax.ppermute(x, axis, [(i, i ^ mask) for i in range(lax.axis_size(axis))])  23.3 us
    pallas_call x10, Pallas kernels, call(): pl.pallas_call(run, out_shape=list(out_shape), in_specs=[smem()] * scalar...  16.4 us
  transfers between devices with their start and end apart: 17, of which 10 were waited for; matrix products, arithmetic and copies ran while one was open for 1% of the time, Pallas kernels for 13%

profile of v2, /device:TPU:0, one launch (start us, length us, event | category | flops | bytes accessed | tf_op | source)
XLA Modules:
  0.0 80.5 jit_solution(10882552405644984072)
XLA Ops:
  0.8 2.8 %pack_spare.1 = (bf16[80,2048]{1,0:T(8,128)(2,1)S(1)}, bf16[208,2048]{1,0:T(8,128)(2,1)S(1)}, f32[8,128]{1,0:T(8,128)S(1)}) custom-call(s32[1,1]{1,0:T(1,128)S(6)} %copy.17.refs_0_, s32[1,512]{1,0:T(1,128)} %refs_1_.3, s32[1,512]{1,0:T(1,128)} %refs_2_.3, bf16[512,2048]{1,0:T(8,128)(2,1)} %bitcast.7), custom_call_target="tpu_custom_call" | custom-call | flops 536870912 | bytes 3284996 | tf_op jit(solution)/shard_map/pack_spare/pallas_call | solution.py:38
  3.6 4.1 %collective-permute-start.8 = (bf16[80,2048]{1,0:T(8,128)(2,1)S(1)}, bf16[80,2048]{1,0:T(8,128)(2,1)S(1)}, u32[]{:S(2)}, u32[]{:S(2)}) collective-permute-start(bf16[80,2048]{1,0:T(8,128)(2,1)S(1)} %get-tuple-element.49), channel_id=1, source_target_pairs={{0,8},{4,12},{8,0},{12,4},{1,9},{5,13},{9,1},{13,5},{2,10},{6,14},... | collective-permute-start | bytes 983048 | tf_op jit(solution)/shard_map/ppermute | solution.py:192
  7.7 1.4 %pack_rest.1 = (bf16[80,2048]{1,0:T(8,128)(2,1)S(1)}, bf16[80,2048]{1,0:T(8,128)(2,1)S(1)}, bf16[144,2048]{1,0:T(8,128)(2,1)S(1)}, bf16[48,2048]{1,0:T(8,128)(2,...) custom-call(s32[1,1]{1,0:T(1,128)S(6)} %copy.17.refs_0_, s32[1,512]{1,0:T(1,128)S(1)} %copy-done.6, ...), custom_call_target="tpu_custom_call" | custom-call | flops 939524096 | bytes 4001796 | tf_op jit(solution)/shard_map/pack_rest/pallas_call | solution.py:38
  9.1 1.6 %collective-permute-start.11 = (bf16[144,2048]{1,0:T(8,128)(2,1)S(1)}, bf16[144,2048]{1,0:T(8,128)(2,1)S(1)}, u32[]{:S(2)}, u32[]{:S(2)}) collective-permute-start(bf16[144,2048]{1,0:T(8,128)(2,1)S(1)} %get-tuple-element.52), channel_id=1, source_target_pairs={{0,4},{4,0},{8,12},{12,8},{1,5},{5,1},{9,13},{13,9},{2,6},{6,2},{1... | collective-permute-start | bytes 1769480 | tf_op jit(solution)/shard_map/ppermute | solution.py:192
  10.7 1.2 %collective-permute-done.12 = f32[8,128]{1,0:T(8,128)S(1)} collective-permute-done((f32[8,128]{1,0:T(8,128)S(1)}, f32[8,128]{1,0:T(8,128)S(1)}, u32[]{:S(2)}, u32[]{:S(2)}) %collective-permute-start.12) | collective-permute-done | bytes 4128 | tf_op jit(solution)/shard_map/ppermute | solution.py:192
  11.9 1.5 %collective-permute-start.13 = (f32[8,128]{1,0:T(8,128)S(1)}, f32[8,128]{1,0:T(8,128)S(1)}, u32[]{:S(2)}, u32[]{:S(2)}) collective-permute-start(f32[8,128]{1,0:T(8,128)S(1)} %max.12), channel_id=1, source_target_pairs={{0,2},{2,0},{1,3},{3,1},{4,6},{6,4},{5,7},{7,5},{8,10},{10,8},{9,1... | collective-permute-start | bytes 12296 | tf_op jit(solution)/shard_map/ppermute | solution.py:192
  13.4 2.1 %collective-permute-done.13 = f32[8,128]{1,0:T(8,128)S(1)} collective-permute-done((f32[8,128]{1,0:T(8,128)S(1)}, f32[8,128]{1,0:T(8,128)S(1)}, u32[]{:S(2)}, u32[]{:S(2)}) %collective-permute-start.13) | collective-permute-done | bytes 4128 | tf_op jit(solution)/shard_map/ppermute | solution.py:192
  15.5 1.5 %collective-permute-start.14 = (f32[8,128]{1,0:T(8,128)S(1)}, f32[8,128]{1,0:T(8,128)S(1)}, u32[]{:S(2)}, u32[]{:S(2)}) collective-permute-start(f32[8,128]{1,0:T(8,128)S(1)} %max.13), channel_id=1, source_target_pairs={{0,16},{16,0},{1,17},{17,1},{2,18},{18,2},{3,19},{19,3},{4,20},{20... | collective-permute-start | bytes 12296 | tf_op jit(solution)/shard_map/ppermute | solution.py:192
  17.3 1.7 %collective-permute-start.9 = (bf16[80,2048]{1,0:T(8,128)(2,1)S(1)}, bf16[80,2048]{1,0:T(8,128)(2,1)S(1)}, u32[]{:S(2)}, u32[]{:S(2)}) collective-permute-start(bf16[80,2048]{1,0:T(8,128)(2,1)S(1)} %get-tuple-element.50), channel_id=1, source_target_pairs={{0,8},{4,12},{8,0},{12,4},{1,9},{5,13},{9,1},{13,5},{2,10},{6,14},... | collective-permute-start | bytes 983048 | tf_op jit(solution)/shard_map/ppermute | solution.py:192
  19.1 4.2 %collective-permute-done.8.refs_0_ = bf16[80,2048]{1,0:T(8,128)(2,1)S(1)} collective-permute-done((bf16[80,2048]{1,0:T(8,128)(2,1)S(1)}, bf16[80,2048]{1,0:T(8,128)(2,1)S(1)}, u32[]{:S(2)}, u32[]{:S(2)}) %collective-permute-start.8) | collective-permute-done | bytes 327712 | tf_op jit(solution)/shard_map/ppermute | solution.py:192
  23.5 13.9 %collective-permute-done.10.refs_2_ = bf16[80,2048]{1,0:T(8,128)(2,1)S(1)} collective-permute-done((bf16[80,2048]{1,0:T(8,128)(2,1)S(1)}, bf16[80,2048]{1,0:T(8,128)(2,1)S(1)}, u32[]{:S(2)}, u32[]{:S(2)}) %collective-permute-start.10) | collective-permute-done | bytes 327712 | tf_op jit(solution)/shard_map/ppermute | solution.py:192
  37.4 13.3 %collective-permute-done.9.refs_1_ = bf16[80,2048]{1,0:T(8,128)(2,1)S(1)} collective-permute-done((bf16[80,2048]{1,0:T(8,128)(2,1)S(1)}, bf16[80,2048]{1,0:T(8,128)(2,1)S(1)}, u32[]{:S(2)}, u32[]{:S(2)}) %collective-permute-start.9) | collective-permute-done | bytes 327712 | tf_op jit(solution)/shard_map/ppermute | solution.py:192
  51.6 2.9 %collective-permute-start.19 = (bf16[48,2048]{1,0:T(8,128)(2,1)S(1)}, bf16[48,2048]{1,0:T(8,128)(2,1)S(1)}, u32[]{:S(2)}, u32[]{:S(2)}) collective-permute-start(bf16[48,2048]{1,0:T(8,128)(2,1)S(1)} %get-tuple-element.57), channel_id=1, source_target_pairs={{0,8},{4,12},{8,0},{12,4},{1,9},{5,13},{9,1},{13,5},{2,10},{6,14},... | collective-permute-start | bytes 589832 | tf_op jit(solution)/shard_map/ppermute | solution.py:192
  54.5 0.9 %collective-permute-start.21 = (bf16[64,2048]{1,0:T(8,128)(2,1)S(1)}, bf16[64,2048]{1,0:T(8,128)(2,1)S(1)}, u32[]{:S(2)}, u32[]{:S(2)}) collective-permute-start(bf16[64,2048]{1,0:T(8,128)(2,1)S(1)} %get-tuple-element.65), channel_id=1, source_target_pairs={{0,4},{4,0},{8,12},{12,8},{1,5},{5,1},{9,13},{13,9},{2,6},{6,2},{1... | collective-permute-start | bytes 786440 | tf_op jit(solution)/shard_map/ppermute | solution.py:192
  56.1 5.9 %collective-permute-start.20 = (bf16[48,2048]{1,0:T(8,128)(2,1)S(1)}, bf16[48,2048]{1,0:T(8,128)(2,1)S(1)}, u32[]{:S(2)}, u32[]{:S(2)}) collective-permute-start(bf16[48,2048]{1,0:T(8,128)(2,1)S(1)} %get-tuple-element.64), channel_id=1, source_target_pairs={{0,12},{4,8},{8,4},{12,0},{1,13},{5,9},{9,5},{13,1},{2,14},{6,10},... | collective-permute-start | bytes 589832 | tf_op jit(solution)/shard_map/ppermute | solution.py:192
  62.1 3.4 %stack_sent.1 = (bf16[512,2048]{1,0:T(8,128)(2,1)S(1)}, f32[8,320]{1,0:T(8,128)S(1)}) custom-call(bf16[432,2048]{1,0:T(8,128)(2,1)S(1)} %get-tuple-element.59.refs_0_, bf16[432,2048]{1,0:T(8,128)(2,1)S(1)} %collective-permute-done.17.refs_1_, bf16[208,2048]{1,0:T(8,128)(2,1)S(1)} %get-tuple-element.60.refs_2_, ...), custom_call_target="tpu_custom_call" | custom-call | flops 2550136832 | bytes 7350272 | tf_op jit(solution)/shard_map/stack_sent/pallas_call | solution.py:38
  65.5 1.9 %operate.3 = (bf16[256,256]{1,0:T(8,128)(2,1)S(1)}, bf16[256,256]{1,0:T(8,128)(2,1)S(1)}) custom-call(s32[2,4,8]{2,1,0:T(4,128)S(1)} %bitcast.10, bf16[2,4,8,128,128]{4,3,2,1,0:T(8,128)(2,1)S(1)} %bitcast.4, bf16[512,2048]{1,0:T(8,128)(2,1)S(1)} %get-tuple-element.62.refs_2_), custom_call_target="tpu_custom_call" | custom-call | flops 536870912 | bytes 4456704 | tf_op jit(solution)/shard_map/operate/pallas_call | solution.py:38
  67.5 1.6 %collective-permute-start.22 = (bf16[256,256]{1,0:T(8,128)(2,1)S(1)}, bf16[256,256]{1,0:T(8,128)(2,1)S(1)}, u32[]{:S(2)}, u32[]{:S(2)}) collective-permute-start(bf16[256,256]{1,0:T(8,128)(2,1)S(1)} %get-tuple-element.63), channel_id=1, source_target_pairs={{0,2},{2,0},{1,3},{3,1},{4,6},{6,4},{5,7},{7,5},{8,10},{10,8},{9,1... | collective-permute-start | bytes 393224 | tf_op jit(solution)/shard_map/ppermute | solution.py:192
  69.6 3.4 %stack_kept.1.refs_1_ = f32[512,2048]{1,0:T(8,128)S(1)} custom-call(bf16[432,2048]{1,0:T(8,128)(2,1)S(1)} %get-tuple-element.59.refs_0_, bf16[432,2048]{1,0:T(8,128)(2,1)S(1)} %collective-permute-done.17.refs_1_, bf16[208,2048]{1,0:T(8,128)(2,1)S(1)} %get-tuple-element.60.refs_2_, bf16[208,2048]{1,0:T(8,128)(2,1)S(1)} %collective-permute-done.18.refs_3_, ...), custom_call_target="tpu_custom_call" | custom-call | flops 2550136832 | bytes 9437184 | tf_op jit(solution)/shard_map/stack_kept/pallas_call | solution.py:38
  73.0 1.0 %collective-permute-done.23.refs_4_ = bf16[256,256]{1,0:T(8,128)(2,1)S(1)} collective-permute-done((bf16[256,256]{1,0:T(8,128)(2,1)S(1)}, bf16[256,256]{1,0:T(8,128)(2,1)S(1)}, u32[]{:S(2)}, u32[]{:S(2)}) %collective-permute-start.23) | collective-permute-done | bytes 131104 | tf_op jit(solution)/shard_map/ppermute | solution.py:192
  75.3 0.9 %collective-permute-done.24.refs_3_ = bf16[160,2048]{1,0:T(8,128)(2,1)S(1)} collective-permute-done((bf16[160,2048]{1,0:T(8,128)(2,1)S(1)}, bf16[160,2048]{1,0:T(8,128)(2,1)S(1)}, u32[]{:S(2)}, u32[]{:S(2)}) %collective-permute-start.24) | collective-permute-done | bytes 655392 | tf_op jit(solution)/shard_map/ppermute | solution.py:192
  76.3 1.3 %stack_second.1.refs_2_ = bf16[512,2048]{1,0:T(8,128)(2,1)S(1)} custom-call(f32[8,320]{1,0:T(8,128)S(1)} %get-tuple-element.61.refs_0_, f32[512,2048]{1,0:T(8,128)S(1)} %stack_kept.1.refs_1_, bf16[160,2048]{1,0:T(8,128)(2,1)S(1)} %join.1.refs_2_, bf16[160,2048]{1,0:T(8,128)(2,1)S(1)} %collective-permute-done.24.refs_3_), custom_call_target="tpu_custom_call" | custom-call | flops 671088640 | bytes 7612416 | tf_op jit(solution)/shard_map/stack_second/pallas_call | solution.py:38
  77.6 1.9 %finish.1 = f32[256,512]{1,0:T(8,128)S(1)} custom-call(s32[2,4,8]{2,1,0:T(4,128)S(1)} %bitcast.11, bf16[2,4,8,128,128]{4,3,2,1,0:T(8,128)(2,1)S(1)} %bitcast.5, bf16[512,2048]{1,0:T(8,128)(2,1)S(1)} %stack_second.1.refs_2_, bf16[256,256]{1,0:T(8,128)(2,1)S(1)} %collective-permute-done.22.refs_3_, bf16[256,256]{1,0:T(8,128)(2,1)S(1)} %collective-permute-done.23.refs_4_), custom_call_target="tpu_custom_call" | custom-call | flops 536870912 | bytes 4980992 | tf_op jit(solution)/shard_map/finish/pallas_call | solution.py:38
  79.7 0.8 copy-done.4
  (46 shorter events, 3.4 us)
Async XLA Ops:
  0.0 7.7 %copy-start.3 = (bf16[1,512,2048]{2,1,0:T(8,128)(2,1)S(1)}, bf16[1,512,2048]{2,1,0:T(8,128)(2,1)}, u32[]{:S(2)}) copy-start(bf16[1,512,2048]{2,1,0:T(8,128)(2,1)} %param.8) | copy-start | bytes 6291460
  0.0 7.7 %copy-start.7 = (s32[1,512]{1,0:T(1,128)S(1)}, s32[1,512]{1,0:T(1,128)}, u32[]{:S(2)}) copy-start(s32[1,512]{1,0:T(1,128)} %refs_2_.3) | copy-start | bytes 6148
  0.0 7.7 %copy-start.6 = (s32[1,512]{1,0:T(1,128)S(1)}, s32[1,512]{1,0:T(1,128)}, u32[]{:S(2)}) copy-start(s32[1,512]{1,0:T(1,128)} %refs_1_.3) | copy-start | bytes 6148
  3.6 19.7 %collective-permute-start.8 = (bf16[80,2048]{1,0:T(8,128)(2,1)S(1)}, bf16[80,2048]{1,0:T(8,128)(2,1)S(1)}, u32[]{:S(2)}, u32[]{:S(2)}) collective-permute-start(bf16[80,2048]{1,0:T(8,128)(2,1)S(1)} %get-tuple-element.49), channel_id=1, source_target_pairs={{0,8},{4,12},{8,0},{12,4},{1,9},{5,13},{9,1},{13,5},{2,10},{6,14},... | collective-permute-start | bytes 983048 | tf_op jit(solution)/shard_map/ppermute | solution.py:192
  9.1 41.6 %collective-permute-start.11 = (bf16[144,2048]{1,0:T(8,128)(2,1)S(1)}, bf16[144,2048]{1,0:T(8,128)(2,1)S(1)}, u32[]{:S(2)}, u32[]{:S(2)}) collective-permute-start(bf16[144,2048]{1,0:T(8,128)(2,1)S(1)} %get-tuple-element.52), channel_id=1, source_target_pairs={{0,4},{4,0},{8,12},{12,8},{1,5},{5,1},{9,13},{13,9},{2,6},{6,2},{1... | collective-permute-start | bytes 1769480 | tf_op jit(solution)/shard_map/ppermute | solution.py:192
  10.7 1.2 %collective-permute-start.12 = (f32[8,128]{1,0:T(8,128)S(1)}, f32[8,128]{1,0:T(8,128)S(1)}, u32[]{:S(2)}, u32[]{:S(2)}) collective-permute-start(f32[8,128]{1,0:T(8,128)S(1)} %get-tuple-element.53), channel_id=1, source_target_pairs={{0,1},{1,0},{2,3},{3,2},{4,5},{5,4},{6,7},{7,6},{8,9},{9,8},{10,11... | collective-permute-start | bytes 12296 | tf_op jit(solution)/shard_map/ppermute | solution.py:192
  11.9 3.6 %collective-permute-start.13 = (f32[8,128]{1,0:T(8,128)S(1)}, f32[8,128]{1,0:T(8,128)S(1)}, u32[]{:S(2)}, u32[]{:S(2)}) collective-permute-start(f32[8,128]{1,0:T(8,128)S(1)} %max.12), channel_id=1, source_target_pairs={{0,2},{2,0},{1,3},{3,1},{4,6},{6,4},{5,7},{7,5},{8,10},{10,8},{9,1... | collective-permute-start | bytes 12296 | tf_op jit(solution)/shard_map/ppermute | solution.py:192
  15.5 3.6 %collective-permute-start.14 = (f32[8,128]{1,0:T(8,128)S(1)}, f32[8,128]{1,0:T(8,128)S(1)}, u32[]{:S(2)}, u32[]{:S(2)}) collective-permute-start(f32[8,128]{1,0:T(8,128)S(1)} %max.13), channel_id=1, source_target_pairs={{0,16},{16,0},{1,17},{17,1},{2,18},{18,2},{3,19},{19,3},{4,20},{20... | collective-permute-start | bytes 12296 | tf_op jit(solution)/shard_map/ppermute | solution.py:192
  17.1 20.3 %collective-permute-start.10 = (bf16[80,2048]{1,0:T(8,128)(2,1)S(1)}, bf16[80,2048]{1,0:T(8,128)(2,1)S(1)}, u32[]{:S(2)}, u32[]{:S(2)}) collective-permute-start(bf16[80,2048]{1,0:T(8,128)(2,1)S(1)} %get-tuple-element.51), channel_id=1, source_target_pairs={{0,12},{4,8},{8,4},{12,0},{1,13},{5,9},{9,5},{13,1},{2,14},{6,10},... | collective-permute-start | bytes 983048 | tf_op jit(solution)/shard_map/ppermute | solution.py:192
  17.3 33.4 %collective-permute-start.9 = (bf16[80,2048]{1,0:T(8,128)(2,1)S(1)}, bf16[80,2048]{1,0:T(8,128)(2,1)S(1)}, u32[]{:S(2)}, u32[]{:S(2)}) collective-permute-start(bf16[80,2048]{1,0:T(8,128)(2,1)S(1)} %get-tuple-element.50), channel_id=1, source_target_pairs={{0,8},{4,12},{8,0},{12,4},{1,9},{5,13},{9,1},{13,5},{2,10},{6,14},... | collective-permute-start | bytes 983048 | tf_op jit(solution)/shard_map/ppermute | solution.py:192
  23.4 27.5 %collective-permute-start.15 = (bf16[80,2048]{1,0:T(8,128)(2,1)S(1)}, bf16[80,2048]{1,0:T(8,128)(2,1)S(1)}, u32[]{:S(2)}, u32[]{:S(2)}) collective-permute-start(bf16[80,2048]{1,0:T(8,128)(2,1)S(1)} %relay.1), channel_id=1, source_target_pairs={{0,4},{4,0},{8,12},{12,8},{1,5},{5,1},{9,13},{13,9},{2,6},{6,2},{1... | collective-permute-start | bytes 983048 | tf_op jit(solution)/shard_map/ppermute | solution.py:192
  51.0 11.1 %collective-permute-start.17 = (bf16[432,2048]{1,0:T(8,128)(2,1)S(1)}, bf16[432,2048]{1,0:T(8,128)(2,1)S(1)}, u32[]{:S(2)}, u32[]{:S(2)}) collective-permute-start(bf16[432,2048]{1,0:T(8,128)(2,1)S(1)} %get-tuple-element.59.refs_0_), channel_id=1, source_target_pairs={{0,1},{1,0},{2,3},{3,2},{4,5},{5,4},{6,7},{7,6},{8,9},{9,8},{10,11... | collective-permute-start | bytes 5308424 | tf_op jit(solution)/shard_map/ppermute | solution.py:192
  51.1 11.0 %collective-permute-start.18 = (bf16[208,2048]{1,0:T(8,128)(2,1)S(1)}, bf16[208,2048]{1,0:T(8,128)(2,1)S(1)}, u32[]{:S(2)}, u32[]{:S(2)}) collective-permute-start(bf16[208,2048]{1,0:T(8,128)(2,1)S(1)} %get-tuple-element.60.refs_2_), channel_id=1, source_target_pairs={{0,1},{1,0},{2,3},{3,2},{4,5},{5,4},{6,7},{7,6},{8,9},{9,8},{10,11... | collective-permute-start | bytes 2555912 | tf_op jit(solution)/shard_map/ppermute | solution.py:192
  51.6 4.5 %collective-permute-start.16 = (f32[8,128]{1,0:T(8,128)S(1)}, f32[8,128]{1,0:T(8,128)S(1)}, u32[]{:S(2)}, u32[]{:S(2)}) collective-permute-start(f32[8,128]{1,0:T(8,128)S(1)} %get-tuple-element.58), channel_id=1, source_target_pairs={{0,8},{4,12},{8,0},{12,4},{1,9},{5,13},{9,1},{13,5},{2,10},{6,14},... | collective-permute-start | bytes 12296 | tf_op jit(solution)/shard_map/ppermute | solution.py:192
  51.6 22.4 %collective-permute-start.19 = (bf16[48,2048]{1,0:T(8,128)(2,1)S(1)}, bf16[48,2048]{1,0:T(8,128)(2,1)S(1)}, u32[]{:S(2)}, u32[]{:S(2)}) collective-permute-start(bf16[48,2048]{1,0:T(8,128)(2,1)S(1)} %get-tuple-element.57), channel_id=1, source_target_pairs={{0,8},{4,12},{8,0},{12,4},{1,9},{5,13},{9,1},{13,5},{2,10},{6,14},... | collective-permute-start | bytes 589832 | tf_op jit(solution)/shard_map/ppermute | solution.py:192
  54.5 19.5 %collective-permute-start.21 = (bf16[64,2048]{1,0:T(8,128)(2,1)S(1)}, bf16[64,2048]{1,0:T(8,128)(2,1)S(1)}, u32[]{:S(2)}, u32[]{:S(2)}) collective-permute-start(bf16[64,2048]{1,0:T(8,128)(2,1)S(1)} %get-tuple-element.65), channel_id=1, source_target_pairs={{0,4},{4,0},{8,12},{12,8},{1,5},{5,1},{9,13},{13,9},{2,6},{6,2},{1... | collective-permute-start | bytes 786440 | tf_op jit(solution)/shard_map/ppermute | solution.py:192
  56.1 17.9 %collective-permute-start.20 = (bf16[48,2048]{1,0:T(8,128)(2,1)S(1)}, bf16[48,2048]{1,0:T(8,128)(2,1)S(1)}, u32[]{:S(2)}, u32[]{:S(2)}) collective-permute-start(bf16[48,2048]{1,0:T(8,128)(2,1)S(1)} %get-tuple-element.64), channel_id=1, source_target_pairs={{0,12},{4,8},{8,4},{12,0},{1,13},{5,9},{9,5},{13,1},{2,14},{6,10},... | collective-permute-start | bytes 589832 | tf_op jit(solution)/shard_map/ppermute | solution.py:192
  62.1 3.4 %copy-start = (bf16[1,2,1,4,8,128,128]{6,5,4,3,2,1,0:T(8,128)(2,1)S(1)}, bf16[1,2,1,4,8,128,128]{6,5,4,3,2,1,0:T(8,128)(2,1)}, u32[]{:S(2)}) copy-start(bf16[1,2,1,4,8,128,128]{6,5,4,3,2,1,0:T(8,128)(2,1)} %param.12) | copy-start | bytes 6291460
  62.1 3.5 %copy-start.5 = (s32[1,2,1,4,8]{4,3,2,1,0:T(4,128)S(1)}, s32[1,2,1,4,8]{4,3,2,1,0:T(4,128)}, u32[]{:S(2)}) copy-start(s32[1,2,1,4,8]{4,3,2,1,0:T(4,128)} %param.13) | copy-start | bytes 772
  67.5 5.5 %collective-permute-start.22 = (bf16[256,256]{1,0:T(8,128)(2,1)S(1)}, bf16[256,256]{1,0:T(8,128)(2,1)S(1)}, u32[]{:S(2)}, u32[]{:S(2)}) collective-permute-start(bf16[256,256]{1,0:T(8,128)(2,1)S(1)} %get-tuple-element.63), channel_id=1, source_target_pairs={{0,2},{2,0},{1,3},{3,1},{4,6},{6,4},{5,7},{7,5},{8,10},{10,8},{9,1... | collective-permute-start | bytes 393224 | tf_op jit(solution)/shard_map/ppermute | solution.py:192
  69.1 5.0 %collective-permute-start.23 = (bf16[256,256]{1,0:T(8,128)(2,1)S(1)}, bf16[256,256]{1,0:T(8,128)(2,1)S(1)}, u32[]{:S(2)}, u32[]{:S(2)}) collective-permute-start(bf16[256,256]{1,0:T(8,128)(2,1)S(1)} %get-tuple-element.66), channel_id=1, source_target_pairs={{0,2},{2,0},{1,3},{3,1},{4,6},{6,4},{5,7},{7,5},{8,10},{10,8},{9,1... | collective-permute-start | bytes 393224 | tf_op jit(solution)/shard_map/ppermute | solution.py:192
  74.1 2.2 %collective-permute-start.24 = (bf16[160,2048]{1,0:T(8,128)(2,1)S(1)}, bf16[160,2048]{1,0:T(8,128)(2,1)S(1)}, u32[]{:S(2)}, u32[]{:S(2)}) collective-permute-start(bf16[160,2048]{1,0:T(8,128)(2,1)S(1)} %join.1.refs_2_), channel_id=1, source_target_pairs={{0,1},{1,0},{2,3},{3,2},{4,5},{5,4},{6,7},{7,6},{8,9},{9,8},{10,11... | collective-permute-start | bytes 1966088 | tf_op jit(solution)/shard_map/ppermute | solution.py:192
  79.7 0.8 copy-start.4

commit v3 on v2

--- a/solution.py
+++ b/solution.py
@@ -274,7 +274,22 @@
     ref[size : size + LINES, 0 : tags.shape[1]] = tags.astype(BF)
 
 
-def pack_spare_kernel(q, live_ref, mid_ref, fine_ref, traces_ref, spare_ref, own_ref, flag_ref):
+def pack_spare_kernel(
+    q, live_ref, mid_hbm, fine_hbm, traces_ref, spare_ref, lines_ref, own_ref, flag_ref, held_ref, mid_ref, fine_ref, sems
+):
+    copies = [
+        pltpu.make_async_copy(mid_hbm, mid_ref, sems.at[0]),
+        pltpu.make_async_copy(fine_hbm, fine_ref, sems.at[1]),
+    ]
+    count = sems.shape[0] - 2
+    step = held_ref.shape[0] // count
+    for i in range(count):
+        span = pl.ds(i * step, step)
+        copies.append(pltpu.make_async_copy(traces_ref.at[span], held_ref.at[span], sems.at[i + 2]))
+    for copy in copies:
+        copy.start()
+    for copy in copies[:2]:
+        copy.wait()
     live, mid, owner, place, spare, late, excess = positions(q, live_ref, mid_ref)
     digits = tag_digits(live, owner, mid, fine_ref[...])
     extra = [choose(jnp.where(late[i], spare, -1.0), q.spare) for i in range(2)]
@@ -282,8 +297,12 @@
     crossing = jnp.concatenate([tags[0][0:4], tags[1][0:4], jnp.zeros((LINES - 8, q.cap), F32)], axis=0)
     own = choose(place[0], q.cap)
     chosen = jnp.concatenate([extra[0] + extra[1], own], axis=0)
-    rows = jnp.dot(chosen, traces_ref[...], preferred_element_type=F32).astype(BF)
-    lay(spare_ref, rows[: q.spare], crossing)
+    lines_ref[...] = jnp.zeros(lines_ref.shape, BF)
+    lines_ref[:, 0 : q.cap] = crossing.astype(BF)
+    for copy in copies[2:]:
+        copy.wait()
+    rows = jnp.dot(chosen, held_ref[...], preferred_element_type=F32).astype(BF)
+    spare_ref[...] = rows[: q.spare]
     lay(own_ref, rows[q.spare :], across(digits, own))
     flag_ref[...] = jnp.broadcast_to(jnp.where(excess > 0.0, 1.0, 0.0), flag_ref.shape)
 
@@ -305,15 +324,17 @@
     near_back_ref[...] = rows[at:]
 
 
-def relay_kernel(q, spare_ref, flag_ref, out_ref):
-    out_ref[0 : q.spare, :] = spare_ref[0 : q.spare, :]
-    lines = spare_ref[q.spare : q.spare + LINES, :]
-    row = lax.broadcasted_iota(jnp.int32, lines.shape, 0)
-    out_ref[q.spare : q.spare + LINES, :] = jnp.where(row == 3, flag_ref[0:1, 0:1].astype(BF), lines)
+def relay_kernel(q, spare_ref, lines_ref, flag_ref, out_ref):
+    out_ref[0 : q.spare, :] = spare_ref[...]
+    row = lax.broadcasted_iota(jnp.int32, lines_ref.shape, 0)
+    out_ref[q.spare : q.spare + LINES, :] = jnp.zeros((LINES, out_ref.shape[1]), BF)
+    out_ref[q.spare : q.spare + LINES, 0 : lines_ref.shape[1]] = jnp.where(
+        row == 3, flag_ref[0:1, 0:1].astype(BF), lines_ref[...]
+    )
 
 
 def gather_kernel(
-    q, spare_ref, cross2_ref, cross3_ref, near_ref, relay_ref, own_flag_ref, rows_ref, flag_ref
+    q, spare_ref, lines_ref, cross2_ref, cross3_ref, near_ref, relay_ref, own_flag_ref, rows_ref, flag_ref
 ):
     at = 0
     for ref, size in (
@@ -327,7 +348,7 @@
         at += size
     cross2, cross3, near = (
         ref[size : size + LINES, 0 : q.cap].astype(F32)
-        for ref, size in ((spare_ref, q.spare), (relay_ref, q.spare), (near_ref, q.near_front))
+        for ref, size in ((lines_ref, 0), (relay_ref, q.spare), (near_ref, q.near_front))
     )
     flag_ref[...] = jnp.maximum(own_flag_ref[...], jnp.broadcast_to(cross3[3:4, 0:128], flag_ref.shape))
     cross2, cross3, near = cross2[0:2], cross3[4:6], near[0:2]
@@ -404,22 +425,33 @@
     q = Slots(cap)
     samples = records.shape[1]
     share, depth = COLS // 2, ops.shape[1] * ops.shape[-1]
-    packed, own, flag = call(
+    packed, lines, own, flag, held = pl.pallas_call(
         functools.partial(pack_spare_kernel, q),
-        [shape(q.spare + LINES, samples), shape(q.cap + LINES, samples), shape(8, 128, F32)],
-        [live_count, mid_bin, fine_class, records],
-        1,
-        "pack_spare",
-        flops=2 * (q.spare + q.cap) * records.size,
-    )
-    spare, own_other = swap(packed, "bin", 2), swap(own, "sub", 1)
+        out_shape=[
+            shape(q.spare, samples),
+            shape(LINES, TILE),
+            shape(q.cap + LINES, samples),
+            shape(8, 128, F32),
+            shape(*records.shape),
+        ],
+        in_specs=[smem()] + [pl.BlockSpec(memory_space=pltpu.HBM)] * 3,
+        out_specs=[vmem()] * 5,
+        scratch_shapes=[
+            pltpu.VMEM(mid_bin.shape, jnp.int32),
+            pltpu.VMEM(fine_class.shape, jnp.int32),
+            pltpu.SemaphoreType.DMA((10,)),
+        ],
+        compiler_params=params(24),
+        name="pack_spare",
+    )(live_count, mid_bin, fine_class, records)
+    spare, lines, own_other = swap(packed, "bin", 2), swap(lines, "bin", 2), swap(own, "sub", 1)
     cross2, cross3, near, back2, back3, near_back = call(
         functools.partial(pack_rest_kernel, q),
         [shape(q.front, samples)] * 2
         + [shape(q.near_front + LINES, samples)]
         + [shape(q.back, samples)] * 2
         + [shape(q.near_back, samples)],
-        [live_count, mid_bin, fine_class, records],
+        [live_count, mid_bin, fine_class, held],
         1,
         "pack_rest",
         flops=2 * (2 * q.each + q.cap) * records.size,
@@ -432,18 +464,19 @@
             flag = jnp.maximum(flag, swap(flag, axis, mask))
             mask *= 2
     (relay,) = call(
-        functools.partial(relay_kernel, q), [shape(q.spare + LINES, samples)], [spare, flag], 0, "relay"
+        functools.partial(relay_kernel, q), [shape(q.spare + LINES, samples)], [spare, lines, flag], 0, "relay"
     )
     relay = swap(relay, "bin", 1)
     back2, back3, near_back = gate([back2, back3, near_back], [cross3])
     rows, flag = call(
         functools.partial(gather_kernel, q),
         [shape(q.first + LINES, samples), shape(8, 128, F32)],
-        [spare, cross2, cross3, near, relay, flag],
+        [spare, lines, cross2, cross3, near, relay, flag],
         0,
         "gather",
-        after=[back2],
-    )
+        after=[back2, own_other],
+    )
+    flag = jnp.maximum(flag, swap(flag, "bin", 2))
     back2, back3, near_back = swap(back2, "bin", 2), swap(back3, "bin", 3), swap(near_back, "bin", 1)
     given = [rows, swap(rows, "sub", 1), own, own_other]
     flops = 2 * FINE * COLS * (q.first + q.cap) * samples
@@ -454,6 +487,7 @@
         0,
         "stack_sent",
         flops=flops,
+        after=[flag],
     )
     terms = call(
         send_kernel,
@@ -473,14 +507,13 @@
         flops=flops,
         after=[terms[0]],
     )
-    flag = jnp.maximum(flag, swap(flag, "bin", 2))
     (late,) = call(
         join_kernel,
         [shape(q.second, samples)],
         [back2, back3, near_back],
         0,
         "join",
-        after=[kept, *came, flag],
+        after=[kept, *came],
     )
     (stacked,) = call(
         functools.partial(stack_second_kernel, q),

time: 80.7 us -> 77 us (0.954)
  starting transfers between devices: 23.3 us -> 21.1 us
  waiting for transfers between devices: 37.6 us -> 36.7 us
    pallas_call x10 -> x9, Pallas kernels: 16.4 us -> 13.6 us  [call(): pl.pallas_call(run, out_shape=list(out_shape), in_specs=[smem()] * scalar...]
    pallas_call x0 -> x1, Pallas kernels: none -> 2.34 us  [short_path(): pl.pallas_call(functools.partial(pack_spare_kernel, q), out_shape=[shape(...]
    ppermute x17 -> x18, starting transfers between devices: 23.3 us -> 21.1 us  [swap(): lax.ppermute(x, axis, [(i, i ^ mask) for i in range(lax.axis_size(axis))])]
    ppermute x17 -> x18, waiting for transfers between devices: 37.6 us -> 36.7 us  [swap(): lax.ppermute(x, axis, [(i, i ^ mask) for i in range(lax.axis_size(axis))])]
  transfers between devices with their start and end apart: 17 -> 18, of which waited for: 10 -> 11; matrix products, arithmetic and copies ran while one was open for 1% -> 1% of each run, Pallas kernels for 13% -> 13%
where the time goes in v3:
time: 77 us; the launch traced here: 76.8 us
  waiting for transfers between devices  36.7 us (48%)
  starting transfers between devices  21.1 us (27%)
  Pallas kernels  15.9 us (21%)
  between operations  1.53 us (2%)
  local copies, waits for them, and re-layouts  1.34 us (2%)
    ppermute x18, waiting for transfers between devices, swap(): lax.ppermute(x, axis, [(i, i ^ mask) for i in range(lax.axis_size(axis))])  36.7 us
    ppermute x18, starting transfers between devices, swap(): lax.ppermute(x, axis, [(i, i ^ mask) for i in range(lax.axis_size(axis))])  21.1 us
    pallas_call x9, Pallas kernels, call(): pl.pallas_call(run, out_shape=list(out_shape), in_specs=[smem()] * scalar...  13.6 us
    pallas_call x1, Pallas kernels, short_path(): pl.pallas_call(functools.partial(pack_spare_kernel, q), out_shape=[shape(...  2.34 us
  transfers between devices with their start and end apart: 18, of which 11 were waited for; matrix products, arithmetic and copies ran while one was open for 1% of the time, Pallas kernels for 13%

profile of v3, /device:TPU:0, one launch (start us, length us, event | category | flops | bytes accessed | tf_op | source)
XLA Modules:
  0.0 76.8 jit_solution(10105222307858773883)
XLA Ops:
  0.7 2.3 %pack_spare.1 = (bf16[64,2048]{1,0:T(8,128)(2,1)S(1)}, bf16[16,256]{1,0:T(8,128)(2,1)S(1)}, bf16[208,2048]{1,0:T(8,128)(2,1)S(1)}, f32[8,128]{1,0:T(8,128)S(1)}, bf16[512,2048]{1,0:T(8,128)(2,1)S(1)}) custom-call(s32[1,1]{1,0:T(1,128)S(6)} %copy.17.live_ref.refs_0_, s32[1,512]{1,0:T(1,128)} %refs_1_.1, s32[1,512]{1,0:T(1,128)} %refs_2_.1, ...), custom_call_target="tpu_custom_call" | custom-call | tf_op jit(solution)/shard_map/pack_spare/pallas_call | solution.py:428
  3.6 3.7 %collective-permute-start.8 = (bf16[64,2048]{1,0:T(8,128)(2,1)S(1)}, bf16[64,2048]{1,0:T(8,128)(2,1)S(1)}, u32[]{:S(2)}, u32[]{:S(2)}) collective-permute-start(bf16[64,2048]{1,0:T(8,128)(2,1)S(1)} %get-tuple-element.51), channel_id=1, source_target_pairs={{0,8},{4,12},{8,0},{12,4},{1,9},{5,13},{9,1},{13,5},{2,10},{6,14},... | collective-permute-start | bytes 786440 | tf_op jit(solution)/shard_map/ppermute | solution.py:192
  7.2 1.4 %pack_rest.1 = (bf16[80,2048]{1,0:T(8,128)(2,1)S(1)}, bf16[80,2048]{1,0:T(8,128)(2,1)S(1)}, bf16[144,2048]{1,0:T(8,128)(2,1)S(1)}, bf16[48,2048]{1,0:T(8,128)(2,...) custom-call(s32[1,1]{1,0:T(1,128)S(6)} %copy.17.live_ref.refs_0_, s32[1,512]{1,0:T(1,128)S(1)} %copy-done.6, ...), custom_call_target="tpu_custom_call" | custom-call | flops 939524096 | bytes 4001796 | tf_op jit(solution)/shard_map/pack_rest/pallas_call | solution.py:38
  8.6 1.6 %collective-permute-start.12 = (bf16[144,2048]{1,0:T(8,128)(2,1)S(1)}, bf16[144,2048]{1,0:T(8,128)(2,1)S(1)}, u32[]{:S(2)}, u32[]{:S(2)}) collective-permute-start(bf16[144,2048]{1,0:T(8,128)(2,1)S(1)} %get-tuple-element.56), channel_id=1, source_target_pairs={{0,4},{4,0},{8,12},{12,8},{1,5},{5,1},{9,13},{13,9},{2,6},{6,2},{1... | collective-permute-start | bytes 1769480 | tf_op jit(solution)/shard_map/ppermute | solution.py:192
  10.2 1.2 %collective-permute-done.13 = f32[8,128]{1,0:T(8,128)S(1)} collective-permute-done((f32[8,128]{1,0:T(8,128)S(1)}, f32[8,128]{1,0:T(8,128)S(1)}, u32[]{:S(2)}, u32[]{:S(2)}) %collective-permute-start.13) | collective-permute-done | bytes 4128 | tf_op jit(solution)/shard_map/ppermute | solution.py:192
  11.4 1.5 %collective-permute-start.14 = (f32[8,128]{1,0:T(8,128)S(1)}, f32[8,128]{1,0:T(8,128)S(1)}, u32[]{:S(2)}, u32[]{:S(2)}) collective-permute-start(f32[8,128]{1,0:T(8,128)S(1)} %max.12), channel_id=1, source_target_pairs={{0,2},{2,0},{1,3},{3,1},{4,6},{6,4},{5,7},{7,5},{8,10},{10,8},{9,1... | collective-permute-start | bytes 12296 | tf_op jit(solution)/shard_map/ppermute | solution.py:192
  13.2 1.8 %collective-permute-done.14 = f32[8,128]{1,0:T(8,128)S(1)} collective-permute-done((f32[8,128]{1,0:T(8,128)S(1)}, f32[8,128]{1,0:T(8,128)S(1)}, u32[]{:S(2)}, u32[]{:S(2)}) %collective-permute-start.14) | collective-permute-done | bytes 4128 | tf_op jit(solution)/shard_map/ppermute | solution.py:192
  15.0 1.5 %collective-permute-start.15 = (f32[8,128]{1,0:T(8,128)S(1)}, f32[8,128]{1,0:T(8,128)S(1)}, u32[]{:S(2)}, u32[]{:S(2)}) collective-permute-start(f32[8,128]{1,0:T(8,128)S(1)} %max.13), channel_id=1, source_target_pairs={{0,16},{16,0},{1,17},{17,1},{2,18},{18,2},{3,19},{19,3},{4,20},{20... | collective-permute-start | bytes 12296 | tf_op jit(solution)/shard_map/ppermute | solution.py:192
  16.5 2.1 %collective-permute-done.15 = f32[8,128]{1,0:T(8,128)S(1)} collective-permute-done((f32[8,128]{1,0:T(8,128)S(1)}, f32[8,128]{1,0:T(8,128)S(1)}, u32[]{:S(2)}, u32[]{:S(2)}) %collective-permute-start.15) | collective-permute-done | bytes 4128 | tf_op jit(solution)/shard_map/ppermute | solution.py:192
  19.3 7.4 %collective-permute-done.9.refs_1_ = bf16[16,256]{1,0:T(8,128)(2,1)S(1)} collective-permute-done((bf16[16,256]{1,0:T(8,128)(2,1)S(1)}, bf16[16,256]{1,0:T(8,128)(2,1)S(1)}, u32[]{:S(2)}, u32[]{:S(2)}) %collective-permute-start.9) | collective-permute-done | bytes 8224 | tf_op jit(solution)/shard_map/ppermute | solution.py:192
  26.7 3.5 %collective-permute-start.10 = (bf16[80,2048]{1,0:T(8,128)(2,1)S(1)}, bf16[80,2048]{1,0:T(8,128)(2,1)S(1)}, u32[]{:S(2)}, u32[]{:S(2)}) collective-permute-start(bf16[80,2048]{1,0:T(8,128)(2,1)S(1)} %get-tuple-element.54), channel_id=1, source_target_pairs={{0,8},{4,12},{8,0},{12,4},{1,9},{5,13},{9,1},{13,5},{2,10},{6,14},... | collective-permute-start | bytes 983048 | tf_op jit(solution)/shard_map/ppermute | solution.py:192
  30.3 5.3 %collective-permute-done.11.refs_3_ = bf16[80,2048]{1,0:T(8,128)(2,1)S(1)} collective-permute-done((bf16[80,2048]{1,0:T(8,128)(2,1)S(1)}, bf16[80,2048]{1,0:T(8,128)(2,1)S(1)}, u32[]{:S(2)}, u32[]{:S(2)}) %collective-permute-start.11) | collective-permute-done | bytes 327712 | tf_op jit(solution)/shard_map/ppermute | solution.py:192
  35.7 13.6 %collective-permute-done.10.refs_2_ = bf16[80,2048]{1,0:T(8,128)(2,1)S(1)} collective-permute-done((bf16[80,2048]{1,0:T(8,128)(2,1)S(1)}, bf16[80,2048]{1,0:T(8,128)(2,1)S(1)}, u32[]{:S(2)}, u32[]{:S(2)}) %collective-permute-start.10) | collective-permute-done | bytes 327712 | tf_op jit(solution)/shard_map/ppermute | solution.py:192
  50.6 2.3 %collective-permute-start.20 = (bf16[48,2048]{1,0:T(8,128)(2,1)S(1)}, bf16[48,2048]{1,0:T(8,128)(2,1)S(1)}, u32[]{:S(2)}, u32[]{:S(2)}) collective-permute-start(bf16[48,2048]{1,0:T(8,128)(2,1)S(1)} %get-tuple-element.61), channel_id=1, source_target_pairs={{0,8},{4,12},{8,0},{12,4},{1,9},{5,13},{9,1},{13,5},{2,10},{6,14},... | collective-permute-start | bytes 589832 | tf_op jit(solution)/shard_map/ppermute | solution.py:192
  53.1 2.3 %collective-permute-start.21 = (bf16[48,2048]{1,0:T(8,128)(2,1)S(1)}, bf16[48,2048]{1,0:T(8,128)(2,1)S(1)}, u32[]{:S(2)}, u32[]{:S(2)}) collective-permute-start(bf16[48,2048]{1,0:T(8,128)(2,1)S(1)} %get-tuple-element.68), channel_id=1, source_target_pairs={{0,12},{4,8},{8,4},{12,0},{1,13},{5,9},{9,5},{13,1},{2,14},{6,10},... | collective-permute-start | bytes 589832 | tf_op jit(solution)/shard_map/ppermute | solution.py:192
  55.4 3.4 %stack_sent.1 = (bf16[512,2048]{1,0:T(8,128)(2,1)S(1)}, f32[8,320]{1,0:T(8,128)S(1)}) custom-call(bf16[432,2048]{1,0:T(8,128)(2,1)S(1)} %get-tuple-element.64.refs_0_, bf16[432,2048]{1,0:T(8,128)(2,1)S(1)} %collective-permute-done.19.refs_1_, bf16[208,2048]{1,0:T(8,128)(2,1)S(1)} %get-tuple-element.62.refs_2_, ...), custom_call_target="tpu_custom_call" | custom-call | flops 2550136832 | bytes 7350272 | tf_op jit(solution)/shard_map/stack_sent/pallas_call | solution.py:38
  58.9 1.9 %operate.3 = (bf16[256,256]{1,0:T(8,128)(2,1)S(1)}, bf16[256,256]{1,0:T(8,128)(2,1)S(1)}) custom-call(s32[2,4,8]{2,1,0:T(4,128)S(1)} %bitcast.9, bf16[2,4,8,128,128]{4,3,2,1,0:T(8,128)(2,1)S(1)} %bitcast.4, bf16[512,2048]{1,0:T(8,128)(2,1)S(1)} %get-tuple-element.66.refs_2_), custom_call_target="tpu_custom_call" | custom-call | flops 536870912 | bytes 4456704 | tf_op jit(solution)/shard_map/operate/pallas_call | solution.py:38
  60.9 1.5 %collective-permute-start.23 = (bf16[256,256]{1,0:T(8,128)(2,1)S(1)}, bf16[256,256]{1,0:T(8,128)(2,1)S(1)}, u32[]{:S(2)}, u32[]{:S(2)}) collective-permute-start(bf16[256,256]{1,0:T(8,128)(2,1)S(1)} %get-tuple-element.67), channel_id=1, source_target_pairs={{0,2},{2,0},{1,3},{3,1},{4,6},{6,4},{5,7},{7,5},{8,10},{10,8},{9,1... | collective-permute-start | bytes 393224 | tf_op jit(solution)/shard_map/ppermute | solution.py:192
  62.9 3.4 %stack_kept.1.refs_1_ = f32[512,2048]{1,0:T(8,128)S(1)} custom-call(bf16[432,2048]{1,0:T(8,128)(2,1)S(1)} %get-tuple-element.64.refs_0_, bf16[432,2048]{1,0:T(8,128)(2,1)S(1)} %collective-permute-done.19.refs_1_, bf16[208,2048]{1,0:T(8,128)(2,1)S(1)} %get-tuple-element.62.refs_2_, bf16[208,2048]{1,0:T(8,128)(2,1)S(1)} %collective-permute-done.17.refs_3_, ...), custom_call_target="tpu_custom_call" | custom-call | flops 2550136832 | bytes 9437184 | tf_op jit(solution)/shard_map/stack_kept/pallas_call | solution.py:38
  66.4 1.0 %collective-permute-done.23.refs_3_ = bf16[256,256]{1,0:T(8,128)(2,1)S(1)} collective-permute-done((bf16[256,256]{1,0:T(8,128)(2,1)S(1)}, bf16[256,256]{1,0:T(8,128)(2,1)S(1)}, u32[]{:S(2)}, u32[]{:S(2)}) %collective-permute-start.23) | collective-permute-done | bytes 131104 | tf_op jit(solution)/shard_map/ppermute | solution.py:192
  67.3 1.4 %collective-permute-done.24.refs_4_ = bf16[256,256]{1,0:T(8,128)(2,1)S(1)} collective-permute-done((bf16[256,256]{1,0:T(8,128)(2,1)S(1)}, bf16[256,256]{1,0:T(8,128)(2,1)S(1)}, u32[]{:S(2)}, u32[]{:S(2)}) %collective-permute-start.24) | collective-permute-done | bytes 131104 | tf_op jit(solution)/shard_map/ppermute | solution.py:192
  68.7 1.6 %collective-permute-done.21.refs_1_ = bf16[48,2048]{1,0:T(8,128)(2,1)S(1)} collective-permute-done((bf16[48,2048]{1,0:T(8,128)(2,1)S(1)}, bf16[48,2048]{1,0:T(8,128)(2,1)S(1)}, u32[]{:S(2)}, u32[]{:S(2)}) %collective-permute-start.21) | collective-permute-done | bytes 196640 | tf_op jit(solution)/shard_map/ppermute | solution.py:192
  72.6 1.3 %stack_second.1.refs_2_ = bf16[512,2048]{1,0:T(8,128)(2,1)S(1)} custom-call(f32[8,320]{1,0:T(8,128)S(1)} %get-tuple-element.65.refs_0_, f32[512,2048]{1,0:T(8,128)S(1)} %stack_kept.1.refs_1_, bf16[160,2048]{1,0:T(8,128)(2,1)S(1)} %join.1.refs_2_, bf16[160,2048]{1,0:T(8,128)(2,1)S(1)} %collective-permute-done.25.refs_3_), custom_call_target="tpu_custom_call" | custom-call | flops 671088640 | bytes 7612416 | tf_op jit(solution)/shard_map/stack_second/pallas_call | solution.py:38
  73.9 1.9 %finish.1 = f32[256,512]{1,0:T(8,128)S(1)} custom-call(s32[2,4,8]{2,1,0:T(4,128)S(1)} %bitcast.10, bf16[2,4,8,128,128]{4,3,2,1,0:T(8,128)(2,1)S(1)} %bitcast.5, bf16[512,2048]{1,0:T(8,128)(2,1)S(1)} %stack_second.1.refs_2_, bf16[256,256]{1,0:T(8,128)(2,1)S(1)} %collective-permute-done.23.refs_3_, bf16[256,256]{1,0:T(8,128)(2,1)S(1)} %collective-permute-done.24.refs_4_), custom_call_target="tpu_custom_call" | custom-call | flops 536870912 | bytes 4980992 | tf_op jit(solution)/shard_map/finish/pallas_call | solution.py:38
  (49 shorter events, 6.3 us)
Async XLA Ops:
  0.0 7.2 %copy-start.7 = (s32[1,512]{1,0:T(1,128)S(1)}, s32[1,512]{1,0:T(1,128)}, u32[]{:S(2)}) copy-start(s32[1,512]{1,0:T(1,128)} %refs_2_.1) | copy-start | bytes 6148
  0.0 7.2 %copy-start.6 = (s32[1,512]{1,0:T(1,128)S(1)}, s32[1,512]{1,0:T(1,128)}, u32[]{:S(2)}) copy-start(s32[1,512]{1,0:T(1,128)} %refs_1_.1) | copy-start | bytes 6148
  3.0 32.7 %collective-permute-start.17 = (bf16[208,2048]{1,0:T(8,128)(2,1)S(1)}, bf16[208,2048]{1,0:T(8,128)(2,1)S(1)}, u32[]{:S(2)}, u32[]{:S(2)}) collective-permute-start(bf16[208,2048]{1,0:T(8,128)(2,1)S(1)} %get-tuple-element.62.refs_2_), channel_id=1, source_target_pairs={{0,1},{1,0},{2,3},{3,2},{4,5},{5,4},{6,7},{7,6},{8,9},{9,8},{10,11... | collective-permute-start | bytes 2555912 | tf_op jit(solution)/shard_map/ppermute | solution.py:192
  3.6 26.6 %collective-permute-start.8 = (bf16[64,2048]{1,0:T(8,128)(2,1)S(1)}, bf16[64,2048]{1,0:T(8,128)(2,1)S(1)}, u32[]{:S(2)}, u32[]{:S(2)}) collective-permute-start(bf16[64,2048]{1,0:T(8,128)(2,1)S(1)} %get-tuple-element.51), channel_id=1, source_target_pairs={{0,8},{4,12},{8,0},{12,4},{1,9},{5,13},{9,1},{13,5},{2,10},{6,14},... | collective-permute-start | bytes 786440 | tf_op jit(solution)/shard_map/ppermute | solution.py:192
  8.6 41.1 %collective-permute-start.12 = (bf16[144,2048]{1,0:T(8,128)(2,1)S(1)}, bf16[144,2048]{1,0:T(8,128)(2,1)S(1)}, u32[]{:S(2)}, u32[]{:S(2)}) collective-permute-start(bf16[144,2048]{1,0:T(8,128)(2,1)S(1)} %get-tuple-element.56), channel_id=1, source_target_pairs={{0,4},{4,0},{8,12},{12,8},{1,5},{5,1},{9,13},{13,9},{2,6},{6,2},{1... | collective-permute-start | bytes 1769480 | tf_op jit(solution)/shard_map/ppermute | solution.py:192
  10.2 1.2 %collective-permute-start.13 = (f32[8,128]{1,0:T(8,128)S(1)}, f32[8,128]{1,0:T(8,128)S(1)}, u32[]{:S(2)}, u32[]{:S(2)}) collective-permute-start(f32[8,128]{1,0:T(8,128)S(1)} %get-tuple-element.57), channel_id=1, source_target_pairs={{0,1},{1,0},{2,3},{3,2},{4,5},{5,4},{6,7},{7,6},{8,9},{9,8},{10,11... | collective-permute-start | bytes 12296 | tf_op jit(solution)/shard_map/ppermute | solution.py:192
  11.4 3.6 %collective-permute-start.14 = (f32[8,128]{1,0:T(8,128)S(1)}, f32[8,128]{1,0:T(8,128)S(1)}, u32[]{:S(2)}, u32[]{:S(2)}) collective-permute-start(f32[8,128]{1,0:T(8,128)S(1)} %max.12), channel_id=1, source_target_pairs={{0,2},{2,0},{1,3},{3,1},{4,6},{6,4},{5,7},{7,5},{8,10},{10,8},{9,1... | collective-permute-start | bytes 12296 | tf_op jit(solution)/shard_map/ppermute | solution.py:192
  12.9 13.8 %collective-permute-start.9 = (bf16[16,256]{1,0:T(8,128)(2,1)S(1)}, bf16[16,256]{1,0:T(8,128)(2,1)S(1)}, u32[]{:S(2)}, u32[]{:S(2)}) collective-permute-start(bf16[16,256]{1,0:T(8,128)(2,1)S(1)} %get-tuple-element.52), channel_id=1, source_target_pairs={{0,8},{4,12},{8,0},{12,4},{1,9},{5,13},{9,1},{13,5},{2,10},{6,14},... | collective-permute-start | bytes 24584 | tf_op jit(solution)/shard_map/ppermute | solution.py:192
  15.0 3.6 %collective-permute-start.15 = (f32[8,128]{1,0:T(8,128)S(1)}, f32[8,128]{1,0:T(8,128)S(1)}, u32[]{:S(2)}, u32[]{:S(2)}) collective-permute-start(f32[8,128]{1,0:T(8,128)S(1)} %max.13), channel_id=1, source_target_pairs={{0,16},{16,0},{1,17},{17,1},{2,18},{18,2},{3,19},{19,3},{4,20},{20... | collective-permute-start | bytes 12296 | tf_op jit(solution)/shard_map/ppermute | solution.py:192
  18.6 17.1 %collective-permute-start.11 = (bf16[80,2048]{1,0:T(8,128)(2,1)S(1)}, bf16[80,2048]{1,0:T(8,128)(2,1)S(1)}, u32[]{:S(2)}, u32[]{:S(2)}) collective-permute-start(bf16[80,2048]{1,0:T(8,128)(2,1)S(1)} %get-tuple-element.55), channel_id=1, source_target_pairs={{0,12},{4,8},{8,4},{12,0},{1,13},{5,9},{9,5},{13,1},{2,14},{6,10},... | collective-permute-start | bytes 983048 | tf_op jit(solution)/shard_map/ppermute | solution.py:192
  26.7 22.6 %collective-permute-start.10 = (bf16[80,2048]{1,0:T(8,128)(2,1)S(1)}, bf16[80,2048]{1,0:T(8,128)(2,1)S(1)}, u32[]{:S(2)}, u32[]{:S(2)}) collective-permute-start(bf16[80,2048]{1,0:T(8,128)(2,1)S(1)} %get-tuple-element.54), channel_id=1, source_target_pairs={{0,8},{4,12},{8,0},{12,4},{1,9},{5,13},{9,1},{13,5},{2,10},{6,14},... | collective-permute-start | bytes 983048 | tf_op jit(solution)/shard_map/ppermute | solution.py:192
  30.3 19.5 %collective-permute-start.16 = (bf16[80,2048]{1,0:T(8,128)(2,1)S(1)}, bf16[80,2048]{1,0:T(8,128)(2,1)S(1)}, u32[]{:S(2)}, u32[]{:S(2)}) collective-permute-start(bf16[80,2048]{1,0:T(8,128)(2,1)S(1)} %relay.1), channel_id=1, source_target_pairs={{0,4},{4,0},{8,12},{12,8},{1,5},{5,1},{9,13},{13,9},{2,6},{6,2},{1... | collective-permute-start | bytes 983048 | tf_op jit(solution)/shard_map/ppermute | solution.py:192
  49.9 5.6 %collective-permute-start.19 = (bf16[432,2048]{1,0:T(8,128)(2,1)S(1)}, bf16[432,2048]{1,0:T(8,128)(2,1)S(1)}, u32[]{:S(2)}, u32[]{:S(2)}) collective-permute-start(bf16[432,2048]{1,0:T(8,128)(2,1)S(1)} %get-tuple-element.64.refs_0_), channel_id=1, source_target_pairs={{0,1},{1,0},{2,3},{3,2},{4,5},{5,4},{6,7},{7,6},{8,9},{9,8},{10,11... | collective-permute-start | bytes 5308424 | tf_op jit(solution)/shard_map/ppermute | solution.py:192
  49.9 5.5 %collective-permute-start.18 = (f32[8,128]{1,0:T(8,128)S(1)}, f32[8,128]{1,0:T(8,128)S(1)}, u32[]{:S(2)}, u32[]{:S(2)}) collective-permute-start(f32[8,128]{1,0:T(8,128)S(1)} %get-tuple-element.63), channel_id=1, source_target_pairs={{0,8},{4,12},{8,0},{12,4},{1,9},{5,13},{9,1},{13,5},{2,10},{6,14},... | collective-permute-start | bytes 12296 | tf_op jit(solution)/shard_map/ppermute | solution.py:192
  50.6 18.1 %collective-permute-start.20 = (bf16[48,2048]{1,0:T(8,128)(2,1)S(1)}, bf16[48,2048]{1,0:T(8,128)(2,1)S(1)}, u32[]{:S(2)}, u32[]{:S(2)}) collective-permute-start(bf16[48,2048]{1,0:T(8,128)(2,1)S(1)} %get-tuple-element.61), channel_id=1, source_target_pairs={{0,8},{4,12},{8,0},{12,4},{1,9},{5,13},{9,1},{13,5},{2,10},{6,14},... | collective-permute-start | bytes 589832 | tf_op jit(solution)/shard_map/ppermute | solution.py:192
  52.9 17.4 %collective-permute-start.22 = (bf16[64,2048]{1,0:T(8,128)(2,1)S(1)}, bf16[64,2048]{1,0:T(8,128)(2,1)S(1)}, u32[]{:S(2)}, u32[]{:S(2)}) collective-permute-start(bf16[64,2048]{1,0:T(8,128)(2,1)S(1)} %get-tuple-element.69), channel_id=1, source_target_pairs={{0,4},{4,0},{8,12},{12,8},{1,5},{5,1},{9,13},{13,9},{2,6},{6,2},{1... | collective-permute-start | bytes 786440 | tf_op jit(solution)/shard_map/ppermute | solution.py:192
  53.1 17.2 %collective-permute-start.21 = (bf16[48,2048]{1,0:T(8,128)(2,1)S(1)}, bf16[48,2048]{1,0:T(8,128)(2,1)S(1)}, u32[]{:S(2)}, u32[]{:S(2)}) collective-permute-start(bf16[48,2048]{1,0:T(8,128)(2,1)S(1)} %get-tuple-element.68), channel_id=1, source_target_pairs={{0,12},{4,8},{8,4},{12,0},{1,13},{5,9},{9,5},{13,1},{2,14},{6,10},... | collective-permute-start | bytes 589832 | tf_op jit(solution)/shard_map/ppermute | solution.py:192
  55.4 3.5 %copy-start = (bf16[1,2,1,4,8,128,128]{6,5,4,3,2,1,0:T(8,128)(2,1)S(1)}, bf16[1,2,1,4,8,128,128]{6,5,4,3,2,1,0:T(8,128)(2,1)}, u32[]{:S(2)}) copy-start(bf16[1,2,1,4,8,128,128]{6,5,4,3,2,1,0:T(8,128)(2,1)} %param.12) | copy-start | bytes 6291460
  55.4 3.5 %copy-start.5 = (s32[1,2,1,4,8]{4,3,2,1,0:T(4,128)S(1)}, s32[1,2,1,4,8]{4,3,2,1,0:T(4,128)}, u32[]{:S(2)}) copy-start(s32[1,2,1,4,8]{4,3,2,1,0:T(4,128)} %param.13) | copy-start | bytes 772
  60.9 6.5 %collective-permute-start.23 = (bf16[256,256]{1,0:T(8,128)(2,1)S(1)}, bf16[256,256]{1,0:T(8,128)(2,1)S(1)}, u32[]{:S(2)}, u32[]{:S(2)}) collective-permute-start(bf16[256,256]{1,0:T(8,128)(2,1)S(1)} %get-tuple-element.67), channel_id=1, source_target_pairs={{0,2},{2,0},{1,3},{3,1},{4,6},{6,4},{5,7},{7,5},{8,10},{10,8},{9,1... | collective-permute-start | bytes 393224 | tf_op jit(solution)/shard_map/ppermute | solution.py:192
  62.4 6.3 %collective-permute-start.24 = (bf16[256,256]{1,0:T(8,128)(2,1)S(1)}, bf16[256,256]{1,0:T(8,128)(2,1)S(1)}, u32[]{:S(2)}, u32[]{:S(2)}) collective-permute-start(bf16[256,256]{1,0:T(8,128)(2,1)S(1)} %get-tuple-element.70), channel_id=1, source_target_pairs={{0,2},{2,0},{1,3},{3,1},{4,6},{6,4},{5,7},{7,5},{8,10},{10,8},{9,1... | collective-permute-start | bytes 393224 | tf_op jit(solution)/shard_map/ppermute | solution.py:192
  70.4 2.2 %collective-permute-start.25 = (bf16[160,2048]{1,0:T(8,128)(2,1)S(1)}, bf16[160,2048]{1,0:T(8,128)(2,1)S(1)}, u32[]{:S(2)}, u32[]{:S(2)}) collective-permute-start(bf16[160,2048]{1,0:T(8,128)(2,1)S(1)} %join.1.refs_2_), channel_id=1, source_target_pairs={{0,1},{1,0},{2,3},{3,2},{4,5},{5,4},{6,7},{7,6},{8,9},{9,8},{10,11... | collective-permute-start | bytes 1966088 | tf_op jit(solution)/shard_map/ppermute | solution.py:192
  73.9 2.0 %copy-start.3 = (bf16[1,512,2048]{2,1,0:T(8,128)(2,1)S(1)}, bf16[1,512,2048]{2,1,0:T(8,128)(2,1)}, u32[]{:S(2)}) copy-start(bf16[1,512,2048]{2,1,0:T(8,128)(2,1)} %param.8) | copy-start | bytes 6291460
  76.0 0.8 %copy-start.4 = (f32[256,512]{1,0:T(8,128)}, f32[256,512]{1,0:T(8,128)S(1)}, u32[]{:S(2)}) copy-start(f32[256,512]{1,0:T(8,128)S(1)} %get-tuple-element.116) | copy-start | bytes 1572868

commit v4 on v3

--- a/solution.py
+++ b/solution.py
@@ -247,23 +247,29 @@
     hits = lax.broadcasted_iota(jnp.int32, (16, rows), 0) == kind
     rank = running_count(hits)
     seat = jnp.where(hits, rank - 1.0, -1.0)
-    place, late = [], []
+    place, late, spare = [], [], -1.0
+    base = jnp.zeros((1, 1), F32)
     for d in range(4):
         first, second = seat[2 * d : 2 * d + 1], seat[2 * d + 1 : 2 * d + 2]
         if d < 2:
             place.append(jnp.where(first >= 0, first, jnp.where(second >= 0, q.cap - 1.0 - second, -1.0)))
             continue
-        taken = jnp.minimum(rank[2 * d : 2 * d + 1, rows - 1 : rows], float(q.front))
-        mirrored = q.each - 1.0 - second
-        in_front = (first >= 0) & (first < q.front)
-        in_rest = (second >= 0) & (mirrored >= taken)
-        place.append(jnp.where(in_front, first, jnp.where(in_rest, mirrored, -1.0)))
-        late.append(((first >= q.front) | ((second >= 0) & (mirrored < taken))))
-    line = lax.broadcasted_iota(jnp.int32, (16, rows), 0)
-    either = jnp.where(late[0] | late[1], 1, 0)
-    after = running_count((line == 0) & (either == 1))[0:1]
-    spare = jnp.where(either == 1, after - 1.0, -1.0)
-    excess = jnp.maximum(after[:, rows - 1 : rows] - q.spare, rank[2:3, rows - 1 : rows] - q.near_front)
+        ahead = rank[2 * d : 2 * d + 1, rows - 1 : rows]
+        behind = rank[2 * d + 1 : 2 * d + 2, rows - 1 : rows]
+        room = q.each - jnp.minimum(ahead, float(q.front))
+        late_first, late_second = first >= q.front, second >= room
+        place.append(
+            jnp.where(
+                late_first | late_second, -1.0, jnp.where(first >= 0, first, jnp.where(second >= 0, q.each - 1.0 - second, -1.0))
+            )
+        )
+        late.append(late_first | late_second)
+        over = jnp.maximum(ahead - q.front, 0.0)
+        spare = jnp.where(
+            late_first, base + first - q.front, jnp.where(late_second, base + over + second - room, spare)
+        )
+        base = base + over + jnp.maximum(behind - room, 0.0)
+    excess = jnp.maximum(base - q.spare, rank[2:3, rows - 1 : rows] - q.near_front)
     return live, mid, owner, place, spare, late, excess
 
 
@@ -375,30 +381,32 @@
     return (lax.broadcasted_iota(jnp.int32, (COLS // 2, 1), 0) + base).astype(F32)
 
 
-def stack_into(out_ref, given, part):
-    labels = []
-    for ref in given:
-        count = ref.shape[0] - LINES
-        labels.append(tag_of(ref[count : count + LINES, 0:count]))
+def stack_into(out_ref, label, rows_ref, part):
     share = COLS // 2
     for f in range(FINE):
-        line = segment_line(f, part)
-        out_ref[f * share : (f + 1) * share, :] = sum(
-            jnp.dot(one_hot(label == line), ref[0 : label.shape[1], :], preferred_element_type=F32)
-            for label, ref in zip(labels, given)
+        chosen = one_hot(label == segment_line(f, part))
+        out_ref[f * share : (f + 1) * share, :] = jnp.dot(
+            chosen, rows_ref[...], preferred_element_type=F32
         ).astype(out_ref.dtype)
 
 
 def stack_sent_kernel(q, *refs):
-    *given, sent_ref, tags_ref = refs
-    tags = [tag_of(ref[q.first : q.first + LINES, q.first : q.first + q.second]) for ref in given[:2]]
-    tags_ref[...] = jnp.broadcast_to(jnp.concatenate(tags, axis=1), tags_ref.shape)
-    stack_into(sent_ref, given, 1 - lax.axis_index("off"))
-
-
-def stack_kept_kernel(*refs):
-    *given, kept_ref = refs
-    stack_into(kept_ref, given, lax.axis_index("off"))
+    *given, sent_ref, all_ref, labels_ref, tags_ref = refs
+    labels, later, at = [], [], 0
+    for ref, size in zip(given, (q.first, q.first, q.cap, q.cap)):
+        labels.append(tag_of(ref[size : size + LINES, 0:size]))
+        all_ref[at : at + size, :] = ref[0:size, :]
+        at += size
+    for ref in given[:2]:
+        later.append(tag_of(ref[q.first : q.first + LINES, q.first : q.first + q.second]))
+    label = jnp.concatenate(labels, axis=1)
+    labels_ref[...] = jnp.broadcast_to(label, labels_ref.shape)
+    tags_ref[...] = jnp.broadcast_to(jnp.concatenate(later, axis=1), tags_ref.shape)
+    stack_into(sent_ref, label, all_ref, 1 - lax.axis_index("off"))
+
+
+def stack_kept_kernel(all_ref, labels_ref, kept_ref):
+    stack_into(kept_ref, labels_ref[0:1, :], all_ref, lax.axis_index("off"))
 
 
 def join_kernel(*refs):
@@ -479,10 +487,16 @@
     flag = jnp.maximum(flag, swap(flag, "bin", 2))
     back2, back3, near_back = swap(back2, "bin", 2), swap(back3, "bin", 3), swap(near_back, "bin", 1)
     given = [rows, swap(rows, "sub", 1), own, own_other]
-    flops = 2 * FINE * COLS * (q.first + q.cap) * samples
-    sent, tags = call(
+    slots = 2 * (q.first + q.cap)
+    flops = FINE * COLS * slots * samples
+    sent, every, labels, tags = call(
         functools.partial(stack_sent_kernel, q),
-        [shape(FINE * share, samples), shape(8, 2 * q.second, F32)],
+        [
+            shape(FINE * share, samples),
+            shape(slots, samples),
+            shape(8, slots, F32),
+            shape(8, 2 * q.second, F32),
+        ],
         given,
         0,
         "stack_sent",
@@ -501,7 +515,7 @@
     (kept,) = call(
         stack_kept_kernel,
         [shape(FINE * share, samples, F32)],
-        given,
+        [every, labels],
         0,
         "stack_kept",
         flops=flops,

time: 77 us -> 77 us (level)
  Pallas kernels: 15.9 us -> 15 us
  waiting for transfers between devices: 36.7 us -> 37.6 us
    pallas_call x9, Pallas kernels: 13.6 us -> 12.7 us  [call(): pl.pallas_call(run, out_shape=list(out_shape), in_specs=[smem()] * scalar...]
    ppermute x18, waiting for transfers between devices: 36.7 us -> 37.6 us  [swap(): lax.ppermute(x, axis, [(i, i ^ mask) for i in range(lax.axis_size(axis))])]
  transfers between devices with their start and end apart: 18 -> 18, of which waited for: 11 -> 11; matrix products, arithmetic and copies ran while one was open for 1% -> 1% of each run, Pallas kernels for 13% -> 12%
where the time goes in v4:
time: 77 us; the launch traced here: 76.8 us
  waiting for transfers between devices  37.6 us (49%)
  starting transfers between devices  21.2 us (28%)
  Pallas kernels  15 us (19%)
  between operations  1.54 us (2%)
  local copies, waits for them, and re-layouts  1.34 us (2%)
    ppermute x18, waiting for transfers between devices, swap(): lax.ppermute(x, axis, [(i, i ^ mask) for i in range(lax.axis_size(axis))])  37.6 us
    ppermute x18, starting transfers between devices, swap(): lax.ppermute(x, axis, [(i, i ^ mask) for i in range(lax.axis_size(axis))])  21.2 us
    pallas_call x9, Pallas kernels, call(): pl.pallas_call(run, out_shape=list(out_shape), in_specs=[smem()] * scalar...  12.7 us
    pallas_call x1, Pallas kernels, short_path(): pl.pallas_call(functools.partial(pack_spare_kernel, q), out_shape=[shape(...  2.34 us
  transfers between devices with their start and end apart: 18, of which 11 were waited for; matrix products, arithmetic and copies ran while one was open for 1% of the time, Pallas kernels for 12%

profile of v4, /device:TPU:0, one launch (start us, length us, event | category | flops | bytes accessed | tf_op | source)
XLA Modules:
  0.0 76.8 jit_solution(1286638333544981656)
XLA Ops:
  0.7 2.3 %pack_spare.1 = (bf16[64,2048]{1,0:T(8,128)(2,1)S(1)}, bf16[16,256]{1,0:T(8,128)(2,1)S(1)}, bf16[208,2048]{1,0:T(8,128)(2,1)S(1)}, f32[8,128]{1,0:T(8,128)S(1)}, bf16[512,2048]{1,0:T(8,128)(2,1)S(1)}) custom-call(s32[1,1]{1,0:T(1,128)S(6)} %copy.17.live_ref.refs_0_, s32[1,512]{1,0:T(1,128)} %refs_1_.1, s32[1,512]{1,0:T(1,128)} %refs_2_.1, ...), custom_call_target="tpu_custom_call" | custom-call | tf_op jit(solution)/shard_map/pack_spare/pallas_call | solution.py:436
  3.6 3.7 %collective-permute-start.8 = (bf16[64,2048]{1,0:T(8,128)(2,1)S(1)}, bf16[64,2048]{1,0:T(8,128)(2,1)S(1)}, u32[]{:S(2)}, u32[]{:S(2)}) collective-permute-start(bf16[64,2048]{1,0:T(8,128)(2,1)S(1)} %get-tuple-element.53), channel_id=1, source_target_pairs={{0,8},{4,12},{8,0},{12,4},{1,9},{5,13},{9,1},{13,5},{2,10},{6,14},... | collective-permute-start | bytes 786440 | tf_op jit(solution)/shard_map/ppermute | solution.py:192
  7.2 1.4 %pack_rest.1 = (bf16[80,2048]{1,0:T(8,128)(2,1)S(1)}, bf16[80,2048]{1,0:T(8,128)(2,1)S(1)}, bf16[144,2048]{1,0:T(8,128)(2,1)S(1)}, bf16[48,2048]{1,0:T(8,128)(2,...) custom-call(s32[1,1]{1,0:T(1,128)S(6)} %copy.17.live_ref.refs_0_, s32[1,512]{1,0:T(1,128)S(1)} %copy-done.6, ...), custom_call_target="tpu_custom_call" | custom-call | flops 939524096 | bytes 4001796 | tf_op jit(solution)/shard_map/pack_rest/pallas_call | solution.py:38
  8.6 1.6 %collective-permute-start.12 = (bf16[144,2048]{1,0:T(8,128)(2,1)S(1)}, bf16[144,2048]{1,0:T(8,128)(2,1)S(1)}, u32[]{:S(2)}, u32[]{:S(2)}) collective-permute-start(bf16[144,2048]{1,0:T(8,128)(2,1)S(1)} %get-tuple-element.58), channel_id=1, source_target_pairs={{0,4},{4,0},{8,12},{12,8},{1,5},{5,1},{9,13},{13,9},{2,6},{6,2},{1... | collective-permute-start | bytes 1769480 | tf_op jit(solution)/shard_map/ppermute | solution.py:192
  10.2 1.2 %collective-permute-done.13 = f32[8,128]{1,0:T(8,128)S(1)} collective-permute-done((f32[8,128]{1,0:T(8,128)S(1)}, f32[8,128]{1,0:T(8,128)S(1)}, u32[]{:S(2)}, u32[]{:S(2)}) %collective-permute-start.13) | collective-permute-done | bytes 4128 | tf_op jit(solution)/shard_map/ppermute | solution.py:192
  11.4 1.5 %collective-permute-start.14 = (f32[8,128]{1,0:T(8,128)S(1)}, f32[8,128]{1,0:T(8,128)S(1)}, u32[]{:S(2)}, u32[]{:S(2)}) collective-permute-start(f32[8,128]{1,0:T(8,128)S(1)} %max.12), channel_id=1, source_target_pairs={{0,2},{2,0},{1,3},{3,1},{4,6},{6,4},{5,7},{7,5},{8,10},{10,8},{9,1... | collective-permute-start | bytes 12296 | tf_op jit(solution)/shard_map/ppermute | solution.py:192
  13.2 1.8 %collective-permute-done.14 = f32[8,128]{1,0:T(8,128)S(1)} collective-permute-done((f32[8,128]{1,0:T(8,128)S(1)}, f32[8,128]{1,0:T(8,128)S(1)}, u32[]{:S(2)}, u32[]{:S(2)}) %collective-permute-start.14) | collective-permute-done | bytes 4128 | tf_op jit(solution)/shard_map/ppermute | solution.py:192
  15.0 1.5 %collective-permute-start.15 = (f32[8,128]{1,0:T(8,128)S(1)}, f32[8,128]{1,0:T(8,128)S(1)}, u32[]{:S(2)}, u32[]{:S(2)}) collective-permute-start(f32[8,128]{1,0:T(8,128)S(1)} %max.13), channel_id=1, source_target_pairs={{0,16},{16,0},{1,17},{17,1},{2,18},{18,2},{3,19},{19,3},{4,20},{20... | collective-permute-start | bytes 12296 | tf_op jit(solution)/shard_map/ppermute | solution.py:192
  16.5 2.1 %collective-permute-done.15 = f32[8,128]{1,0:T(8,128)S(1)} collective-permute-done((f32[8,128]{1,0:T(8,128)S(1)}, f32[8,128]{1,0:T(8,128)S(1)}, u32[]{:S(2)}, u32[]{:S(2)}) %collective-permute-start.15) | collective-permute-done | bytes 4128 | tf_op jit(solution)/shard_map/ppermute | solution.py:192
  19.3 7.4 %collective-permute-done.9.refs_1_ = bf16[16,256]{1,0:T(8,128)(2,1)S(1)} collective-permute-done((bf16[16,256]{1,0:T(8,128)(2,1)S(1)}, bf16[16,256]{1,0:T(8,128)(2,1)S(1)}, u32[]{:S(2)}, u32[]{:S(2)}) %collective-permute-start.9) | collective-permute-done | bytes 8224 | tf_op jit(solution)/shard_map/ppermute | solution.py:192
  26.7 3.5 %collective-permute-start.10 = (bf16[80,2048]{1,0:T(8,128)(2,1)S(1)}, bf16[80,2048]{1,0:T(8,128)(2,1)S(1)}, u32[]{:S(2)}, u32[]{:S(2)}) collective-permute-start(bf16[80,2048]{1,0:T(8,128)(2,1)S(1)} %get-tuple-element.56), channel_id=1, source_target_pairs={{0,8},{4,12},{8,0},{12,4},{1,9},{5,13},{9,1},{13,5},{2,10},{6,14},... | collective-permute-start | bytes 983048 | tf_op jit(solution)/shard_map/ppermute | solution.py:192
  30.3 5.3 %collective-permute-done.11.refs_3_ = bf16[80,2048]{1,0:T(8,128)(2,1)S(1)} collective-permute-done((bf16[80,2048]{1,0:T(8,128)(2,1)S(1)}, bf16[80,2048]{1,0:T(8,128)(2,1)S(1)}, u32[]{:S(2)}, u32[]{:S(2)}) %collective-permute-start.11) | collective-permute-done | bytes 327712 | tf_op jit(solution)/shard_map/ppermute | solution.py:192
  35.7 13.6 %collective-permute-done.10.refs_2_ = bf16[80,2048]{1,0:T(8,128)(2,1)S(1)} collective-permute-done((bf16[80,2048]{1,0:T(8,128)(2,1)S(1)}, bf16[80,2048]{1,0:T(8,128)(2,1)S(1)}, u32[]{:S(2)}, u32[]{:S(2)}) %collective-permute-start.10) | collective-permute-done | bytes 327712 | tf_op jit(solution)/shard_map/ppermute | solution.py:192
  50.6 2.3 %collective-permute-start.20 = (bf16[48,2048]{1,0:T(8,128)(2,1)S(1)}, bf16[48,2048]{1,0:T(8,128)(2,1)S(1)}, u32[]{:S(2)}, u32[]{:S(2)}) collective-permute-start(bf16[48,2048]{1,0:T(8,128)(2,1)S(1)} %get-tuple-element.63), channel_id=1, source_target_pairs={{0,8},{4,12},{8,0},{12,4},{1,9},{5,13},{9,1},{13,5},{2,10},{6,14},... | collective-permute-start | bytes 589832 | tf_op jit(solution)/shard_map/ppermute | solution.py:192
  53.1 2.3 %collective-permute-start.21 = (bf16[48,2048]{1,0:T(8,128)(2,1)S(1)}, bf16[48,2048]{1,0:T(8,128)(2,1)S(1)}, u32[]{:S(2)}, u32[]{:S(2)}) collective-permute-start(bf16[48,2048]{1,0:T(8,128)(2,1)S(1)} %get-tuple-element.72), channel_id=1, source_target_pairs={{0,12},{4,8},{8,4},{12,0},{1,13},{5,9},{9,5},{13,1},{2,14},{6,10},... | collective-permute-start | bytes 589832 | tf_op jit(solution)/shard_map/ppermute | solution.py:192
  55.5 3.0 %stack_sent.1 = (bf16[512,2048]{1,0:T(8,128)(2,1)S(1)}, bf16[1216,2048]{1,0:T(8,128)(2,1)S(1)}, f32[8,1216]{1,0:T(8,128)S(1)}, f32[8,320]{1,0:T(8,128)S(1)}) custom-call(bf16[432,2048]{1,0:T(8,128)(2,1)S(1)} %get-tuple-element.66.refs_0_, bf16[432,2048]{1,0:T(8,128)(2,1)S(1)} %collective-permute-done.19.refs_1_, ...), custom_call_target="tpu_custom_call" | custom-call | flops 2550136832 | bytes 12369920 | tf_op jit(solution)/shard_map/stack_sent/pallas_call | solution.py:38
  58.5 1.9 %operate.3 = (bf16[256,256]{1,0:T(8,128)(2,1)S(1)}, bf16[256,256]{1,0:T(8,128)(2,1)S(1)}) custom-call(s32[2,4,8]{2,1,0:T(4,128)S(1)} %bitcast.9, bf16[2,4,8,128,128]{4,3,2,1,0:T(8,128)(2,1)S(1)} %bitcast.4, bf16[512,2048]{1,0:T(8,128)(2,1)S(1)} %get-tuple-element.70.refs_2_), custom_call_target="tpu_custom_call" | custom-call | flops 536870912 | bytes 4456704 | tf_op jit(solution)/shard_map/operate/pallas_call | solution.py:38
  60.4 1.6 %collective-permute-start.23 = (bf16[256,256]{1,0:T(8,128)(2,1)S(1)}, bf16[256,256]{1,0:T(8,128)(2,1)S(1)}, u32[]{:S(2)}, u32[]{:S(2)}) collective-permute-start(bf16[256,256]{1,0:T(8,128)(2,1)S(1)} %get-tuple-element.71), channel_id=1, source_target_pairs={{0,2},{2,0},{1,3},{3,1},{4,6},{6,4},{5,7},{7,5},{8,10},{10,8},{9,1... | collective-permute-start | bytes 393224 | tf_op jit(solution)/shard_map/ppermute | solution.py:192
  62.5 2.9 %stack_kept.1.refs_1_ = f32[512,2048]{1,0:T(8,128)S(1)} custom-call(bf16[1216,2048]{1,0:T(8,128)(2,1)S(1)} %get-tuple-element.68.refs_0_, f32[8,1216]{1,0:T(8,128)S(1)} %get-tuple-element.69.refs_1_, bf16[16,128]{1,0:T(8,128)(2,1)S(1)} %slice.32.refs_2_), custom_call_target="tpu_custom_call" | custom-call | flops 2550136832 | bytes 9213952 | tf_op jit(solution)/shard_map/stack_kept/pallas_call | solution.py:38
  65.4 1.5 %collective-permute-done.23.refs_3_ = bf16[256,256]{1,0:T(8,128)(2,1)S(1)} collective-permute-done((bf16[256,256]{1,0:T(8,128)(2,1)S(1)}, bf16[256,256]{1,0:T(8,128)(2,1)S(1)}, u32[]{:S(2)}, u32[]{:S(2)}) %collective-permute-start.23) | collective-permute-done | bytes 131104 | tf_op jit(solution)/shard_map/ppermute | solution.py:192
  66.9 1.4 %collective-permute-done.24.refs_4_ = bf16[256,256]{1,0:T(8,128)(2,1)S(1)} collective-permute-done((bf16[256,256]{1,0:T(8,128)(2,1)S(1)}, bf16[256,256]{1,0:T(8,128)(2,1)S(1)}, u32[]{:S(2)}, u32[]{:S(2)}) %collective-permute-start.24) | collective-permute-done | bytes 131104 | tf_op jit(solution)/shard_map/ppermute | solution.py:192
  68.3 2.0 %collective-permute-done.21.refs_1_ = bf16[48,2048]{1,0:T(8,128)(2,1)S(1)} collective-permute-done((bf16[48,2048]{1,0:T(8,128)(2,1)S(1)}, bf16[48,2048]{1,0:T(8,128)(2,1)S(1)}, u32[]{:S(2)}, u32[]{:S(2)}) %collective-permute-start.21) | collective-permute-done | bytes 196640 | tf_op jit(solution)/shard_map/ppermute | solution.py:192
  72.6 1.3 %stack_second.1.refs_2_ = bf16[512,2048]{1,0:T(8,128)(2,1)S(1)} custom-call(f32[8,320]{1,0:T(8,128)S(1)} %get-tuple-element.67.refs_0_, f32[512,2048]{1,0:T(8,128)S(1)} %stack_kept.1.refs_1_, bf16[160,2048]{1,0:T(8,128)(2,1)S(1)} %join.1.refs_2_, bf16[160,2048]{1,0:T(8,128)(2,1)S(1)} %collective-permute-done.25.refs_3_), custom_call_target="tpu_custom_call" | custom-call | flops 671088640 | bytes 7612416 | tf_op jit(solution)/shard_map/stack_second/pallas_call | solution.py:38
  73.9 1.9 %finish.1 = f32[256,512]{1,0:T(8,128)S(1)} custom-call(s32[2,4,8]{2,1,0:T(4,128)S(1)} %bitcast.10, bf16[2,4,8,128,128]{4,3,2,1,0:T(8,128)(2,1)S(1)} %bitcast.5, bf16[512,2048]{1,0:T(8,128)(2,1)S(1)} %stack_second.1.refs_2_, bf16[256,256]{1,0:T(8,128)(2,1)S(1)} %collective-permute-done.23.refs_3_, bf16[256,256]{1,0:T(8,128)(2,1)S(1)} %collective-permute-done.24.refs_4_), custom_call_target="tpu_custom_call" | custom-call | flops 536870912 | bytes 4980992 | tf_op jit(solution)/shard_map/finish/pallas_call | solution.py:38
  (49 shorter events, 6.3 us)
Async XLA Ops:
  0.0 7.2 %copy-start.7 = (s32[1,512]{1,0:T(1,128)S(1)}, s32[1,512]{1,0:T(1,128)}, u32[]{:S(2)}) copy-start(s32[1,512]{1,0:T(1,128)} %refs_2_.1) | copy-start | bytes 6148
  0.0 7.2 %copy-start.6 = (s32[1,512]{1,0:T(1,128)S(1)}, s32[1,512]{1,0:T(1,128)}, u32[]{:S(2)}) copy-start(s32[1,512]{1,0:T(1,128)} %refs_1_.1) | copy-start | bytes 6148
  3.0 32.7 %collective-permute-start.17 = (bf16[208,2048]{1,0:T(8,128)(2,1)S(1)}, bf16[208,2048]{1,0:T(8,128)(2,1)S(1)}, u32[]{:S(2)}, u32[]{:S(2)}) collective-permute-start(bf16[208,2048]{1,0:T(8,128)(2,1)S(1)} %get-tuple-element.64.refs_2_), channel_id=1, source_target_pairs={{0,1},{1,0},{2,3},{3,2},{4,5},{5,4},{6,7},{7,6},{8,9},{9,8},{10,11... | collective-permute-start | bytes 2555912 | tf_op jit(solution)/shard_map/ppermute | solution.py:192
  3.6 26.6 %collective-permute-start.8 = (bf16[64,2048]{1,0:T(8,128)(2,1)S(1)}, bf16[64,2048]{1,0:T(8,128)(2,1)S(1)}, u32[]{:S(2)}, u32[]{:S(2)}) collective-permute-start(bf16[64,2048]{1,0:T(8,128)(2,1)S(1)} %get-tuple-element.53), channel_id=1, source_target_pairs={{0,8},{4,12},{8,0},{12,4},{1,9},{5,13},{9,1},{13,5},{2,10},{6,14},... | collective-permute-start | bytes 786440 | tf_op jit(solution)/shard_map/ppermute | solution.py:192
  8.6 41.1 %collective-permute-start.12 = (bf16[144,2048]{1,0:T(8,128)(2,1)S(1)}, bf16[144,2048]{1,0:T(8,128)(2,1)S(1)}, u32[]{:S(2)}, u32[]{:S(2)}) collective-permute-start(bf16[144,2048]{1,0:T(8,128)(2,1)S(1)} %get-tuple-element.58), channel_id=1, source_target_pairs={{0,4},{4,0},{8,12},{12,8},{1,5},{5,1},{9,13},{13,9},{2,6},{6,2},{1... | collective-permute-start | bytes 1769480 | tf_op jit(solution)/shard_map/ppermute | solution.py:192
  10.2 1.2 %collective-permute-start.13 = (f32[8,128]{1,0:T(8,128)S(1)}, f32[8,128]{1,0:T(8,128)S(1)}, u32[]{:S(2)}, u32[]{:S(2)}) collective-permute-start(f32[8,128]{1,0:T(8,128)S(1)} %get-tuple-element.59), channel_id=1, source_target_pairs={{0,1},{1,0},{2,3},{3,2},{4,5},{5,4},{6,7},{7,6},{8,9},{9,8},{10,11... | collective-permute-start | bytes 12296 | tf_op jit(solution)/shard_map/ppermute | solution.py:192
  11.4 3.6 %collective-permute-start.14 = (f32[8,128]{1,0:T(8,128)S(1)}, f32[8,128]{1,0:T(8,128)S(1)}, u32[]{:S(2)}, u32[]{:S(2)}) collective-permute-start(f32[8,128]{1,0:T(8,128)S(1)} %max.12), channel_id=1, source_target_pairs={{0,2},{2,0},{1,3},{3,1},{4,6},{6,4},{5,7},{7,5},{8,10},{10,8},{9,1... | collective-permute-start | bytes 12296 | tf_op jit(solution)/shard_map/ppermute | solution.py:192
  12.9 13.8 %collective-permute-start.9 = (bf16[16,256]{1,0:T(8,128)(2,1)S(1)}, bf16[16,256]{1,0:T(8,128)(2,1)S(1)}, u32[]{:S(2)}, u32[]{:S(2)}) collective-permute-start(bf16[16,256]{1,0:T(8,128)(2,1)S(1)} %get-tuple-element.54), channel_id=1, source_target_pairs={{0,8},{4,12},{8,0},{12,4},{1,9},{5,13},{9,1},{13,5},{2,10},{6,14},... | collective-permute-start | bytes 24584 | tf_op jit(solution)/shard_map/ppermute | solution.py:192
  15.0 3.6 %collective-permute-start.15 = (f32[8,128]{1,0:T(8,128)S(1)}, f32[8,128]{1,0:T(8,128)S(1)}, u32[]{:S(2)}, u32[]{:S(2)}) collective-permute-start(f32[8,128]{1,0:T(8,128)S(1)} %max.13), channel_id=1, source_target_pairs={{0,16},{16,0},{1,17},{17,1},{2,18},{18,2},{3,19},{19,3},{4,20},{20... | collective-permute-start | bytes 12296 | tf_op jit(solution)/shard_map/ppermute | solution.py:192
  18.6 17.1 %collective-permute-start.11 = (bf16[80,2048]{1,0:T(8,128)(2,1)S(1)}, bf16[80,2048]{1,0:T(8,128)(2,1)S(1)}, u32[]{:S(2)}, u32[]{:S(2)}) collective-permute-start(bf16[80,2048]{1,0:T(8,128)(2,1)S(1)} %get-tuple-element.57), channel_id=1, source_target_pairs={{0,12},{4,8},{8,4},{12,0},{1,13},{5,9},{9,5},{13,1},{2,14},{6,10},... | collective-permute-start | bytes 983048 | tf_op jit(solution)/shard_map/ppermute | solution.py:192
  26.7 22.6 %collective-permute-start.10 = (bf16[80,2048]{1,0:T(8,128)(2,1)S(1)}, bf16[80,2048]{1,0:T(8,128)(2,1)S(1)}, u32[]{:S(2)}, u32[]{:S(2)}) collective-permute-start(bf16[80,2048]{1,0:T(8,128)(2,1)S(1)} %get-tuple-element.56), channel_id=1, source_target_pairs={{0,8},{4,12},{8,0},{12,4},{1,9},{5,13},{9,1},{13,5},{2,10},{6,14},... | collective-permute-start | bytes 983048 | tf_op jit(solution)/shard_map/ppermute | solution.py:192
  30.3 19.5 %collective-permute-start.16 = (bf16[80,2048]{1,0:T(8,128)(2,1)S(1)}, bf16[80,2048]{1,0:T(8,128)(2,1)S(1)}, u32[]{:S(2)}, u32[]{:S(2)}) collective-permute-start(bf16[80,2048]{1,0:T(8,128)(2,1)S(1)} %relay.1), channel_id=1, source_target_pairs={{0,4},{4,0},{8,12},{12,8},{1,5},{5,1},{9,13},{13,9},{2,6},{6,2},{1... | collective-permute-start | bytes 983048 | tf_op jit(solution)/shard_map/ppermute | solution.py:192
  49.9 5.6 %collective-permute-start.19 = (bf16[432,2048]{1,0:T(8,128)(2,1)S(1)}, bf16[432,2048]{1,0:T(8,128)(2,1)S(1)}, u32[]{:S(2)}, u32[]{:S(2)}) collective-permute-start(bf16[432,2048]{1,0:T(8,128)(2,1)S(1)} %get-tuple-element.66.refs_0_), channel_id=1, source_target_pairs={{0,1},{1,0},{2,3},{3,2},{4,5},{5,4},{6,7},{7,6},{8,9},{9,8},{10,11... | collective-permute-start | bytes 5308424 | tf_op jit(solution)/shard_map/ppermute | solution.py:192
  49.9 5.5 %collective-permute-start.18 = (f32[8,128]{1,0:T(8,128)S(1)}, f32[8,128]{1,0:T(8,128)S(1)}, u32[]{:S(2)}, u32[]{:S(2)}) collective-permute-start(f32[8,128]{1,0:T(8,128)S(1)} %get-tuple-element.65), channel_id=1, source_target_pairs={{0,8},{4,12},{8,0},{12,4},{1,9},{5,13},{9,1},{13,5},{2,10},{6,14},... | collective-permute-start | bytes 12296 | tf_op jit(solution)/shard_map/ppermute | solution.py:192
  50.6 17.7 %collective-permute-start.20 = (bf16[48,2048]{1,0:T(8,128)(2,1)S(1)}, bf16[48,2048]{1,0:T(8,128)(2,1)S(1)}, u32[]{:S(2)}, u32[]{:S(2)}) collective-permute-start(bf16[48,2048]{1,0:T(8,128)(2,1)S(1)} %get-tuple-element.63), channel_id=1, source_target_pairs={{0,8},{4,12},{8,0},{12,4},{1,9},{5,13},{9,1},{13,5},{2,10},{6,14},... | collective-permute-start | bytes 589832 | tf_op jit(solution)/shard_map/ppermute | solution.py:192
  52.9 17.4 %collective-permute-start.22 = (bf16[64,2048]{1,0:T(8,128)(2,1)S(1)}, bf16[64,2048]{1,0:T(8,128)(2,1)S(1)}, u32[]{:S(2)}, u32[]{:S(2)}) collective-permute-start(bf16[64,2048]{1,0:T(8,128)(2,1)S(1)} %get-tuple-element.73), channel_id=1, source_target_pairs={{0,4},{4,0},{8,12},{12,8},{1,5},{5,1},{9,13},{13,9},{2,6},{6,2},{1... | collective-permute-start | bytes 786440 | tf_op jit(solution)/shard_map/ppermute | solution.py:192
  53.1 17.2 %collective-permute-start.21 = (bf16[48,2048]{1,0:T(8,128)(2,1)S(1)}, bf16[48,2048]{1,0:T(8,128)(2,1)S(1)}, u32[]{:S(2)}, u32[]{:S(2)}) collective-permute-start(bf16[48,2048]{1,0:T(8,128)(2,1)S(1)} %get-tuple-element.72), channel_id=1, source_target_pairs={{0,12},{4,8},{8,4},{12,0},{1,13},{5,9},{9,5},{13,1},{2,14},{6,10},... | collective-permute-start | bytes 589832 | tf_op jit(solution)/shard_map/ppermute | solution.py:192
  55.4 3.0 %copy-start = (bf16[1,2,1,4,8,128,128]{6,5,4,3,2,1,0:T(8,128)(2,1)S(1)}, bf16[1,2,1,4,8,128,128]{6,5,4,3,2,1,0:T(8,128)(2,1)}, u32[]{:S(2)}) copy-start(bf16[1,2,1,4,8,128,128]{6,5,4,3,2,1,0:T(8,128)(2,1)} %param.12) | copy-start | bytes 6291460
  55.4 3.0 %copy-start.5 = (s32[1,2,1,4,8]{4,3,2,1,0:T(4,128)S(1)}, s32[1,2,1,4,8]{4,3,2,1,0:T(4,128)}, u32[]{:S(2)}) copy-start(s32[1,2,1,4,8]{4,3,2,1,0:T(4,128)} %param.13) | copy-start | bytes 772
  60.4 6.5 %collective-permute-start.23 = (bf16[256,256]{1,0:T(8,128)(2,1)S(1)}, bf16[256,256]{1,0:T(8,128)(2,1)S(1)}, u32[]{:S(2)}, u32[]{:S(2)}) collective-permute-start(bf16[256,256]{1,0:T(8,128)(2,1)S(1)} %get-tuple-element.71), channel_id=1, source_target_pairs={{0,2},{2,0},{1,3},{3,1},{4,6},{6,4},{5,7},{7,5},{8,10},{10,8},{9,1... | collective-permute-start | bytes 393224 | tf_op jit(solution)/shard_map/ppermute | solution.py:192
  62.0 6.3 %collective-permute-start.24 = (bf16[256,256]{1,0:T(8,128)(2,1)S(1)}, bf16[256,256]{1,0:T(8,128)(2,1)S(1)}, u32[]{:S(2)}, u32[]{:S(2)}) collective-permute-start(bf16[256,256]{1,0:T(8,128)(2,1)S(1)} %get-tuple-element.74), channel_id=1, source_target_pairs={{0,2},{2,0},{1,3},{3,1},{4,6},{6,4},{5,7},{7,5},{8,10},{10,8},{9,1... | collective-permute-start | bytes 393224 | tf_op jit(solution)/shard_map/ppermute | solution.py:192
  70.4 2.2 %collective-permute-start.25 = (bf16[160,2048]{1,0:T(8,128)(2,1)S(1)}, bf16[160,2048]{1,0:T(8,128)(2,1)S(1)}, u32[]{:S(2)}, u32[]{:S(2)}) collective-permute-start(bf16[160,2048]{1,0:T(8,128)(2,1)S(1)} %join.1.refs_2_), channel_id=1, source_target_pairs={{0,1},{1,0},{2,3},{3,2},{4,5},{5,4},{6,7},{7,6},{8,9},{9,8},{10,11... | collective-permute-start | bytes 1966088 | tf_op jit(solution)/shard_map/ppermute | solution.py:192
  73.9 2.0 %copy-start.3 = (bf16[1,512,2048]{2,1,0:T(8,128)(2,1)S(1)}, bf16[1,512,2048]{2,1,0:T(8,128)(2,1)}, u32[]{:S(2)}) copy-start(bf16[1,512,2048]{2,1,0:T(8,128)(2,1)} %param.8) | copy-start | bytes 6291460
  76.0 0.8 %copy-start.4 = (f32[256,512]{1,0:T(8,128)}, f32[256,512]{1,0:T(8,128)S(1)}, u32[]{:S(2)}) copy-start(f32[256,512]{1,0:T(8,128)S(1)} %get-tuple-element.120) | copy-start | bytes 1572868

commit v5 on v4

--- a/solution.py
+++ b/solution.py
@@ -305,9 +305,14 @@
     chosen = jnp.concatenate([extra[0] + extra[1], own], axis=0)
     lines_ref[...] = jnp.zeros(lines_ref.shape, BF)
     lines_ref[:, 0 : q.cap] = crossing.astype(BF)
-    for copy in copies[2:]:
-        copy.wait()
-    rows = jnp.dot(chosen, held_ref[...], preferred_element_type=F32).astype(BF)
+    rows = 0.0
+    size = held_ref.shape[0] // 2
+    for part in range(2):
+        for copy in copies[2 + part * count // 2 : 2 + (part + 1) * count // 2]:
+            copy.wait()
+        span = slice(part * size, (part + 1) * size)
+        rows = rows + jnp.dot(chosen[:, span], held_ref[span, :], preferred_element_type=F32)
+    rows = rows.astype(BF)
     spare_ref[...] = rows[: q.spare]
     lay(own_ref, rows[q.spare :], across(digits, own))
     flag_ref[...] = jnp.broadcast_to(jnp.where(excess > 0.0, 1.0, 0.0), flag_ref.shape)

time: 77 us -> 77 us (level)
  no operation moved by 1% of the time
where the time goes in v5:
time: 77 us; the launch traced here: 76.8 us
  waiting for transfers between devices  37.6 us (49%)
  starting transfers between devices  21.1 us (27%)
  Pallas kernels  15 us (19%)
  between operations  1.54 us (2%)
  local copies, waits for them, and re-layouts  1.34 us (2%)
    ppermute x18, waiting for transfers between devices, swap(): lax.ppermute(x, axis, [(i, i ^ mask) for i in range(lax.axis_size(axis))])  37.6 us
    ppermute x18, starting transfers between devices, swap(): lax.ppermute(x, axis, [(i, i ^ mask) for i in range(lax.axis_size(axis))])  21.1 us
    pallas_call x9, Pallas kernels, call(): pl.pallas_call(run, out_shape=list(out_shape), in_specs=[smem()] * scalar...  12.7 us
    pallas_call x1, Pallas kernels, short_path(): pl.pallas_call(functools.partial(pack_spare_kernel, q), out_shape=[shape(...  2.34 us
  transfers between devices with their start and end apart: 18, of which 11 were waited for; matrix products, arithmetic and copies ran while one was open for 1% of the time, Pallas kernels for 12%

profile of v5, /device:TPU:0, one launch (start us, length us, event | category | flops | bytes accessed | tf_op | source)
XLA Modules:
  0.0 76.8 jit_solution(5481120494284351569)
XLA Ops:
  0.7 2.3 %pack_spare.1 = (bf16[64,2048]{1,0:T(8,128)(2,1)S(1)}, bf16[16,256]{1,0:T(8,128)(2,1)S(1)}, bf16[208,2048]{1,0:T(8,128)(2,1)S(1)}, f32[8,128]{1,0:T(8,128)S(1)}, bf16[512,2048]{1,0:T(8,128)(2,1)S(1)}) custom-call(s32[1,1]{1,0:T(1,128)S(6)} %copy.17.live_ref.refs_0_, s32[1,512]{1,0:T(1,128)} %refs_1_.1, s32[1,512]{1,0:T(1,128)} %refs_2_.1, ...), custom_call_target="tpu_custom_call" | custom-call | tf_op jit(solution)/shard_map/pack_spare/pallas_call | solution.py:441
  3.6 3.7 %collective-permute-start.8 = (bf16[64,2048]{1,0:T(8,128)(2,1)S(1)}, bf16[64,2048]{1,0:T(8,128)(2,1)S(1)}, u32[]{:S(2)}, u32[]{:S(2)}) collective-permute-start(bf16[64,2048]{1,0:T(8,128)(2,1)S(1)} %get-tuple-element.53), channel_id=1, source_target_pairs={{0,8},{4,12},{8,0},{12,4},{1,9},{5,13},{9,1},{13,5},{2,10},{6,14},... | collective-permute-start | bytes 786440 | tf_op jit(solution)/shard_map/ppermute | solution.py:192
  7.2 1.4 %pack_rest.1 = (bf16[80,2048]{1,0:T(8,128)(2,1)S(1)}, bf16[80,2048]{1,0:T(8,128)(2,1)S(1)}, bf16[144,2048]{1,0:T(8,128)(2,1)S(1)}, bf16[48,2048]{1,0:T(8,128)(2,...) custom-call(s32[1,1]{1,0:T(1,128)S(6)} %copy.17.live_ref.refs_0_, s32[1,512]{1,0:T(1,128)S(1)} %copy-done.6, ...), custom_call_target="tpu_custom_call" | custom-call | flops 939524096 | bytes 4001796 | tf_op jit(solution)/shard_map/pack_rest/pallas_call | solution.py:38
  8.6 1.6 %collective-permute-start.12 = (bf16[144,2048]{1,0:T(8,128)(2,1)S(1)}, bf16[144,2048]{1,0:T(8,128)(2,1)S(1)}, u32[]{:S(2)}, u32[]{:S(2)}) collective-permute-start(bf16[144,2048]{1,0:T(8,128)(2,1)S(1)} %get-tuple-element.58), channel_id=1, source_target_pairs={{0,4},{4,0},{8,12},{12,8},{1,5},{5,1},{9,13},{13,9},{2,6},{6,2},{1... | collective-permute-start | bytes 1769480 | tf_op jit(solution)/shard_map/ppermute | solution.py:192
  10.2 1.2 %collective-permute-done.13 = f32[8,128]{1,0:T(8,128)S(1)} collective-permute-done((f32[8,128]{1,0:T(8,128)S(1)}, f32[8,128]{1,0:T(8,128)S(1)}, u32[]{:S(2)}, u32[]{:S(2)}) %collective-permute-start.13) | collective-permute-done | bytes 4128 | tf_op jit(solution)/shard_map/ppermute | solution.py:192
  11.4 1.5 %collective-permute-start.14 = (f32[8,128]{1,0:T(8,128)S(1)}, f32[8,128]{1,0:T(8,128)S(1)}, u32[]{:S(2)}, u32[]{:S(2)}) collective-permute-start(f32[8,128]{1,0:T(8,128)S(1)} %max.12), channel_id=1, source_target_pairs={{0,2},{2,0},{1,3},{3,1},{4,6},{6,4},{5,7},{7,5},{8,10},{10,8},{9,1... | collective-permute-start | bytes 12296 | tf_op jit(solution)/shard_map/ppermute | solution.py:192
  13.2 1.8 %collective-permute-done.14 = f32[8,128]{1,0:T(8,128)S(1)} collective-permute-done((f32[8,128]{1,0:T(8,128)S(1)}, f32[8,128]{1,0:T(8,128)S(1)}, u32[]{:S(2)}, u32[]{:S(2)}) %collective-permute-start.14) | collective-permute-done | bytes 4128 | tf_op jit(solution)/shard_map/ppermute | solution.py:192
  15.0 1.5 %collective-permute-start.15 = (f32[8,128]{1,0:T(8,128)S(1)}, f32[8,128]{1,0:T(8,128)S(1)}, u32[]{:S(2)}, u32[]{:S(2)}) collective-permute-start(f32[8,128]{1,0:T(8,128)S(1)} %max.13), channel_id=1, source_target_pairs={{0,16},{16,0},{1,17},{17,1},{2,18},{18,2},{3,19},{19,3},{4,20},{20... | collective-permute-start | bytes 12296 | tf_op jit(solution)/shard_map/ppermute | solution.py:192
  16.5 2.1 %collective-permute-done.15 = f32[8,128]{1,0:T(8,128)S(1)} collective-permute-done((f32[8,128]{1,0:T(8,128)S(1)}, f32[8,128]{1,0:T(8,128)S(1)}, u32[]{:S(2)}, u32[]{:S(2)}) %collective-permute-start.15) | collective-permute-done | bytes 4128 | tf_op jit(solution)/shard_map/ppermute | solution.py:192
  19.3 7.4 %collective-permute-done.9.refs_1_ = bf16[16,256]{1,0:T(8,128)(2,1)S(1)} collective-permute-done((bf16[16,256]{1,0:T(8,128)(2,1)S(1)}, bf16[16,256]{1,0:T(8,128)(2,1)S(1)}, u32[]{:S(2)}, u32[]{:S(2)}) %collective-permute-start.9) | collective-permute-done | bytes 8224 | tf_op jit(solution)/shard_map/ppermute | solution.py:192
  26.7 3.5 %collective-permute-start.10 = (bf16[80,2048]{1,0:T(8,128)(2,1)S(1)}, bf16[80,2048]{1,0:T(8,128)(2,1)S(1)}, u32[]{:S(2)}, u32[]{:S(2)}) collective-permute-start(bf16[80,2048]{1,0:T(8,128)(2,1)S(1)} %get-tuple-element.56), channel_id=1, source_target_pairs={{0,8},{4,12},{8,0},{12,4},{1,9},{5,13},{9,1},{13,5},{2,10},{6,14},... | collective-permute-start | bytes 983048 | tf_op jit(solution)/shard_map/ppermute | solution.py:192
  30.3 5.3 %collective-permute-done.11.refs_3_ = bf16[80,2048]{1,0:T(8,128)(2,1)S(1)} collective-permute-done((bf16[80,2048]{1,0:T(8,128)(2,1)S(1)}, bf16[80,2048]{1,0:T(8,128)(2,1)S(1)}, u32[]{:S(2)}, u32[]{:S(2)}) %collective-permute-start.11) | collective-permute-done | bytes 327712 | tf_op jit(solution)/shard_map/ppermute | solution.py:192
  35.7 13.6 %collective-permute-done.10.refs_2_ = bf16[80,2048]{1,0:T(8,128)(2,1)S(1)} collective-permute-done((bf16[80,2048]{1,0:T(8,128)(2,1)S(1)}, bf16[80,2048]{1,0:T(8,128)(2,1)S(1)}, u32[]{:S(2)}, u32[]{:S(2)}) %collective-permute-start.10) | collective-permute-done | bytes 327712 | tf_op jit(solution)/shard_map/ppermute | solution.py:192
  50.6 2.3 %collective-permute-start.20 = (bf16[48,2048]{1,0:T(8,128)(2,1)S(1)}, bf16[48,2048]{1,0:T(8,128)(2,1)S(1)}, u32[]{:S(2)}, u32[]{:S(2)}) collective-permute-start(bf16[48,2048]{1,0:T(8,128)(2,1)S(1)} %get-tuple-element.63), channel_id=1, source_target_pairs={{0,8},{4,12},{8,0},{12,4},{1,9},{5,13},{9,1},{13,5},{2,10},{6,14},... | collective-permute-start | bytes 589832 | tf_op jit(solution)/shard_map/ppermute | solution.py:192
  53.1 2.3 %collective-permute-start.21 = (bf16[48,2048]{1,0:T(8,128)(2,1)S(1)}, bf16[48,2048]{1,0:T(8,128)(2,1)S(1)}, u32[]{:S(2)}, u32[]{:S(2)}) collective-permute-start(bf16[48,2048]{1,0:T(8,128)(2,1)S(1)} %get-tuple-element.72), channel_id=1, source_target_pairs={{0,12},{4,8},{8,4},{12,0},{1,13},{5,9},{9,5},{13,1},{2,14},{6,10},... | collective-permute-start | bytes 589832 | tf_op jit(solution)/shard_map/ppermute | solution.py:192
  55.4 3.0 %stack_sent.1 = (bf16[512,2048]{1,0:T(8,128)(2,1)S(1)}, bf16[1216,2048]{1,0:T(8,128)(2,1)S(1)}, f32[8,1216]{1,0:T(8,128)S(1)}, f32[8,320]{1,0:T(8,128)S(1)}) custom-call(bf16[432,2048]{1,0:T(8,128)(2,1)S(1)} %get-tuple-element.66.refs_0_, bf16[432,2048]{1,0:T(8,128)(2,1)S(1)} %collective-permute-done.19.refs_1_, ...), custom_call_target="tpu_custom_call" | custom-call | flops 2550136832 | bytes 12369920 | tf_op jit(solution)/shard_map/stack_sent/pallas_call | solution.py:38
  58.5 1.9 %operate.3 = (bf16[256,256]{1,0:T(8,128)(2,1)S(1)}, bf16[256,256]{1,0:T(8,128)(2,1)S(1)}) custom-call(s32[2,4,8]{2,1,0:T(4,128)S(1)} %bitcast.9, bf16[2,4,8,128,128]{4,3,2,1,0:T(8,128)(2,1)S(1)} %bitcast.4, bf16[512,2048]{1,0:T(8,128)(2,1)S(1)} %get-tuple-element.70.refs_2_), custom_call_target="tpu_custom_call" | custom-call | flops 536870912 | bytes 4456704 | tf_op jit(solution)/shard_map/operate/pallas_call | solution.py:38
  60.4 1.6 %collective-permute-start.23 = (bf16[256,256]{1,0:T(8,128)(2,1)S(1)}, bf16[256,256]{1,0:T(8,128)(2,1)S(1)}, u32[]{:S(2)}, u32[]{:S(2)}) collective-permute-start(bf16[256,256]{1,0:T(8,128)(2,1)S(1)} %get-tuple-element.71), channel_id=1, source_target_pairs={{0,2},{2,0},{1,3},{3,1},{4,6},{6,4},{5,7},{7,5},{8,10},{10,8},{9,1... | collective-permute-start | bytes 393224 | tf_op jit(solution)/shard_map/ppermute | solution.py:192
  62.5 2.9 %stack_kept.1.refs_1_ = f32[512,2048]{1,0:T(8,128)S(1)} custom-call(bf16[1216,2048]{1,0:T(8,128)(2,1)S(1)} %get-tuple-element.68.refs_0_, f32[8,1216]{1,0:T(8,128)S(1)} %get-tuple-element.69.refs_1_, bf16[16,128]{1,0:T(8,128)(2,1)S(1)} %slice.32.refs_2_), custom_call_target="tpu_custom_call" | custom-call | flops 2550136832 | bytes 9213952 | tf_op jit(solution)/shard_map/stack_kept/pallas_call | solution.py:38
  65.5 1.4 %collective-permute-done.23.refs_3_ = bf16[256,256]{1,0:T(8,128)(2,1)S(1)} collective-permute-done((bf16[256,256]{1,0:T(8,128)(2,1)S(1)}, bf16[256,256]{1,0:T(8,128)(2,1)S(1)}, u32[]{:S(2)}, u32[]{:S(2)}) %collective-permute-start.23) | collective-permute-done | bytes 131104 | tf_op jit(solution)/shard_map/ppermute | solution.py:192
  66.9 1.4 %collective-permute-done.24.refs_4_ = bf16[256,256]{1,0:T(8,128)(2,1)S(1)} collective-permute-done((bf16[256,256]{1,0:T(8,128)(2,1)S(1)}, bf16[256,256]{1,0:T(8,128)(2,1)S(1)}, u32[]{:S(2)}, u32[]{:S(2)}) %collective-permute-start.24) | collective-permute-done | bytes 131104 | tf_op jit(solution)/shard_map/ppermute | solution.py:192
  68.3 2.0 %collective-permute-done.21.refs_1_ = bf16[48,2048]{1,0:T(8,128)(2,1)S(1)} collective-permute-done((bf16[48,2048]{1,0:T(8,128)(2,1)S(1)}, bf16[48,2048]{1,0:T(8,128)(2,1)S(1)}, u32[]{:S(2)}, u32[]{:S(2)}) %collective-permute-start.21) | collective-permute-done | bytes 196640 | tf_op jit(solution)/shard_map/ppermute | solution.py:192
  72.5 1.3 %stack_second.1.refs_2_ = bf16[512,2048]{1,0:T(8,128)(2,1)S(1)} custom-call(f32[8,320]{1,0:T(8,128)S(1)} %get-tuple-element.67.refs_0_, f32[512,2048]{1,0:T(8,128)S(1)} %stack_kept.1.refs_1_, bf16[160,2048]{1,0:T(8,128)(2,1)S(1)} %join.1.refs_2_, bf16[160,2048]{1,0:T(8,128)(2,1)S(1)} %collective-permute-done.25.refs_3_), custom_call_target="tpu_custom_call" | custom-call | flops 671088640 | bytes 7612416 | tf_op jit(solution)/shard_map/stack_second/pallas_call | solution.py:38
  73.9 1.9 %finish.1 = f32[256,512]{1,0:T(8,128)S(1)} custom-call(s32[2,4,8]{2,1,0:T(4,128)S(1)} %bitcast.10, bf16[2,4,8,128,128]{4,3,2,1,0:T(8,128)(2,1)S(1)} %bitcast.5, bf16[512,2048]{1,0:T(8,128)(2,1)S(1)} %stack_second.1.refs_2_, bf16[256,256]{1,0:T(8,128)(2,1)S(1)} %collective-permute-done.23.refs_3_, bf16[256,256]{1,0:T(8,128)(2,1)S(1)} %collective-permute-done.24.refs_4_), custom_call_target="tpu_custom_call" | custom-call | flops 536870912 | bytes 4980992 | tf_op jit(solution)/shard_map/finish/pallas_call | solution.py:38
  (49 shorter events, 6.3 us)
Async XLA Ops:
  0.0 7.2 %copy-start.7 = (s32[1,512]{1,0:T(1,128)S(1)}, s32[1,512]{1,0:T(1,128)}, u32[]{:S(2)}) copy-start(s32[1,512]{1,0:T(1,128)} %refs_2_.1) | copy-start | bytes 6148
  0.0 7.2 %copy-start.6 = (s32[1,512]{1,0:T(1,128)S(1)}, s32[1,512]{1,0:T(1,128)}, u32[]{:S(2)}) copy-start(s32[1,512]{1,0:T(1,128)} %refs_1_.1) | copy-start | bytes 6148
  3.0 32.6 %collective-permute-start.17 = (bf16[208,2048]{1,0:T(8,128)(2,1)S(1)}, bf16[208,2048]{1,0:T(8,128)(2,1)S(1)}, u32[]{:S(2)}, u32[]{:S(2)}) collective-permute-start(bf16[208,2048]{1,0:T(8,128)(2,1)S(1)} %get-tuple-element.64.refs_2_), channel_id=1, source_target_pairs={{0,1},{1,0},{2,3},{3,2},{4,5},{5,4},{6,7},{7,6},{8,9},{9,8},{10,11... | collective-permute-start | bytes 2555912 | tf_op jit(solution)/shard_map/ppermute | solution.py:192
  3.6 26.6 %collective-permute-start.8 = (bf16[64,2048]{1,0:T(8,128)(2,1)S(1)}, bf16[64,2048]{1,0:T(8,128)(2,1)S(1)}, u32[]{:S(2)}, u32[]{:S(2)}) collective-permute-start(bf16[64,2048]{1,0:T(8,128)(2,1)S(1)} %get-tuple-element.53), channel_id=1, source_target_pairs={{0,8},{4,12},{8,0},{12,4},{1,9},{5,13},{9,1},{13,5},{2,10},{6,14},... | collective-permute-start | bytes 786440 | tf_op jit(solution)/shard_map/ppermute | solution.py:192
  8.6 41.1 %collective-permute-start.12 = (bf16[144,2048]{1,0:T(8,128)(2,1)S(1)}, bf16[144,2048]{1,0:T(8,128)(2,1)S(1)}, u32[]{:S(2)}, u32[]{:S(2)}) collective-permute-start(bf16[144,2048]{1,0:T(8,128)(2,1)S(1)} %get-tuple-element.58), channel_id=1, source_target_pairs={{0,4},{4,0},{8,12},{12,8},{1,5},{5,1},{9,13},{13,9},{2,6},{6,2},{1... | collective-permute-start | bytes 1769480 | tf_op jit(solution)/shard_map/ppermute | solution.py:192
  10.2 1.2 %collective-permute-start.13 = (f32[8,128]{1,0:T(8,128)S(1)}, f32[8,128]{1,0:T(8,128)S(1)}, u32[]{:S(2)}, u32[]{:S(2)}) collective-permute-start(f32[8,128]{1,0:T(8,128)S(1)} %get-tuple-element.59), channel_id=1, source_target_pairs={{0,1},{1,0},{2,3},{3,2},{4,5},{5,4},{6,7},{7,6},{8,9},{9,8},{10,11... | collective-permute-start | bytes 12296 | tf_op jit(solution)/shard_map/ppermute | solution.py:192
  11.4 3.6 %collective-permute-start.14 = (f32[8,128]{1,0:T(8,128)S(1)}, f32[8,128]{1,0:T(8,128)S(1)}, u32[]{:S(2)}, u32[]{:S(2)}) collective-permute-start(f32[8,128]{1,0:T(8,128)S(1)} %max.12), channel_id=1, source_target_pairs={{0,2},{2,0},{1,3},{3,1},{4,6},{6,4},{5,7},{7,5},{8,10},{10,8},{9,1... | collective-permute-start | bytes 12296 | tf_op jit(solution)/shard_map/ppermute | solution.py:192
  12.9 13.8 %collective-permute-start.9 = (bf16[16,256]{1,0:T(8,128)(2,1)S(1)}, bf16[16,256]{1,0:T(8,128)(2,1)S(1)}, u32[]{:S(2)}, u32[]{:S(2)}) collective-permute-start(bf16[16,256]{1,0:T(8,128)(2,1)S(1)} %get-tuple-element.54), channel_id=1, source_target_pairs={{0,8},{4,12},{8,0},{12,4},{1,9},{5,13},{9,1},{13,5},{2,10},{6,14},... | collective-permute-start | bytes 24584 | tf_op jit(solution)/shard_map/ppermute | solution.py:192
  15.0 3.6 %collective-permute-start.15 = (f32[8,128]{1,0:T(8,128)S(1)}, f32[8,128]{1,0:T(8,128)S(1)}, u32[]{:S(2)}, u32[]{:S(2)}) collective-permute-start(f32[8,128]{1,0:T(8,128)S(1)} %max.13), channel_id=1, source_target_pairs={{0,16},{16,0},{1,17},{17,1},{2,18},{18,2},{3,19},{19,3},{4,20},{20... | collective-permute-start | bytes 12296 | tf_op jit(solution)/shard_map/ppermute | solution.py:192
  18.6 17.0 %collective-permute-start.11 = (bf16[80,2048]{1,0:T(8,128)(2,1)S(1)}, bf16[80,2048]{1,0:T(8,128)(2,1)S(1)}, u32[]{:S(2)}, u32[]{:S(2)}) collective-permute-start(bf16[80,2048]{1,0:T(8,128)(2,1)S(1)} %get-tuple-element.57), channel_id=1, source_target_pairs={{0,12},{4,8},{8,4},{12,0},{1,13},{5,9},{9,5},{13,1},{2,14},{6,10},... | collective-permute-start | bytes 983048 | tf_op jit(solution)/shard_map/ppermute | solution.py:192
  26.7 22.6 %collective-permute-start.10 = (bf16[80,2048]{1,0:T(8,128)(2,1)S(1)}, bf16[80,2048]{1,0:T(8,128)(2,1)S(1)}, u32[]{:S(2)}, u32[]{:S(2)}) collective-permute-start(bf16[80,2048]{1,0:T(8,128)(2,1)S(1)} %get-tuple-element.56), channel_id=1, source_target_pairs={{0,8},{4,12},{8,0},{12,4},{1,9},{5,13},{9,1},{13,5},{2,10},{6,14},... | collective-permute-start | bytes 983048 | tf_op jit(solution)/shard_map/ppermute | solution.py:192
  30.2 19.5 %collective-permute-start.16 = (bf16[80,2048]{1,0:T(8,128)(2,1)S(1)}, bf16[80,2048]{1,0:T(8,128)(2,1)S(1)}, u32[]{:S(2)}, u32[]{:S(2)}) collective-permute-start(bf16[80,2048]{1,0:T(8,128)(2,1)S(1)} %relay.1), channel_id=1, source_target_pairs={{0,4},{4,0},{8,12},{12,8},{1,5},{5,1},{9,13},{13,9},{2,6},{6,2},{1... | collective-permute-start | bytes 983048 | tf_op jit(solution)/shard_map/ppermute | solution.py:192
  49.9 5.6 %collective-permute-start.19 = (bf16[432,2048]{1,0:T(8,128)(2,1)S(1)}, bf16[432,2048]{1,0:T(8,128)(2,1)S(1)}, u32[]{:S(2)}, u32[]{:S(2)}) collective-permute-start(bf16[432,2048]{1,0:T(8,128)(2,1)S(1)} %get-tuple-element.66.refs_0_), channel_id=1, source_target_pairs={{0,1},{1,0},{2,3},{3,2},{4,5},{5,4},{6,7},{7,6},{8,9},{9,8},{10,11... | collective-permute-start | bytes 5308424 | tf_op jit(solution)/shard_map/ppermute | solution.py:192
  49.9 5.5 %collective-permute-start.18 = (f32[8,128]{1,0:T(8,128)S(1)}, f32[8,128]{1,0:T(8,128)S(1)}, u32[]{:S(2)}, u32[]{:S(2)}) collective-permute-start(f32[8,128]{1,0:T(8,128)S(1)} %get-tuple-element.65), channel_id=1, source_target_pairs={{0,8},{4,12},{8,0},{12,4},{1,9},{5,13},{9,1},{13,5},{2,10},{6,14},... | collective-permute-start | bytes 12296 | tf_op jit(solution)/shard_map/ppermute | solution.py:192
  50.6 17.7 %collective-permute-start.20 = (bf16[48,2048]{1,0:T(8,128)(2,1)S(1)}, bf16[48,2048]{1,0:T(8,128)(2,1)S(1)}, u32[]{:S(2)}, u32[]{:S(2)}) collective-permute-start(bf16[48,2048]{1,0:T(8,128)(2,1)S(1)} %get-tuple-element.63), channel_id=1, source_target_pairs={{0,8},{4,12},{8,0},{12,4},{1,9},{5,13},{9,1},{13,5},{2,10},{6,14},... | collective-permute-start | bytes 589832 | tf_op jit(solution)/shard_map/ppermute | solution.py:192
  52.9 17.4 %collective-permute-start.22 = (bf16[64,2048]{1,0:T(8,128)(2,1)S(1)}, bf16[64,2048]{1,0:T(8,128)(2,1)S(1)}, u32[]{:S(2)}, u32[]{:S(2)}) collective-permute-start(bf16[64,2048]{1,0:T(8,128)(2,1)S(1)} %get-tuple-element.73), channel_id=1, source_target_pairs={{0,4},{4,0},{8,12},{12,8},{1,5},{5,1},{9,13},{13,9},{2,6},{6,2},{1... | collective-permute-start | bytes 786440 | tf_op jit(solution)/shard_map/ppermute | solution.py:192
  53.1 17.2 %collective-permute-start.21 = (bf16[48,2048]{1,0:T(8,128)(2,1)S(1)}, bf16[48,2048]{1,0:T(8,128)(2,1)S(1)}, u32[]{:S(2)}, u32[]{:S(2)}) collective-permute-start(bf16[48,2048]{1,0:T(8,128)(2,1)S(1)} %get-tuple-element.72), channel_id=1, source_target_pairs={{0,12},{4,8},{8,4},{12,0},{1,13},{5,9},{9,5},{13,1},{2,14},{6,10},... | collective-permute-start | bytes 589832 | tf_op jit(solution)/shard_map/ppermute | solution.py:192
  55.4 3.0 %copy-start = (bf16[1,2,1,4,8,128,128]{6,5,4,3,2,1,0:T(8,128)(2,1)S(1)}, bf16[1,2,1,4,8,128,128]{6,5,4,3,2,1,0:T(8,128)(2,1)}, u32[]{:S(2)}) copy-start(bf16[1,2,1,4,8,128,128]{6,5,4,3,2,1,0:T(8,128)(2,1)} %param.12) | copy-start | bytes 6291460
  55.4 3.0 %copy-start.5 = (s32[1,2,1,4,8]{4,3,2,1,0:T(4,128)S(1)}, s32[1,2,1,4,8]{4,3,2,1,0:T(4,128)}, u32[]{:S(2)}) copy-start(s32[1,2,1,4,8]{4,3,2,1,0:T(4,128)} %param.13) | copy-start | bytes 772
  60.4 6.5 %collective-permute-start.23 = (bf16[256,256]{1,0:T(8,128)(2,1)S(1)}, bf16[256,256]{1,0:T(8,128)(2,1)S(1)}, u32[]{:S(2)}, u32[]{:S(2)}) collective-permute-start(bf16[256,256]{1,0:T(8,128)(2,1)S(1)} %get-tuple-element.71), channel_id=1, source_target_pairs={{0,2},{2,0},{1,3},{3,1},{4,6},{6,4},{5,7},{7,5},{8,10},{10,8},{9,1... | collective-permute-start | bytes 393224 | tf_op jit(solution)/shard_map/ppermute | solution.py:192
  62.0 6.3 %collective-permute-start.24 = (bf16[256,256]{1,0:T(8,128)(2,1)S(1)}, bf16[256,256]{1,0:T(8,128)(2,1)S(1)}, u32[]{:S(2)}, u32[]{:S(2)}) collective-permute-start(bf16[256,256]{1,0:T(8,128)(2,1)S(1)} %get-tuple-element.74), channel_id=1, source_target_pairs={{0,2},{2,0},{1,3},{3,1},{4,6},{6,4},{5,7},{7,5},{8,10},{10,8},{9,1... | collective-permute-start | bytes 393224 | tf_op jit(solution)/shard_map/ppermute | solution.py:192
  70.4 2.2 %collective-permute-start.25 = (bf16[160,2048]{1,0:T(8,128)(2,1)S(1)}, bf16[160,2048]{1,0:T(8,128)(2,1)S(1)}, u32[]{:S(2)}, u32[]{:S(2)}) collective-permute-start(bf16[160,2048]{1,0:T(8,128)(2,1)S(1)} %join.1.refs_2_), channel_id=1, source_target_pairs={{0,1},{1,0},{2,3},{3,2},{4,5},{5,4},{6,7},{7,6},{8,9},{9,8},{10,11... | collective-permute-start | bytes 1966088 | tf_op jit(solution)/shard_map/ppermute | solution.py:192
  73.8 2.0 %copy-start.3 = (bf16[1,512,2048]{2,1,0:T(8,128)(2,1)S(1)}, bf16[1,512,2048]{2,1,0:T(8,128)(2,1)}, u32[]{:S(2)}) copy-start(bf16[1,512,2048]{2,1,0:T(8,128)(2,1)} %param.8) | copy-start | bytes 6291460
  76.0 0.8 %copy-start.4 = (f32[256,512]{1,0:T(8,128)}, f32[256,512]{1,0:T(8,128)S(1)}, u32[]{:S(2)}) copy-start(f32[256,512]{1,0:T(8,128)S(1)} %get-tuple-element.120) | copy-start | bytes 1572868

commit v6 on v4

--- a/solution.py
+++ b/solution.py
@@ -472,7 +472,7 @@
             flag = jnp.maximum(flag, swap(flag, axis, mask))
             mask *= 2
     (relay,) = call(
-        functools.partial(relay_kernel, q), [shape(q.spare + LINES, samples)], [spare, lines, flag], 0, "relay"
+        functools.partial(relay_kernel, q), [shape(q.spare + LINES, samples)], [spare, lines, flag], 0, "relay", after=[own_other]
     )
     relay = swap(relay, "bin", 1)
     back2, back3, near_back = gate([back2, back3, near_back], [cross3])
@@ -482,7 +482,7 @@
         [spare, lines, cross2, cross3, near, relay, flag],
         0,
         "gather",
-        after=[back2, own_other],
+        after=[back2],
     )
     flag = jnp.maximum(flag, swap(flag, "bin", 2))
     back2, back3, near_back = swap(back2, "bin", 2), swap(back3, "bin", 3), swap(near_back, "bin", 1)

time: 77 us -> 77 us (level)
  no operation moved by 1% of the time
where the time goes in v6:
time: 77 us; the launch traced here: 76.8 us
  waiting for transfers between devices  37.4 us (49%)
  starting transfers between devices  21.4 us (28%)
  Pallas kernels  15 us (19%)
  between operations  1.52 us (2%)
  local copies, waits for them, and re-layouts  1.34 us (2%)
    ppermute x18, waiting for transfers between devices, swap(): lax.ppermute(x, axis, [(i, i ^ mask) for i in range(lax.axis_size(axis))])  37.4 us
    ppermute x18, starting transfers between devices, swap(): lax.ppermute(x, axis, [(i, i ^ mask) for i in range(lax.axis_size(axis))])  21.4 us
    pallas_call x9, Pallas kernels, call(): pl.pallas_call(run, out_shape=list(out_shape), in_specs=[smem()] * scalar...  12.7 us
    pallas_call x1, Pallas kernels, short_path(): pl.pallas_call(functools.partial(pack_spare_kernel, q), out_shape=[shape(...  2.34 us
  transfers between devices with their start and end apart: 18, of which 11 were waited for; matrix products, arithmetic and copies ran while one was open for 1% of the time, Pallas kernels for 12%

profile of v6, /device:TPU:0, one launch (start us, length us, event | category | flops | bytes accessed | tf_op | source)
XLA Modules:
  0.0 76.8 jit_solution(5877563843888295251)
XLA Ops:
  0.7 2.3 %pack_spare.1 = (bf16[64,2048]{1,0:T(8,128)(2,1)S(1)}, bf16[16,256]{1,0:T(8,128)(2,1)S(1)}, bf16[208,2048]{1,0:T(8,128)(2,1)S(1)}, f32[8,128]{1,0:T(8,128)S(1)}, bf16[512,2048]{1,0:T(8,128)(2,1)S(1)}) custom-call(s32[1,1]{1,0:T(1,128)S(6)} %copy.17.live_ref.refs_0_, s32[1,512]{1,0:T(1,128)} %refs_1_.1, s32[1,512]{1,0:T(1,128)} %refs_2_.1, ...), custom_call_target="tpu_custom_call" | custom-call | tf_op jit(solution)/shard_map/pack_spare/pallas_call | solution.py:436
  3.6 3.7 %collective-permute-start.8 = (bf16[64,2048]{1,0:T(8,128)(2,1)S(1)}, bf16[64,2048]{1,0:T(8,128)(2,1)S(1)}, u32[]{:S(2)}, u32[]{:S(2)}) collective-permute-start(bf16[64,2048]{1,0:T(8,128)(2,1)S(1)} %get-tuple-element.53), channel_id=1, source_target_pairs={{0,8},{4,12},{8,0},{12,4},{1,9},{5,13},{9,1},{13,5},{2,10},{6,14},... | collective-permute-start | bytes 786440 | tf_op jit(solution)/shard_map/ppermute | solution.py:192
  7.2 1.4 %pack_rest.1 = (bf16[80,2048]{1,0:T(8,128)(2,1)S(1)}, bf16[80,2048]{1,0:T(8,128)(2,1)S(1)}, bf16[144,2048]{1,0:T(8,128)(2,1)S(1)}, bf16[48,2048]{1,0:T(8,128)(2,...) custom-call(s32[1,1]{1,0:T(1,128)S(6)} %copy.17.live_ref.refs_0_, s32[1,512]{1,0:T(1,128)S(1)} %copy-done.6, ...), custom_call_target="tpu_custom_call" | custom-call | flops 939524096 | bytes 4001796 | tf_op jit(solution)/shard_map/pack_rest/pallas_call | solution.py:38
  8.6 1.6 %collective-permute-start.12 = (bf16[144,2048]{1,0:T(8,128)(2,1)S(1)}, bf16[144,2048]{1,0:T(8,128)(2,1)S(1)}, u32[]{:S(2)}, u32[]{:S(2)}) collective-permute-start(bf16[144,2048]{1,0:T(8,128)(2,1)S(1)} %get-tuple-element.58), channel_id=1, source_target_pairs={{0,4},{4,0},{8,12},{12,8},{1,5},{5,1},{9,13},{13,9},{2,6},{6,2},{1... | collective-permute-start | bytes 1769480 | tf_op jit(solution)/shard_map/ppermute | solution.py:192
  11.4 1.5 %collective-permute-start.14 = (f32[8,128]{1,0:T(8,128)S(1)}, f32[8,128]{1,0:T(8,128)S(1)}, u32[]{:S(2)}, u32[]{:S(2)}) collective-permute-start(f32[8,128]{1,0:T(8,128)S(1)} %max.12), channel_id=1, source_target_pairs={{0,2},{2,0},{1,3},{3,1},{4,6},{6,4},{5,7},{7,5},{8,10},{10,8},{9,1... | collective-permute-start | bytes 12296 | tf_op jit(solution)/shard_map/ppermute | solution.py:192
  13.2 1.8 %collective-permute-done.14 = f32[8,128]{1,0:T(8,128)S(1)} collective-permute-done((f32[8,128]{1,0:T(8,128)S(1)}, f32[8,128]{1,0:T(8,128)S(1)}, u32[]{:S(2)}, u32[]{:S(2)}) %collective-permute-start.14) | collective-permute-done | bytes 4128 | tf_op jit(solution)/shard_map/ppermute | solution.py:192
  15.0 1.5 %collective-permute-start.15 = (f32[8,128]{1,0:T(8,128)S(1)}, f32[8,128]{1,0:T(8,128)S(1)}, u32[]{:S(2)}, u32[]{:S(2)}) collective-permute-start(f32[8,128]{1,0:T(8,128)S(1)} %max.13), channel_id=1, source_target_pairs={{0,16},{16,0},{1,17},{17,1},{2,18},{18,2},{3,19},{19,3},{4,20},{20... | collective-permute-start | bytes 12296 | tf_op jit(solution)/shard_map/ppermute | solution.py:192
  16.5 2.1 %collective-permute-done.15 = f32[8,128]{1,0:T(8,128)S(1)} collective-permute-done((f32[8,128]{1,0:T(8,128)S(1)}, f32[8,128]{1,0:T(8,128)S(1)}, u32[]{:S(2)}, u32[]{:S(2)}) %collective-permute-start.15) | collective-permute-done | bytes 4128 | tf_op jit(solution)/shard_map/ppermute | solution.py:192
  20.5 6.2 %collective-permute-done.9.refs_1_ = bf16[16,256]{1,0:T(8,128)(2,1)S(1)} collective-permute-done((bf16[16,256]{1,0:T(8,128)(2,1)S(1)}, bf16[16,256]{1,0:T(8,128)(2,1)S(1)}, u32[]{:S(2)}, u32[]{:S(2)}) %collective-permute-start.9) | collective-permute-done | bytes 8224 | tf_op jit(solution)/shard_map/ppermute | solution.py:192
  26.8 2.5 %collective-permute-start.17 = (bf16[80,2048]{1,0:T(8,128)(2,1)S(1)}, bf16[80,2048]{1,0:T(8,128)(2,1)S(1)}, u32[]{:S(2)}, u32[]{:S(2)}) collective-permute-start(bf16[80,2048]{1,0:T(8,128)(2,1)S(1)} %relay.1), channel_id=1, source_target_pairs={{0,4},{4,0},{8,12},{12,8},{1,5},{5,1},{9,13},{13,9},{2,6},{6,2},{1... | collective-permute-start | bytes 983048 | tf_op jit(solution)/shard_map/ppermute | solution.py:192
  29.3 6.3 %collective-permute-done.11.refs_3_ = bf16[80,2048]{1,0:T(8,128)(2,1)S(1)} collective-permute-done((bf16[80,2048]{1,0:T(8,128)(2,1)S(1)}, bf16[80,2048]{1,0:T(8,128)(2,1)S(1)}, u32[]{:S(2)}, u32[]{:S(2)}) %collective-permute-start.11) | collective-permute-done | bytes 327712 | tf_op jit(solution)/shard_map/ppermute | solution.py:192
  35.7 12.7 %collective-permute-done.10.refs_2_ = bf16[80,2048]{1,0:T(8,128)(2,1)S(1)} collective-permute-done((bf16[80,2048]{1,0:T(8,128)(2,1)S(1)}, bf16[80,2048]{1,0:T(8,128)(2,1)S(1)}, u32[]{:S(2)}, u32[]{:S(2)}) %collective-permute-start.10) | collective-permute-done | bytes 327712 | tf_op jit(solution)/shard_map/ppermute | solution.py:192
  48.3 1.4 %collective-permute-done.17.refs_5_ = bf16[80,2048]{1,0:T(8,128)(2,1)S(1)} collective-permute-done((bf16[80,2048]{1,0:T(8,128)(2,1)S(1)}, bf16[80,2048]{1,0:T(8,128)(2,1)S(1)}, u32[]{:S(2)}, u32[]{:S(2)}) %collective-permute-start.17) | collective-permute-done | bytes 327712 | tf_op jit(solution)/shard_map/ppermute | solution.py:192
  50.6 2.3 %collective-permute-start.20 = (bf16[48,2048]{1,0:T(8,128)(2,1)S(1)}, bf16[48,2048]{1,0:T(8,128)(2,1)S(1)}, u32[]{:S(2)}, u32[]{:S(2)}) collective-permute-start(bf16[48,2048]{1,0:T(8,128)(2,1)S(1)} %get-tuple-element.64), channel_id=1, source_target_pairs={{0,8},{4,12},{8,0},{12,4},{1,9},{5,13},{9,1},{13,5},{2,10},{6,14},... | collective-permute-start | bytes 589832 | tf_op jit(solution)/shard_map/ppermute | solution.py:192
  53.1 2.3 %collective-permute-start.21 = (bf16[48,2048]{1,0:T(8,128)(2,1)S(1)}, bf16[48,2048]{1,0:T(8,128)(2,1)S(1)}, u32[]{:S(2)}, u32[]{:S(2)}) collective-permute-start(bf16[48,2048]{1,0:T(8,128)(2,1)S(1)} %get-tuple-element.72), channel_id=1, source_target_pairs={{0,12},{4,8},{8,4},{12,0},{1,13},{5,9},{9,5},{13,1},{2,14},{6,10},... | collective-permute-start | bytes 589832 | tf_op jit(solution)/shard_map/ppermute | solution.py:192
  55.5 3.0 %stack_sent.1 = (bf16[512,2048]{1,0:T(8,128)(2,1)S(1)}, bf16[1216,2048]{1,0:T(8,128)(2,1)S(1)}, f32[8,1216]{1,0:T(8,128)S(1)}, f32[8,320]{1,0:T(8,128)S(1)}) custom-call(bf16[432,2048]{1,0:T(8,128)(2,1)S(1)} %get-tuple-element.66.refs_0_, bf16[432,2048]{1,0:T(8,128)(2,1)S(1)} %collective-permute-done.19.refs_1_, ...), custom_call_target="tpu_custom_call" | custom-call | flops 2550136832 | bytes 12369920 | tf_op jit(solution)/shard_map/stack_sent/pallas_call | solution.py:38
  58.5 1.9 %operate.3 = (bf16[256,256]{1,0:T(8,128)(2,1)S(1)}, bf16[256,256]{1,0:T(8,128)(2,1)S(1)}) custom-call(s32[2,4,8]{2,1,0:T(4,128)S(1)} %bitcast.9, bf16[2,4,8,128,128]{4,3,2,1,0:T(8,128)(2,1)S(1)} %bitcast.4, bf16[512,2048]{1,0:T(8,128)(2,1)S(1)} %get-tuple-element.70.refs_2_), custom_call_target="tpu_custom_call" | custom-call | flops 536870912 | bytes 4456704 | tf_op jit(solution)/shard_map/operate/pallas_call | solution.py:38
  60.4 1.5 %collective-permute-start.23 = (bf16[256,256]{1,0:T(8,128)(2,1)S(1)}, bf16[256,256]{1,0:T(8,128)(2,1)S(1)}, u32[]{:S(2)}, u32[]{:S(2)}) collective-permute-start(bf16[256,256]{1,0:T(8,128)(2,1)S(1)} %get-tuple-element.71), channel_id=1, source_target_pairs={{0,2},{2,0},{1,3},{3,1},{4,6},{6,4},{5,7},{7,5},{8,10},{10,8},{9,1... | collective-permute-start | bytes 393224 | tf_op jit(solution)/shard_map/ppermute | solution.py:192
  62.5 2.9 %stack_kept.1.refs_1_ = f32[512,2048]{1,0:T(8,128)S(1)} custom-call(bf16[1216,2048]{1,0:T(8,128)(2,1)S(1)} %get-tuple-element.68.refs_0_, f32[8,1216]{1,0:T(8,128)S(1)} %get-tuple-element.69.refs_1_, bf16[16,128]{1,0:T(8,128)(2,1)S(1)} %slice.32.refs_2_), custom_call_target="tpu_custom_call" | custom-call | flops 2550136832 | bytes 9213952 | tf_op jit(solution)/shard_map/stack_kept/pallas_call | solution.py:38
  65.4 1.5 %collective-permute-done.23.refs_3_ = bf16[256,256]{1,0:T(8,128)(2,1)S(1)} collective-permute-done((bf16[256,256]{1,0:T(8,128)(2,1)S(1)}, bf16[256,256]{1,0:T(8,128)(2,1)S(1)}, u32[]{:S(2)}, u32[]{:S(2)}) %collective-permute-start.23) | collective-permute-done | bytes 131104 | tf_op jit(solution)/shard_map/ppermute | solution.py:192
  66.9 1.4 %collective-permute-done.24.refs_4_ = bf16[256,256]{1,0:T(8,128)(2,1)S(1)} collective-permute-done((bf16[256,256]{1,0:T(8,128)(2,1)S(1)}, bf16[256,256]{1,0:T(8,128)(2,1)S(1)}, u32[]{:S(2)}, u32[]{:S(2)}) %collective-permute-start.24) | collective-permute-done | bytes 131104 | tf_op jit(solution)/shard_map/ppermute | solution.py:192
  68.3 2.0 %collective-permute-done.21.refs_1_ = bf16[48,2048]{1,0:T(8,128)(2,1)S(1)} collective-permute-done((bf16[48,2048]{1,0:T(8,128)(2,1)S(1)}, bf16[48,2048]{1,0:T(8,128)(2,1)S(1)}, u32[]{:S(2)}, u32[]{:S(2)}) %collective-permute-start.21) | collective-permute-done | bytes 196640 | tf_op jit(solution)/shard_map/ppermute | solution.py:192
  72.6 1.3 %stack_second.1.refs_2_ = bf16[512,2048]{1,0:T(8,128)(2,1)S(1)} custom-call(f32[8,320]{1,0:T(8,128)S(1)} %get-tuple-element.67.refs_0_, f32[512,2048]{1,0:T(8,128)S(1)} %stack_kept.1.refs_1_, bf16[160,2048]{1,0:T(8,128)(2,1)S(1)} %join.1.refs_2_, bf16[160,2048]{1,0:T(8,128)(2,1)S(1)} %collective-permute-done.25.refs_3_), custom_call_target="tpu_custom_call" | custom-call | flops 671088640 | bytes 7612416 | tf_op jit(solution)/shard_map/stack_second/pallas_call | solution.py:38
  73.9 1.9 %finish.1 = f32[256,512]{1,0:T(8,128)S(1)} custom-call(s32[2,4,8]{2,1,0:T(4,128)S(1)} %bitcast.10, bf16[2,4,8,128,128]{4,3,2,1,0:T(8,128)(2,1)S(1)} %bitcast.5, bf16[512,2048]{1,0:T(8,128)(2,1)S(1)} %stack_second.1.refs_2_, bf16[256,256]{1,0:T(8,128)(2,1)S(1)} %collective-permute-done.23.refs_3_, bf16[256,256]{1,0:T(8,128)(2,1)S(1)} %collective-permute-done.24.refs_4_), custom_call_target="tpu_custom_call" | custom-call | flops 536870912 | bytes 4980992 | tf_op jit(solution)/shard_map/finish/pallas_call | solution.py:38
  (49 shorter events, 8.2 us)
Async XLA Ops:
  0.0 7.2 %copy-start.7 = (s32[1,512]{1,0:T(1,128)S(1)}, s32[1,512]{1,0:T(1,128)}, u32[]{:S(2)}) copy-start(s32[1,512]{1,0:T(1,128)} %refs_2_.1) | copy-start | bytes 6148
  0.0 7.2 %copy-start.6 = (s32[1,512]{1,0:T(1,128)S(1)}, s32[1,512]{1,0:T(1,128)}, u32[]{:S(2)}) copy-start(s32[1,512]{1,0:T(1,128)} %refs_1_.1) | copy-start | bytes 6148
  3.0 16.3 %collective-permute-start.16 = (bf16[208,2048]{1,0:T(8,128)(2,1)S(1)}, bf16[208,2048]{1,0:T(8,128)(2,1)S(1)}, u32[]{:S(2)}, u32[]{:S(2)}) collective-permute-start(bf16[208,2048]{1,0:T(8,128)(2,1)S(1)} %get-tuple-element.60.refs_2_), channel_id=1, source_target_pairs={{0,1},{1,0},{2,3},{3,2},{4,5},{5,4},{6,7},{7,6},{8,9},{9,8},{10,11... | collective-permute-start | bytes 2555912 | tf_op jit(solution)/shard_map/ppermute | solution.py:192
  3.6 23.2 %collective-permute-start.8 = (bf16[64,2048]{1,0:T(8,128)(2,1)S(1)}, bf16[64,2048]{1,0:T(8,128)(2,1)S(1)}, u32[]{:S(2)}, u32[]{:S(2)}) collective-permute-start(bf16[64,2048]{1,0:T(8,128)(2,1)S(1)} %get-tuple-element.53), channel_id=1, source_target_pairs={{0,8},{4,12},{8,0},{12,4},{1,9},{5,13},{9,1},{13,5},{2,10},{6,14},... | collective-permute-start | bytes 786440 | tf_op jit(solution)/shard_map/ppermute | solution.py:192
  8.6 39.7 %collective-permute-start.12 = (bf16[144,2048]{1,0:T(8,128)(2,1)S(1)}, bf16[144,2048]{1,0:T(8,128)(2,1)S(1)}, u32[]{:S(2)}, u32[]{:S(2)}) collective-permute-start(bf16[144,2048]{1,0:T(8,128)(2,1)S(1)} %get-tuple-element.58), channel_id=1, source_target_pairs={{0,4},{4,0},{8,12},{12,8},{1,5},{5,1},{9,13},{13,9},{2,6},{6,2},{1... | collective-permute-start | bytes 1769480 | tf_op jit(solution)/shard_map/ppermute | solution.py:192
  10.2 1.2 %collective-permute-start.13 = (f32[8,128]{1,0:T(8,128)S(1)}, f32[8,128]{1,0:T(8,128)S(1)}, u32[]{:S(2)}, u32[]{:S(2)}) collective-permute-start(f32[8,128]{1,0:T(8,128)S(1)} %get-tuple-element.59), channel_id=1, source_target_pairs={{0,1},{1,0},{2,3},{3,2},{4,5},{5,4},{6,7},{7,6},{8,9},{9,8},{10,11... | collective-permute-start | bytes 12296 | tf_op jit(solution)/shard_map/ppermute | solution.py:192
  11.4 3.6 %collective-permute-start.14 = (f32[8,128]{1,0:T(8,128)S(1)}, f32[8,128]{1,0:T(8,128)S(1)}, u32[]{:S(2)}, u32[]{:S(2)}) collective-permute-start(f32[8,128]{1,0:T(8,128)S(1)} %max.12), channel_id=1, source_target_pairs={{0,2},{2,0},{1,3},{3,1},{4,6},{6,4},{5,7},{7,5},{8,10},{10,8},{9,1... | collective-permute-start | bytes 12296 | tf_op jit(solution)/shard_map/ppermute | solution.py:192
  12.9 13.8 %collective-permute-start.9 = (bf16[16,256]{1,0:T(8,128)(2,1)S(1)}, bf16[16,256]{1,0:T(8,128)(2,1)S(1)}, u32[]{:S(2)}, u32[]{:S(2)}) collective-permute-start(bf16[16,256]{1,0:T(8,128)(2,1)S(1)} %get-tuple-element.54), channel_id=1, source_target_pairs={{0,8},{4,12},{8,0},{12,4},{1,9},{5,13},{9,1},{13,5},{2,10},{6,14},... | collective-permute-start | bytes 24584 | tf_op jit(solution)/shard_map/ppermute | solution.py:192
  15.0 3.6 %collective-permute-start.15 = (f32[8,128]{1,0:T(8,128)S(1)}, f32[8,128]{1,0:T(8,128)S(1)}, u32[]{:S(2)}, u32[]{:S(2)}) collective-permute-start(f32[8,128]{1,0:T(8,128)S(1)} %max.13), channel_id=1, source_target_pairs={{0,16},{16,0},{1,17},{17,1},{2,18},{18,2},{3,19},{19,3},{4,20},{20... | collective-permute-start | bytes 12296 | tf_op jit(solution)/shard_map/ppermute | solution.py:192
  18.6 17.0 %collective-permute-start.11 = (bf16[80,2048]{1,0:T(8,128)(2,1)S(1)}, bf16[80,2048]{1,0:T(8,128)(2,1)S(1)}, u32[]{:S(2)}, u32[]{:S(2)}) collective-permute-start(bf16[80,2048]{1,0:T(8,128)(2,1)S(1)} %get-tuple-element.57), channel_id=1, source_target_pairs={{0,12},{4,8},{8,4},{12,0},{1,13},{5,9},{9,5},{13,1},{2,14},{6,10},... | collective-permute-start | bytes 983048 | tf_op jit(solution)/shard_map/ppermute | solution.py:192
  19.3 29.0 %collective-permute-start.10 = (bf16[80,2048]{1,0:T(8,128)(2,1)S(1)}, bf16[80,2048]{1,0:T(8,128)(2,1)S(1)}, u32[]{:S(2)}, u32[]{:S(2)}) collective-permute-start(bf16[80,2048]{1,0:T(8,128)(2,1)S(1)} %get-tuple-element.56), channel_id=1, source_target_pairs={{0,8},{4,12},{8,0},{12,4},{1,9},{5,13},{9,1},{13,5},{2,10},{6,14},... | collective-permute-start | bytes 983048 | tf_op jit(solution)/shard_map/ppermute | solution.py:192
  26.8 23.0 %collective-permute-start.17 = (bf16[80,2048]{1,0:T(8,128)(2,1)S(1)}, bf16[80,2048]{1,0:T(8,128)(2,1)S(1)}, u32[]{:S(2)}, u32[]{:S(2)}) collective-permute-start(bf16[80,2048]{1,0:T(8,128)(2,1)S(1)} %relay.1), channel_id=1, source_target_pairs={{0,4},{4,0},{8,12},{12,8},{1,5},{5,1},{9,13},{13,9},{2,6},{6,2},{1... | collective-permute-start | bytes 983048 | tf_op jit(solution)/shard_map/ppermute | solution.py:192
  49.9 5.6 %collective-permute-start.19 = (bf16[432,2048]{1,0:T(8,128)(2,1)S(1)}, bf16[432,2048]{1,0:T(8,128)(2,1)S(1)}, u32[]{:S(2)}, u32[]{:S(2)}) collective-permute-start(bf16[432,2048]{1,0:T(8,128)(2,1)S(1)} %get-tuple-element.66.refs_0_), channel_id=1, source_target_pairs={{0,1},{1,0},{2,3},{3,2},{4,5},{5,4},{6,7},{7,6},{8,9},{9,8},{10,11... | collective-permute-start | bytes 5308424 | tf_op jit(solution)/shard_map/ppermute | solution.py:192
  49.9 5.5 %collective-permute-start.18 = (f32[8,128]{1,0:T(8,128)S(1)}, f32[8,128]{1,0:T(8,128)S(1)}, u32[]{:S(2)}, u32[]{:S(2)}) collective-permute-start(f32[8,128]{1,0:T(8,128)S(1)} %get-tuple-element.65), channel_id=1, source_target_pairs={{0,8},{4,12},{8,0},{12,4},{1,9},{5,13},{9,1},{13,5},{2,10},{6,14},... | collective-permute-start | bytes 12296 | tf_op jit(solution)/shard_map/ppermute | solution.py:192
  50.6 17.7 %collective-permute-start.20 = (bf16[48,2048]{1,0:T(8,128)(2,1)S(1)}, bf16[48,2048]{1,0:T(8,128)(2,1)S(1)}, u32[]{:S(2)}, u32[]{:S(2)}) collective-permute-start(bf16[48,2048]{1,0:T(8,128)(2,1)S(1)} %get-tuple-element.64), channel_id=1, source_target_pairs={{0,8},{4,12},{8,0},{12,4},{1,9},{5,13},{9,1},{13,5},{2,10},{6,14},... | collective-permute-start | bytes 589832 | tf_op jit(solution)/shard_map/ppermute | solution.py:192
  52.9 17.4 %collective-permute-start.22 = (bf16[64,2048]{1,0:T(8,128)(2,1)S(1)}, bf16[64,2048]{1,0:T(8,128)(2,1)S(1)}, u32[]{:S(2)}, u32[]{:S(2)}) collective-permute-start(bf16[64,2048]{1,0:T(8,128)(2,1)S(1)} %get-tuple-element.73), channel_id=1, source_target_pairs={{0,4},{4,0},{8,12},{12,8},{1,5},{5,1},{9,13},{13,9},{2,6},{6,2},{1... | collective-permute-start | bytes 786440 | tf_op jit(solution)/shard_map/ppermute | solution.py:192
  53.1 17.2 %collective-permute-start.21 = (bf16[48,2048]{1,0:T(8,128)(2,1)S(1)}, bf16[48,2048]{1,0:T(8,128)(2,1)S(1)}, u32[]{:S(2)}, u32[]{:S(2)}) collective-permute-start(bf16[48,2048]{1,0:T(8,128)(2,1)S(1)} %get-tuple-element.72), channel_id=1, source_target_pairs={{0,12},{4,8},{8,4},{12,0},{1,13},{5,9},{9,5},{13,1},{2,14},{6,10},... | collective-permute-start | bytes 589832 | tf_op jit(solution)/shard_map/ppermute | solution.py:192
  55.4 3.0 %copy-start = (bf16[1,2,1,4,8,128,128]{6,5,4,3,2,1,0:T(8,128)(2,1)S(1)}, bf16[1,2,1,4,8,128,128]{6,5,4,3,2,1,0:T(8,128)(2,1)}, u32[]{:S(2)}) copy-start(bf16[1,2,1,4,8,128,128]{6,5,4,3,2,1,0:T(8,128)(2,1)} %param.12) | copy-start | bytes 6291460
  55.4 3.0 %copy-start.5 = (s32[1,2,1,4,8]{4,3,2,1,0:T(4,128)S(1)}, s32[1,2,1,4,8]{4,3,2,1,0:T(4,128)}, u32[]{:S(2)}) copy-start(s32[1,2,1,4,8]{4,3,2,1,0:T(4,128)} %param.13) | copy-start | bytes 772
  60.4 6.5 %collective-permute-start.23 = (bf16[256,256]{1,0:T(8,128)(2,1)S(1)}, bf16[256,256]{1,0:T(8,128)(2,1)S(1)}, u32[]{:S(2)}, u32[]{:S(2)}) collective-permute-start(bf16[256,256]{1,0:T(8,128)(2,1)S(1)} %get-tuple-element.71), channel_id=1, source_target_pairs={{0,2},{2,0},{1,3},{3,1},{4,6},{6,4},{5,7},{7,5},{8,10},{10,8},{9,1... | collective-permute-start | bytes 393224 | tf_op jit(solution)/shard_map/ppermute | solution.py:192
  62.0 6.3 %collective-permute-start.24 = (bf16[256,256]{1,0:T(8,128)(2,1)S(1)}, bf16[256,256]{1,0:T(8,128)(2,1)S(1)}, u32[]{:S(2)}, u32[]{:S(2)}) collective-permute-start(bf16[256,256]{1,0:T(8,128)(2,1)S(1)} %get-tuple-element.74), channel_id=1, source_target_pairs={{0,2},{2,0},{1,3},{3,1},{4,6},{6,4},{5,7},{7,5},{8,10},{10,8},{9,1... | collective-permute-start | bytes 393224 | tf_op jit(solution)/shard_map/ppermute | solution.py:192
  70.4 2.2 %collective-permute-start.25 = (bf16[160,2048]{1,0:T(8,128)(2,1)S(1)}, bf16[160,2048]{1,0:T(8,128)(2,1)S(1)}, u32[]{:S(2)}, u32[]{:S(2)}) collective-permute-start(bf16[160,2048]{1,0:T(8,128)(2,1)S(1)} %join.1.refs_2_), channel_id=1, source_target_pairs={{0,1},{1,0},{2,3},{3,2},{4,5},{5,4},{6,7},{7,6},{8,9},{9,8},{10,11... | collective-permute-start | bytes 1966088 | tf_op jit(solution)/shard_map/ppermute | solution.py:192
  73.9 2.0 %copy-start.3 = (bf16[1,512,2048]{2,1,0:T(8,128)(2,1)S(1)}, bf16[1,512,2048]{2,1,0:T(8,128)(2,1)}, u32[]{:S(2)}) copy-start(bf16[1,512,2048]{2,1,0:T(8,128)(2,1)} %param.8) | copy-start | bytes 6291460
  76.0 0.8 %copy-start.4 = (f32[256,512]{1,0:T(8,128)}, f32[256,512]{1,0:T(8,128)S(1)}, u32[]{:S(2)}) copy-start(f32[256,512]{1,0:T(8,128)S(1)} %get-tuple-element.120) | copy-start | bytes 1572868
